TPU v7x, 256 devices: a whole 4x4x8 slice. The times are simulated.
256 devices in a mesh: cols: 128 (over x_lo, z, y, core), lev: 2 (over x_hi).
Axes of the slice: x: 4 (x_hi: 2, x_lo: 2; x = x_hi * 2 + x_lo), y: 4, z: 8, core: 2. Of those that a mesh axis runs over, the one named last changes fastest.
Arguments:
- u_adj: float32 [128, 128, 16, 128], P('lev', 'cols'), may hold values from -6 to 6
- v_adj: float32 [128, 128, 16, 128], P('lev', 'cols'), may hold values from -6 to 6
- w_adj: float32 [128, 128, 16, 128], P('lev', 'cols'), may hold values from -6 to 6
- theta_adj: float32 [128, 128, 16, 128], P('lev', 'cols'), may hold values from -6 to 6
- p_adj: float32 [128, 128, 16, 128], P('lev', 'cols'), may hold values from -6 to 6
- grad_coef: float32 [128, 128, 16, 128], P('lev', 'cols'), may hold values from 0.3 to 1.2
- squeeze_coef: float32 [128, 128, 16, 128], P('lev', 'cols'), may hold values from 0.3 to 1.2
- wind_first: float32 [128, 128, 16, 128], P('lev', 'cols'), may hold values from -1 to 1
- wind_second: float32 [128, 128, 16, 128], P('lev', 'cols'), may hold values from -1 to 1
- acoustic_inverse: float32 [256, 256], replicated, may hold values from -0.375 to 0.375
Outputs:
- u_out: float32 [128, 128, 16, 128], P('lev', 'cols')
- v_out: float32 [128, 128, 16, 128], P('lev', 'cols')
- w_out: float32 [128, 128, 16, 128], P('lev', 'cols')
- theta_out: float32 [128, 128, 16, 128], P('lev', 'cols')
- p_out: float32 [128, 128, 16, 128], P('lev', 'cols')
All inputs are finite; a program needn't handle non-finite values.
Results may differ from a plain program's by a relative error of at most 0.000071.
Values sent between devices are 32-bit elements; how exact they have to be, the bound alone decides.
No kernel may reach another device: no remote copies, remote signals or barrier semaphores. Data moves between devices by JAX's collectives and lax.ppermute only.
A program may use at most 64 MiB of HBM per device.

v0:
```python
import jax
import jax.numpy as jnp
from jax import lax
from jax.sharding import PartitionSpec as P

TW = 4


def passed_along(array, axis, by):
    devices = lax.axis_size(axis)
    return lax.ppermute(array, axis, [(i, (i + by) % devices) for i in range(devices)])


def slope_first(wide):
    return (
        8.0 * (wide[..., 3:-1, :] - wide[..., 1:-3, :]) - (wide[..., 4:, :] - wide[..., :-4, :])
    ) / 12.0


def slope_second(wide):
    return (8.0 * (wide[..., 3:-1] - wide[..., 1:-3]) - (wide[..., 4:] - wide[..., :-4])) / 12.0


def widen(first_fields, second_fields):
    before = passed_along(first_fields[:, :, :, -2:, :], "cols", TW)
    after = passed_along(first_fields[:, :, :, :2, :], "cols", -TW)
    wide_first = jnp.concatenate([before, first_fields, after], axis=3)
    left_rim = passed_along(second_fields[:, :, :, :, -2:], "cols", 1)
    right_rim = passed_along(second_fields[:, :, :, :, :2], "cols", -1)
    wide_second = jnp.concatenate([left_rim, second_fields, right_rim], axis=4)
    return (slope_first(wide_first), slope_second(wide_second))


def on_device(
    u_adj,
    v_adj,
    w_adj,
    theta_adj,
    p_adj,
    grad_coef,
    squeeze_coef,
    wind_first,
    wind_second,
    acoustic_inverse,
):
    levels_here = u_adj.shape[0]
    cells = u_adj.shape[2] * u_adj.shape[3]
    total_levels = acoustic_inverse.shape[0] // 2
    offset = lax.axis_index("lev") * levels_here
    blocks = acoustic_inverse.reshape(2, total_levels, 2, total_levels)
    pressure = squeeze_coef * p_adj
    stacked = jnp.stack([w_adj.reshape(levels_here, cells), theta_adj.reshape(levels_here, cells)])
    own_cols = lax.dynamic_slice_in_dim(blocks, offset, levels_here, 3)
    solved = jnp.einsum(
        "tiqu,tip->qup",
        own_cols,
        lax.all_gather(stacked, "lev", axis=1, tiled=True),
        precision=lax.Precision.HIGHEST,
        preferred_element_type=jnp.float32,
    )
    w_new = solved[0]
    theta_star = solved[1]
    star = theta_star.reshape(theta_adj.shape)
    all_first, all_second = widen(
        jnp.stack([u_adj, pressure, wind_first * star]),
        jnp.stack([v_adj, pressure, wind_second * star]),
    )
    slope_u, slope_pu, slope_tu = (all_first[0], all_first[1], all_first[2])
    slope_v, slope_pv, slope_tv = (all_second[0], all_second[1], all_second[2])
    u_out = u_adj + slope_pu
    v_out = v_adj + slope_pv
    p_out = p_adj + grad_coef * (slope_u + slope_v)
    theta_out = star + slope_tu + slope_tv
    w_out = w_new.reshape(w_adj.shape)
    return (u_out, v_out, w_out, theta_out, p_out)


def solution(mesh):
    return jax.shard_map(
        on_device,
        mesh=mesh,
        in_specs=(
            P("lev", "cols", None, None),
            P("lev", "cols", None, None),
            P("lev", "cols", None, None),
            P("lev", "cols", None, None),
            P("lev", "cols", None, None),
            P("lev", "cols", None, None),
            P("lev", "cols", None, None),
            P("lev", "cols", None, None),
            P("lev", "cols", None, None),
            P(),
        ),
        out_specs=(
            P("lev", "cols", None, None),
            P("lev", "cols", None, None),
            P("lev", "cols", None, None),
            P("lev", "cols", None, None),
            P("lev", "cols", None, None),
        ),
        check_vma=False,
    )
```

profile of v0, /device:TPU:2, one launch (start us, length us, event | category | flops | bytes accessed | tf_op | source)
XLA Modules:
  0.0 104.3 jit_solution(676458081911088017)
XLA Ops:
  7.2 1.1 %stack_reshape.6 = f32[1,64,2048]{2,1,0:T(8,128)S(1)} reshape(f32[64,1,16,128]{3,2,1,0:T(8,128)} %param.12) | data formatting | bytes 1048576 | tf_op jit(solution)/shard_map/stack;reshape | solution.py:52
  8.3 1.1 %stack_reshape.7 = f32[1,64,2048]{2,1,0:T(8,128)S(1)} reshape(f32[64,1,16,128]{3,2,1,0:T(8,128)} %param.13) | data formatting | bytes 1048576 | tf_op jit(solution)/shard_map/stack;reshape | solution.py:52
  9.5 1.1 %pad_maximum_fusion.4 = f32[2,64,2048]{2,1,0:T(8,128)} fusion(f32[1,64,2048]{2,1,0:T(8,128)S(1)} %stack_reshape.7, f32[1,64,2048]{2,1,0:T(8,128)S(1)} %stack_reshape.6), kind=kLoop, calls=%fused_computation.20 | loop fusion | flops 262144 | bytes 2097152 | tf_op jit(solution)/shard_map/stack | solution.py:52
  11.8 40.6 %all-gather.2.cloned.1.call-done = f32[2,128,2048]{2,1,0:T(8,128)} async-done(((f32[2,64,2048]{2,1,0:T(8,128)}), f32[2,128,2048]{2,1,0:T(8,128)}) %all-gather.2.cloned.1.call-update) | async-done | bytes 2097168 | tf_op jit(solution)/shard_map/all_gather | solution.py:57
  52.5 2.9 %convolution_bitcast_fusion = f32[2,64,2048]{2,1,0:T(8,128)S(1)} fusion(f32[2,128,2048]{2,1,0:T(8,128)} %all-gather.2.cloned.1.call-done, f32[2,128,2,64]{3,2,1,0:T(2,128)S(1)} %constant_dynamic-slice_fusion), kind=kOutput, calls=%fused_computation.2 | convolution fusion | flops 805306368 | bytes 3276800 | tf_op jit(solution)/shard_map/tiqu,tip->qup/dot_general | solution.py:54
  55.4 0.9 slice_bitcast_fusion.2
  56.9 0.7 copy-done.3
  57.5 0.6 copy-done.4
  58.3 1.5 %fusion.2 = (f32[3,64,1,16,128]{4,3,1,2,0:T(8,128)S(1)}, f32[3,64,1,16,128]{4,3,1,2,0:T(8,128)}) fusion(f32[1,64,1,16,128]{4,3,1,2,0:T(8,128)S(1)} %multiply_bitcast_fusion, f32[1,64,1,16,128]{4,3,1,2,0:T(8,128)S(1)} %bitcast.86, f32[1,64,1,16,128]{4,3,1,2,0:T(8,128)S(1)} %bitcast.88, f32[1,64,1,16,128]{4,3,1,2,0:T(8,128)S(1)} %bitcast.82, ...), kind=kLoop, calls=%fused_computation.9 | loop fusion | flops 1572864 | bytes 5767168 | tf_op jit(solution)/shard_map/stack | solution.py:66
  59.8 1.7 %fusion.19 = (f32[3,64,1,16,2]{4,3,1,2,0:T(8,128)}, f32[3,64,1,16,2]{4,3,1,2,0:T(8,128)S(1)}) fusion(f32[3,64,1,16,128]{4,3,1,2,0:T(8,128)S(1)} %get-tuple-element.49), kind=kLoop, calls=%fused_computation.43 | loop fusion | bytes 98304 | tf_op jit(solution)/shard_map/slice | solution.py:29
  61.5 2.6 %copy.105 = f32[3,64,1,16,2]{1,3,4,2,0:T(8,128)} copy(f32[3,64,1,16,2]{4,3,1,2,0:T(8,128)} %get-tuple-element.41) | data formatting | bytes 49152 | tf_op jit(solution)/shard_map/slice | solution.py:29
  64.1 1.3 %copy.107 = f32[3,64,1,16,2]{1,3,4,2,0:T(8,128)} copy(f32[3,64,1,16,2]{4,3,1,2,0:T(8,128)S(1)} %get-tuple-element.42) | data formatting | bytes 49152 | tf_op jit(solution)/shard_map/slice | solution.py:28
  65.4 6.0 %collective-permute-start.2 = (f32[3,64,1,16,2]{1,3,4,2,0:T(8,128)}, f32[3,64,1,16,2]{1,3,4,2,0:T(8,128)}, u32[]{:S(2)}, u32[]{:S(2)}) collective-permute-start(f32[3,64,1,16,2]{1,3,4,2,0:T(8,128)} %copy.105), channel_id=1, source_target_pairs={{0,254},{2,0},{4,2},{6,4},{8,6},{10,8},{12,10},{14,12},{16,14},{18... | collective-permute-start | bytes 73736 | tf_op jit(solution)/shard_map/ppermute | solution.py:11
  71.3 2.2 %fusion.20 = (f32[3,64,1,2,128]{4,3,1,2,0:T(2,128)}, f32[3,64,1,2,128]{4,3,1,2,0:T(2,128)}) fusion(f32[3,64,1,16,128]{4,3,1,2,0:T(8,128)} %get-tuple-element.50), kind=kLoop, calls=%fused_computation.44 | loop fusion | bytes 786432 | tf_op jit(solution)/shard_map/slice | solution.py:26
  73.6 1.9 %copy.120 = f32[8,8,16,128]{3,2,1,0:T(8,128)} copy(f32[8,8,16,128]{3,1,2,0:T(8,128)} %get-tuple-element.47) | data formatting | bytes 1048576
  75.5 2.4 %collective-permute-start = (f32[3,64,1,2,128]{4,3,1,2,0:T(2,128)}, f32[3,64,1,2,128]{4,3,1,2,0:T(2,128)S(1)}, u32[]{:S(2)}, u32[]{:S(2)}) collective-permute-start(f32[3,64,1,2,128]{4,3,1,2,0:T(2,128)} %get-tuple-element.45), channel_id=1, source_target_pairs={{0,248},{2,250},{4,252},{6,254},{8,0},{10,2},{12,4},{14,6},{16,8},... | collective-permute-start | bytes 589832 | tf_op jit(solution)/shard_map/ppermute | solution.py:11
  78.0 1.1 %collective-permute-start.1 = (f32[3,64,1,2,128]{4,3,1,2,0:T(2,128)}, f32[3,64,1,2,128]{4,3,1,2,0:T(2,128)S(1)}, u32[]{:S(2)}, u32[]{:S(2)}) collective-permute-start(f32[3,64,1,2,128]{4,3,1,2,0:T(2,128)} %get-tuple-element.46), channel_id=1, source_target_pairs={{0,8},{2,10},{4,12},{6,14},{8,16},{10,18},{12,20},{14,22},{16,24},... | collective-permute-start | bytes 589832 | tf_op jit(solution)/shard_map/ppermute | solution.py:11
  79.1 1.5 %copy.106 = f32[3,64,1,16,2]{4,3,1,2,0:T(8,128)S(1)} copy(f32[3,64,1,16,2]{1,3,4,2,0:T(8,128)} %collective-permute-done.2) | data formatting | bytes 49152 | tf_op jit(solution)/shard_map/ppermute | solution.py:11
  80.6 2.6 %copy.108 = f32[3,64,1,16,2]{4,3,1,2,0:T(8,128)} copy(f32[3,64,1,16,2]{1,3,4,2,0:T(8,128)} %collective-permute-done.3) | data formatting | bytes 49152 | tf_op jit(solution)/shard_map/ppermute | solution.py:11
  83.2 2.9 %pad_maximum_fusion = (f32[3,64,1,16,130]{4,3,1,2,0:T(8,128)S(1)}, f32[3,64,1,16,130]{4,3,1,2,0:T(8,128)S(1)}) fusion(f32[3,64,1,16,2]{4,3,1,2,0:T(8,128)S(1)} %copy.106, f32[1,64,1,16,128]{4,3,1,2,0:T(8,128)S(1)} %bitcast.87, f32[1,64,1,16,128]{4,3,1,2,0:T(8,128)S(1)} %multiply_bitcast_fusion, f32[1,64,1,16,128]{4,3,1,2,0:T(8,128)S(1)} %bitcast.89, ...), kind=kLoop, calls=%fused_computation | loop fusion | flops 2396160 | bytes 4816896 | tf_op jit(solution)/shard_map/concatenate | solution.py:30
  86.1 2.6 %collective-permute-done.1 = f32[3,64,1,2,128]{4,3,1,2,0:T(2,128)S(1)} collective-permute-done((f32[3,64,1,2,128]{4,3,1,2,0:T(2,128)}, f32[3,64,1,2,128]{4,3,1,2,0:T(2,128)S(1)}, u32[]{:S(2)}, u32[]{:S(2)}) %collective-permute-start.1) | collective-permute-done | bytes 196640 | tf_op jit(solution)/shard_map/ppermute | solution.py:11
  88.8 1.6 %pad_maximum_fusion.1 = (f32[3,64,1,18,128]{4,3,1,2,0:T(8,128)S(1)}, f32[3,64,1,18,128]{4,3,1,2,0:T(8,128)S(1)}) fusion(f32[3,64,1,2,128]{4,3,1,2,0:T(2,128)S(1)} %collective-permute-done, f32[1,64,1,16,128]{4,3,1,2,0:T(8,128)S(1)} %bitcast.83, f32[1,64,1,16,128]{4,3,1,2,0:T(8,128)} %copy-done, f32[1,64,1,16,128]{4,3,1,2,0:T(8,128)S(1)} %bitcast.85, ...), kind=kLoop, calls=%fused_computation.3 | loop fusion | flops 2654208 | bytes 5505024 | tf_op jit(solution)/shard_map/concatenate | solution.py:27
  90.4 2.9 %fusion.4 = (f32[3,64,1,16,128]{4,3,1,2,0:T(8,128)}, f32[3,64,1,16,128]{4,3,1,2,0:T(8,128)}) fusion(f32[3,64,1,16,130]{4,3,1,2,0:T(8,128)S(1)} %get-tuple-element.40, f32[3,64,1,16,130]{4,3,1,2,0:T(8,128)S(1)} %get-tuple-element.39, f32[3,64,1,18,128]{4,3,1,2,0:T(8,128)S(1)} %get-tuple-element.44, f32[3,64,1,18,128]{4,3,1,2,0:T(8,128)S(1)} %get-tuple-element.43), kind=kLoop, calls=%fused_computation.12 | loop fusion | flops 3932160 | bytes 15728640 | tf_op jit(solution)/shard_map/div | solution.py:21
  93.3 4.1 %fusion.13 = (f32[64,1,16,128]{3,2,1,0:T(8,128)}, f32[64,1,16,128]{3,2,0,1:T(8,128)}, f32[64,1,16,128]{3,2,1,0:T(8,128)}, f32[64,1,16,128]{3,2,1,0:T(8,128)}) fusion(f32[3,64,1,16,128]{4,3,1,2,0:T(8,128)} %get-tuple-element.53, f32[3,64,1,16,128]{4,3,1,2,0:T(8,128)} %get-tuple-element.54, f32[64,1,16,128]{3,2,1,0:T(8,128)} %param.15, ...), kind=kLoop, calls=%fused_computation.29 | loop fusion | flops 917504 | bytes 7864320
  (33 shorter events, 2.1 us)
Async XLA Ops:
  7.2 45.3 %all-gather.2.cloned.1.call-start = ((), (), s32[]{:S(2)}) async-start(), calls=%async_computation | async-start | bytes 3145728 | tf_op jit(solution)/shard_map/all_gather | solution.py:57
  9.5 1.1 %copy-start.11 = (f32[256,256]{1,0:T(8,128)S(1)}, f32[256,256]{1,0:T(8,128)}, u32[]{:S(2)}) copy-start(f32[256,256]{1,0:T(8,128)} %param.19) | copy-start | bytes 786436
  10.6 1.0 copy-start.7
  10.6 1.2 %copy-start.8 = (f32[64,1,16,128]{3,2,1,0:T(8,128)S(1)}, f32[64,1,16,128]{3,2,1,0:T(8,128)}, u32[]{:S(2)}) copy-start(f32[64,1,16,128]{3,2,1,0:T(8,128)} %param.16) | copy-start | bytes 1572868
  11.8 71.4 %copy-start = (f32[1,64,1,16,128]{4,3,1,2,0:T(8,128)}, f32[1,64,1,16,128]{4,3,1,2,0:T(8,128)S(1)}, u32[]{:S(2)}) copy-start(f32[1,64,1,16,128]{4,3,1,2,0:T(8,128)S(1)} %multiply_bitcast_fusion) | copy-start | bytes 1572868
  55.3 1.2 %copy-start.9 = (f32[64,1,16,128]{3,2,1,0:T(8,128)S(1)}, f32[64,1,16,128]{3,2,1,0:T(8,128)}, u32[]{:S(2)}) copy-start(f32[64,1,16,128]{3,2,1,0:T(8,128)} %param.18) | copy-start | bytes 1572868
  55.4 1.4 %copy-start.10 = (f32[64,1,16,128]{3,2,1,0:T(8,128)S(1)}, f32[64,1,16,128]{3,2,1,0:T(8,128)}, u32[]{:S(2)}) copy-start(f32[64,1,16,128]{3,2,1,0:T(8,128)} %param.17) | copy-start | bytes 1572868
  56.7 0.8 copy-start.3
  56.7 1.4 %copy-start.4 = (f32[64,1,16,128]{3,2,1,0:T(8,128)S(1)}, f32[64,1,16,128]{3,2,1,0:T(8,128)}, u32[]{:S(2)}) copy-start(f32[64,1,16,128]{3,2,1,0:T(8,128)} %param.10) | copy-start | bytes 1572868
  56.7 1.6 %copy-start.6 = (f32[64,1,16,128]{3,2,1,0:T(8,128)S(1)}, f32[64,1,16,128]{3,2,1,0:T(8,128)}, u32[]{:S(2)}) copy-start(f32[64,1,16,128]{3,2,1,0:T(8,128)} %param.11) | copy-start | bytes 1572868
  56.9 2.9 %copy-start.1 = (f32[64,1,16,128]{3,2,0,1:T(8,128)}, f32[64,1,16,128]{3,2,0,1:T(8,128)S(1)}, u32[]{:S(2)}) copy-start(f32[64,1,16,128]{3,2,0,1:T(8,128)S(1)} %get-tuple-element.52) | copy-start | bytes 1572868
  65.4 15.2 %collective-permute-start.3 = (f32[3,64,1,16,2]{1,3,4,2,0:T(8,128)}, f32[3,64,1,16,2]{1,3,4,2,0:T(8,128)}, u32[]{:S(2)}, u32[]{:S(2)}) collective-permute-start(f32[3,64,1,16,2]{1,3,4,2,0:T(8,128)} %copy.107), channel_id=1, source_target_pairs={{0,2},{2,4},{4,6},{6,8},{8,10},{10,12},{12,14},{14,16},{16,18},{18... | collective-permute-start | bytes 73736 | tf_op jit(solution)/shard_map/ppermute | solution.py:11
  65.4 13.7 %collective-permute-start.2 = (f32[3,64,1,16,2]{1,3,4,2,0:T(8,128)}, f32[3,64,1,16,2]{1,3,4,2,0:T(8,128)}, u32[]{:S(2)}, u32[]{:S(2)}) collective-permute-start(f32[3,64,1,16,2]{1,3,4,2,0:T(8,128)} %copy.105), channel_id=1, source_target_pairs={{0,254},{2,0},{4,2},{6,4},{8,6},{10,8},{12,10},{14,12},{16,14},{18... | collective-permute-start | bytes 73736 | tf_op jit(solution)/shard_map/ppermute | solution.py:11
  75.5 10.6 %collective-permute-start = (f32[3,64,1,2,128]{4,3,1,2,0:T(2,128)}, f32[3,64,1,2,128]{4,3,1,2,0:T(2,128)S(1)}, u32[]{:S(2)}, u32[]{:S(2)}) collective-permute-start(f32[3,64,1,2,128]{4,3,1,2,0:T(2,128)} %get-tuple-element.45), channel_id=1, source_target_pairs={{0,248},{2,250},{4,252},{6,254},{8,0},{10,2},{12,4},{14,6},{16,8},... | collective-permute-start | bytes 589832 | tf_op jit(solution)/shard_map/ppermute | solution.py:11
  78.0 10.8 %collective-permute-start.1 = (f32[3,64,1,2,128]{4,3,1,2,0:T(2,128)}, f32[3,64,1,2,128]{4,3,1,2,0:T(2,128)S(1)}, u32[]{:S(2)}, u32[]{:S(2)}) collective-permute-start(f32[3,64,1,2,128]{4,3,1,2,0:T(2,128)} %get-tuple-element.46), channel_id=1, source_target_pairs={{0,8},{2,10},{4,12},{6,14},{8,16},{10,18},{12,20},{14,22},{16,24},... | collective-permute-start | bytes 589832 | tf_op jit(solution)/shard_map/ppermute | solution.py:11
  83.2 5.6 %copy-start.2 = (f32[64,1,16,128]{3,2,0,1:T(8,128)S(1)}, f32[64,1,16,128]{3,2,0,1:T(8,128)}, u32[]{:S(2)}) copy-start(f32[64,1,16,128]{3,2,0,1:T(8,128)} %copy-done.1) | copy-start | bytes 1572868
  83.2 5.6 %copy-start.5 = (f32[64,1,16,128]{3,2,1,0:T(8,128)S(1)}, f32[64,1,16,128]{3,2,1,0:T(8,128)}, u32[]{:S(2)}) copy-start(f32[64,1,16,128]{3,2,1,0:T(8,128)} %param.10) | copy-start | bytes 1572868
Sparse Core Ops, SparseCore 0:
  10.7 41.7 all-gather.1
where the time goes:
time: 105 us; the launch traced here: 104 us
  waiting for transfers between devices  43.3 us (41%)
  local copies, waits for them, and re-layouts  20.2 us (19%)
  other arithmetic  14.3 us (14%)
  between operations  14.2 us (14%)
  starting transfers between devices  9.53 us (9%)
  matrix products  2.86 us (3%)
    all_gather x1, waiting for transfers between devices, on_device(): lax.all_gather(stacked, 'lev', axis=1, tiled=True)  40.6 us
    ppermute x4, starting transfers between devices, passed_along(): lax.ppermute(array, axis, [(i, (i + by) % devices) for i in range(devices)])  9.5 us
    unnamed x27, local copies, waits for them, and re-layouts  5.46 us
    slice x2, local copies, waits for them, and re-layouts, widen(): right_rim = passed_along(second_fields[:, :, :, :, :2], 'cols', -1)  4.31 us
    ppermute x2, local copies, waits for them, and re-layouts, passed_along(): lax.ppermute(array, axis, [(i, (i + by) % devices) for i in range(devices)])  4.15 us
    unnamed x1, other arithmetic  4.12 us
    div x1, other arithmetic, slope_second(): (8.0 * (wide[..., 3:-1] - wide[..., 1:-3]) - (wide[..., 4:] - wide[..., :...  2.94 us
    concatenate x1, other arithmetic, widen(): wide_second = jnp.concatenate([left_rim, second_fields, right_rim], axis=4)  2.89 us
  transfers between devices with their start and end apart: 5, of which 2 were waited for; matrix products, arithmetic and copies ran while one was open for 11% of the time, Pallas kernels for 0%

commit v1 on v0

v1 whole, which is shorter than its diff:
```python
import jax
import jax.numpy as jnp
from jax import lax
from jax.experimental import pallas as pl
from jax.experimental.pallas import tpu as pltpu
from jax.sharding import PartitionSpec as P

TW = 4
f32 = jnp.float32
bf16 = jnp.bfloat16
VMEM = pl.BlockSpec(memory_space=pltpu.VMEM)


def passed_along(array, axis, by):
    devices = lax.axis_size(axis)
    return lax.ppermute(array, axis, [(i, (i + by) % devices) for i in range(devices)])


def split(x):
    high = x.astype(bf16)
    return high, (x - high.astype(f32)).astype(bf16)


def split3(x):
    high = x.astype(bf16)
    rest = x - high.astype(f32)
    middle = rest.astype(bf16)
    return high, middle, (rest - middle.astype(f32)).astype(bf16)


def call(kernel, name, outs, scratch, *args, flops=0):
    shapes = tuple(jax.ShapeDtypeStruct(s, f32) for s in outs)
    size = sum(a.size for a in args) + sum(s.size for s in shapes)
    return pl.pallas_call(
        kernel,
        out_shape=shapes,
        in_specs=[VMEM] * len(args),
        out_specs=(VMEM,) * len(shapes),
        scratch_shapes=scratch,
        name=name,
        cost_estimate=pl.CostEstimate(flops=flops, bytes_accessed=4 * size, transcendentals=0),
        compiler_params=pltpu.CompilerParams(vmem_limit_bytes=32 << 20),
    )(*args)


def row(ref, i, levels, px):
    return ref[pl.ds(i, levels, stride=px), :]


def own_rows_transposed(a_ref, at_ref, me, levels):
    rows = jnp.concatenate(
        [a_ref[pl.ds(me * levels, levels), :], a_ref[pl.ds((2 + me) * levels, levels), :]], axis=0
    )
    at_ref[...] = rows.T


def paired(w_ref, t_ref, i, levels, px):
    halves = []
    for d in range(2):
        x = jnp.concatenate([row(w_ref, i + d, levels, px), row(t_ref, i + d, levels, px)], axis=0)
        halves.append(jnp.concatenate(split(x), axis=0))
    return jnp.concatenate(halves, axis=1)


def left_factor(blocks):
    high, low = split(jnp.concatenate(blocks, axis=0))
    return jnp.concatenate(
        [jnp.concatenate([high, high], axis=1), jnp.concatenate([low, low], axis=1)], axis=0
    )


def solve_first(px, w_ref, t_ref, a_ref, o_ref, at_ref):
    levels = o_ref.shape[1]
    py = o_ref.shape[2]
    me = lax.axis_index("lev")
    own_rows_transposed(a_ref, at_ref, me, levels)
    left = left_factor([at_ref[pl.ds((3 - me) * levels, levels), :]])
    for i in range(0, px, 2):
        r = jnp.dot(left, paired(w_ref, t_ref, i, levels, px), preferred_element_type=f32)
        r = r[:levels] + r[levels:]
        o_ref[i] = r[:, :py]
        o_ref[i + 1] = r[:, py:]


def solve_rest(px, w_ref, t_ref, a_ref, ow_ref, mt_ref, mw_ref, at_ref):
    levels = mt_ref.shape[1]
    py = mt_ref.shape[2]
    me = lax.axis_index("lev")
    own_rows_transposed(a_ref, at_ref, me, levels)
    left = left_factor(
        [
            at_ref[pl.ds((1 - me) * levels, levels), :],
            at_ref[pl.ds((2 + me) * levels, levels), :],
            at_ref[pl.ds(me * levels, levels), :],
        ]
    )
    for i in range(0, px, 2):
        r = jnp.dot(left, paired(w_ref, t_ref, i, levels, px), preferred_element_type=f32)
        r = r[: 3 * levels] + r[3 * levels :]
        for d in range(2):
            part = r[:, d * py : (d + 1) * py]
            ow_ref[pl.ds(i + d, levels, stride=px), :] = part[:levels]
            mt_ref[i + d] = part[levels : 2 * levels]
            mw_ref[pl.ds(i + d, levels, stride=px), :] = part[2 * levels :]


def iota2(shape, dim):
    return lax.broadcasted_iota(jnp.int32, shape, dim)


def rim_selector(py):
    k = iota2((8, py), 0)
    j = iota2((8, py), 1)
    want = jnp.where(k < 2, k, py - 4 + k)
    return jnp.where((j == want) & (k < 4), 1.0, 0.0).astype(bf16)


def rims(field, selector):
    total = 0.0
    for piece in split3(field):
        total = total + lax.dot_general(
            selector, piece, (((1,), (1,)), ((), ())), preferred_element_type=f32
        )
    return total


def pack(px, u_ref, v_ref, p_ref, q_ref, up_ref, down_ref, right_ref, left_ref):
    levels = up_ref.shape[2]
    py = up_ref.shape[3]
    for d in range(2):
        for out, i in ((up_ref, px - 2 + d), (down_ref, d)):
            out[0, d] = row(u_ref, i, levels, px)
            out[1, d] = row(p_ref, i, levels, px) * row(q_ref, i, levels, px)
    selector = rim_selector(py)
    v_rims = rims(v_ref[...], selector)
    p_rims = rims(p_ref[...] * q_ref[...], selector)
    left_ref[0:2] = v_rims[0:2]
    left_ref[2:4] = p_rims[0:2]
    right_ref[0:2] = v_rims[2:4]
    right_ref[2:4] = p_rims[2:4]


def band(py):
    k = iota2((py, py), 0)
    j = iota2((py, py), 1)
    d = k - j
    one = jnp.where(d == 1, 8.0, jnp.where(d == -1, -8.0, 0.0))
    two = jnp.where(d == 2, -1.0, jnp.where(d == -2, 1.0, 0.0))
    return (one + two).astype(bf16)


def rim_band(py):
    k = iota2((4, py), 0)
    j = iota2((4, py), 1)
    d = jnp.where(k < 2, k - 2, py - 2 + k) - j
    one = jnp.where(d == 1, 8.0, jnp.where(d == -1, -8.0, 0.0))
    two = jnp.where(d == 2, -1.0, jnp.where(d == -2, 1.0, 0.0))
    return (one + two).astype(bf16)


def second_slope(field, rim):
    py = field.shape[1]
    center = band(py)
    edge = rim_band(py)
    total = 0.0
    for piece in split(field):
        total = total + jnp.dot(piece, center, preferred_element_type=f32)
    for piece in split(rim):
        total = total + lax.dot_general(
            piece, edge, (((0,), (0,)), ((), ())), preferred_element_type=f32
        )
    return total * (1.0 / 12.0)


def first_slope(rows, i):
    return (8.0 * (rows(i + 1) - rows(i - 1)) - (rows(i + 2) - rows(i - 2))) * (1.0 / 12.0)


def update(px, u_ref, v_ref, p_ref, g_ref, q_ref, before_ref, after_ref, lrim_ref, rrim_ref,
           uo_ref, vo_ref, po_ref, pr_ref, gv_ref):
    levels = before_ref.shape[2]
    pressure = p_ref[...] * q_ref[...]
    pr_ref[...] = pressure
    prim = jnp.concatenate([lrim_ref[2:4], rrim_ref[2:4]], axis=0)
    vo_ref[...] = v_ref[...] + second_slope(pressure, prim)
    vrim = jnp.concatenate([lrim_ref[0:2], rrim_ref[0:2]], axis=0)
    gv_ref[...] = second_slope(v_ref[...], vrim)

    def reader(ref, at):
        def rows(i):
            if i < 0:
                return before_ref[at, i + 2]
            if i >= px:
                return after_ref[at, i - px]
            return row(ref, i, levels, px)

        return rows

    u_rows = reader(u_ref, 0)
    p_rows = reader(pr_ref, 1)
    for i in range(px):
        here = pl.ds(i, levels, stride=px)
        uo_ref[here, :] = u_ref[here, :] + first_slope(p_rows, i)
        po_ref[here, :] = p_ref[here, :] + g_ref[here, :] * (
            first_slope(u_rows, i) + gv_ref[here, :]
        )


def theta_pack(px, got_ref, mine_ref, wf_ref, ws_ref, star_ref, up_ref, down_ref, right_ref, left_ref,
               second_ref):
    levels = got_ref.shape[1]
    py = got_ref.shape[2]
    for i in range(px):
        star = got_ref[i] + mine_ref[i]
        star_ref[i] = star
        second_ref[pl.ds(i * levels, levels), :] = row(ws_ref, i, levels, px) * star
        if i < 2:
            down_ref[i] = row(wf_ref, i, levels, px) * star
        if i >= px - 2:
            up_ref[i - px + 2] = row(wf_ref, i, levels, px) * star
    got = rims(second_ref[...], rim_selector(py))
    left_ref[...] = got[0:2]
    right_ref[...] = got[2:4]


def theta_finish(px, star_ref, wf_ref, ws_ref, before_ref, after_ref, lrim_ref, rrim_ref, o_ref,
                 first_ref, second_ref):
    levels = star_ref.shape[1]
    first_ref[0:2] = before_ref[...]
    first_ref[px + 2 :] = after_ref[...]
    for i in range(px):
        star = star_ref[i]
        first_ref[i + 2] = row(wf_ref, i, levels, px) * star
        second_ref[pl.ds(i * levels, levels), :] = row(ws_ref, i, levels, px) * star
    rim = jnp.concatenate([lrim_ref[...], rrim_ref[...]], axis=0)
    second_ref[...] = second_slope(second_ref[...], rim)

    def rows(i):
        return first_ref[i + 2]

    for i in range(px):
        o_ref[pl.ds(i, levels, stride=px), :] = (
            star_ref[i] + first_slope(rows, i) + second_ref[pl.ds(i * levels, levels), :]
        )


def kernel_for(px, body):
    def kernel(*refs):
        body(px, *refs)

    return kernel


def on_device(u, v, w, t, p, grad, squeeze, wind_first, wind_second, a):
    levels, _, px, py = u.shape
    cells = levels * px
    u2, v2, w2, t2, p2, g2, q2, wf2, ws2 = (
        x.reshape(cells, py) for x in (u, v, w, t, p, grad, squeeze, wind_first, wind_second)
    )
    at = pltpu.VMEM((4 * levels, 2 * levels), f32)
    column = (px, levels, py)
    (other_t,) = call(kernel_for(px, solve_first), "solve_first", [column], [at], w2, t2, a)
    got_t = passed_along(other_t, "lev", 1)
    up, down, right, left = call(
        kernel_for(px, pack), "pack",
        [(2, 2, levels, py), (2, 2, levels, py), (4, cells), (4, cells)], [], u2, v2, p2, q2)
    before = passed_along(up, "cols", TW)
    after = passed_along(down, "cols", -TW)
    lrim = passed_along(right, "cols", 1)
    rrim = passed_along(left, "cols", -1)
    other_w, mine_t, mine_w = call(
        kernel_for(px, solve_rest), "solve_rest", [(cells, py), column, (cells, py)], [at], w2, t2, a)
    got_w = passed_along(other_w, "lev", 1)
    u_out, v_out, p_out = call(
        kernel_for(px, update), "update", [(cells, py)] * 3,
        [pltpu.VMEM((cells, py), f32)] * 2, u2, v2, p2, g2, q2, before, after, lrim, rrim)
    star, up, down, right, left = call(
        kernel_for(px, theta_pack), "theta_pack",
        [column, (2, levels, py), (2, levels, py), (2, cells), (2, cells)],
        [pltpu.VMEM((cells, py), f32)], got_t, mine_t, wf2, ws2)
    before = passed_along(up, "cols", TW)
    after = passed_along(down, "cols", -TW)
    lrim = passed_along(right, "cols", 1)
    rrim = passed_along(left, "cols", -1)
    (theta_out,) = call(
        kernel_for(px, theta_finish), "theta_finish", [(cells, py)],
        [pltpu.VMEM((px + 4, levels, py), f32), pltpu.VMEM((cells, py), f32)],
        star, wf2, ws2, before, after, lrim, rrim)
    w_out = mine_w + got_w
    return tuple(x.reshape(u.shape) for x in (u_out, v_out, w_out, theta_out, p_out))


def solution(mesh):
    spread = P("lev", "cols", None, None)
    return jax.shard_map(
        on_device,
        mesh=mesh,
        in_specs=(spread,) * 9 + (P(),),
        out_specs=(spread,) * 5,
        check_vma=False,
    )
```

time: 105 us -> 45.9 us (0.44)
  the two profiles are of different devices: /device:TPU:2 before, /device:TPU:4 now
where the time goes in v1:
time: 45.9 us; the launch traced here: 45.6 us
  starting transfers between devices  31.1 us (68%)
  Pallas kernels  7.15 us (16%)
  local copies, waits for them, and re-layouts  3.06 us (7%)
  waiting for transfers between devices  2.76 us (6%)
  other arithmetic  0.85 us (2%)
  between operations  0.74 us (2%)
    ppermute x10, starting transfers between devices, passed_along(): lax.ppermute(array, axis, [(i, (i + by) % devices) for i in range(devices)])  31.1 us
    pallas_call x6, Pallas kernels, call(): pl.pallas_call(kernel, out_shape=shapes, in_specs=[VMEM] * len(args), out...  7.15 us
    unnamed x20, local copies, waits for them, and re-layouts  3.06 us
    ppermute x10, waiting for transfers between devices, passed_along(): lax.ppermute(array, axis, [(i, (i + by) % devices) for i in range(devices)])  2.76 us
  transfers between devices with their start and end apart: 10, of which 2 were waited for; matrix products, arithmetic and copies ran while one was open for 2% of the time, Pallas kernels for 11%

profile of v1, /device:TPU:4, one launch (start us, length us, event | category | flops | bytes accessed | tf_op | source)
XLA Modules:
  0.0 45.6 jit_solution(8436149735175957308)
XLA Ops:
  0.6 1.0 %copy-done = f32[64,1,16,128]{3,2,1,0:T(8,128)S(1)} copy-done((f32[64,1,16,128]{3,2,1,0:T(8,128)S(1)}, f32[64,1,16,128]{3,2,1,0:T(8,128)}, u32[]{:S(2)}) %copy-start) | copy-done | bytes 524312
  1.7 1.0 %copy-done.1 = f32[64,1,16,128]{3,2,1,0:T(8,128)S(1)} copy-done((f32[64,1,16,128]{3,2,1,0:T(8,128)S(1)}, f32[64,1,16,128]{3,2,1,0:T(8,128)}, u32[]{:S(2)}) %copy-start.1) | copy-done | bytes 524312
  2.7 0.9 %copy-done.8 = f32[256,256]{1,0:T(8,128)S(1)} copy-done((f32[256,256]{1,0:T(8,128)S(1)}, f32[256,256]{1,0:T(8,128)}, u32[]{:S(2)}) %copy-start.8) | copy-done | bytes 262168
  3.7 0.6 %solve_first.1 = f32[16,64,128]{2,1,0:T(8,128)S(1)} custom-call(f32[1024,128]{1,0:T(8,128)S(1)} %bitcast.24, f32[1024,128]{1,0:T(8,128)S(1)} %bitcast.26, f32[256,256]{1,0:T(8,128)S(1)} %copy-done.8), custom_call_target="tpu_custom_call" | custom-call | bytes 1835008 | tf_op jit(solution)/shard_map/solve_first/pallas_call | solution.py:34
  4.2 0.0 copy-start.4
  4.2 0.0 copy-start.5
  4.3 2.3 %collective-permute-start.5 = (f32[16,64,128]{2,1,0:T(8,128)S(1)}, f32[16,64,128]{2,1,0:T(8,128)S(1)}, u32[]{:S(2)}, u32[]{:S(2)}) collective-permute-start(f32[16,64,128]{2,1,0:T(8,128)S(1)} %solve_first.1), channel_id=1, source_target_pairs={{0,1},{1,0},{2,3},{3,2},{4,5},{5,4},{6,7},{7,6},{8,9},{9,8},{10,11... | collective-permute-start | bytes 1572872 | tf_op jit(solution)/shard_map/ppermute | solution.py:16
  6.6 0.8 %solve_rest.1 = (f32[1024,128]{1,0:T(8,128)S(1)}, f32[16,64,128]{2,1,0:T(8,128)S(1)}, f32[1024,128]{1,0:T(8,128)S(1)}) custom-call(f32[1024,128]{1,0:T(8,128)S(1)} %bitcast.25, f32[1024,128]{1,0:T(8,128)S(1)} %bitcast.27, f32[256,256]{1,0:T(8,128)S(1)} %copy-done.8), custom_call_target="tpu_custom_call" | custom-call | bytes 2883584 | tf_op jit(solution)/shard_map/solve_rest/pallas_call | solution.py:34
  7.4 1.4 %collective-permute-start.4 = (f32[1024,128]{1,0:T(8,128)S(1)}, f32[1024,128]{1,0:T(8,128)S(1)}, u32[]{:S(2)}, u32[]{:S(2)}) collective-permute-start(f32[1024,128]{1,0:T(8,128)S(1)} %get-tuple-element.27), channel_id=1, source_target_pairs={{0,1},{1,0},{2,3},{3,2},{4,5},{5,4},{6,7},{7,6},{8,9},{9,8},{10,11... | collective-permute-start | bytes 1572872 | tf_op jit(solution)/shard_map/ppermute | solution.py:16
  8.8 0.0 copy-start.2
  8.8 0.0 copy-start.3
  8.8 0.6 %pack.1 = (f32[2,2,64,128]{3,2,1,0:T(8,128)S(1)}, f32[2,2,64,128]{3,2,1,0:T(8,128)S(1)}, f32[4,1024]{1,0:T(4,128)S(1)}, f32[4,1024]{1,0:T(4,128)S(1)}) custom-call(f32[1024,128]{1,0:T(8,128)S(1)} %bitcast.32, f32[1024,128]{1,0:T(8,128)S(1)} %bitcast.34, f32[1024,128]{1,0:T(8,128)S(1)} %bitcast.36, f32[1024,128]{1,0:T(8,128)S(1)} %bitcast.38), custom_call_target="tpu_custom_call" | custom-call | bytes 2392064 | tf_op jit(solution)/shard_map/pack/pallas_call | solution.py:34
  9.5 3.2 %collective-permute-start = (f32[2,2,64,128]{3,2,1,0:T(8,128)S(1)}, f32[2,2,64,128]{3,2,1,0:T(8,128)S(1)}, u32[]{:S(2)}, u32[]{:S(2)}) collective-permute-start(f32[2,2,64,128]{3,2,1,0:T(8,128)S(1)} %get-tuple-element.20), channel_id=1, source_target_pairs={{0,8},{2,10},{4,12},{6,14},{8,16},{10,18},{12,20},{14,22},{16,24},... | collective-permute-start | bytes 393224 | tf_op jit(solution)/shard_map/ppermute | solution.py:16
  12.7 6.0 %collective-permute-start.1 = (f32[2,2,64,128]{3,2,1,0:T(8,128)S(1)}, f32[2,2,64,128]{3,2,1,0:T(8,128)S(1)}, u32[]{:S(2)}, u32[]{:S(2)}) collective-permute-start(f32[2,2,64,128]{3,2,1,0:T(8,128)S(1)} %get-tuple-element.21), channel_id=1, source_target_pairs={{0,248},{2,250},{4,252},{6,254},{8,0},{10,2},{12,4},{14,6},{16,8},... | collective-permute-start | bytes 393224 | tf_op jit(solution)/shard_map/ppermute | solution.py:16
  18.7 1.9 %collective-permute-done.5.refs_0_ = f32[16,64,128]{2,1,0:T(8,128)S(1)} collective-permute-done((f32[16,64,128]{2,1,0:T(8,128)S(1)}, f32[16,64,128]{2,1,0:T(8,128)S(1)}, u32[]{:S(2)}, u32[]{:S(2)}) %collective-permute-start.5) | collective-permute-done | bytes 524320 | tf_op jit(solution)/shard_map/ppermute | solution.py:16
  20.7 6.4 %collective-permute-start.3 = (f32[4,1024]{1,0:T(4,128)S(1)}, f32[4,1024]{1,0:T(4,128)S(1)}, u32[]{:S(2)}, u32[]{:S(2)}) collective-permute-start(f32[4,1024]{1,0:T(4,128)S(1)} %get-tuple-element.23), channel_id=1, source_target_pairs={{0,254},{2,0},{4,2},{6,4},{8,6},{10,8},{12,10},{14,12},{16,14},{18... | collective-permute-start | bytes 49160 | tf_op jit(solution)/shard_map/ppermute | solution.py:16
  27.0 0.5 %theta_pack.1 = (f32[16,64,128]{2,1,0:T(8,128)S(1)}, f32[2,64,128]{2,1,0:T(8,128)S(1)}, f32[2,64,128]{2,1,0:T(8,128)S(1)}, f32[2,1024]{1,0:T(2,128)S(1)}, f32[2,1024]{1,0:T(2,128)S(1)}) custom-call(f32[16,64,128]{2,1,0:T(8,128)S(1)} %collective-permute-done.5.refs_0_, f32[16,64,128]{2,1,0:T(8,128)S(1)} %get-tuple-element.28.refs_1_, ...), custom_call_target="tpu_custom_call" | custom-call | bytes 2768896 | tf_op jit(solution)/shard_map/theta_pack/pallas_call | solution.py:34
  27.6 0.1 collective-permute-start.6
  27.7 0.8 %collective-permute-done.3.refs_8_ = f32[4,1024]{1,0:T(4,128)S(1)} collective-permute-done((f32[4,1024]{1,0:T(4,128)S(1)}, f32[4,1024]{1,0:T(4,128)S(1)}, u32[]{:S(2)}, u32[]{:S(2)}) %collective-permute-start.3) | collective-permute-done | bytes 16416 | tf_op jit(solution)/shard_map/ppermute | solution.py:16
  28.5 5.7 %collective-permute-start.7 = (f32[2,64,128]{2,1,0:T(8,128)S(1)}, f32[2,64,128]{2,1,0:T(8,128)S(1)}, u32[]{:S(2)}, u32[]{:S(2)}) collective-permute-start(f32[2,64,128]{2,1,0:T(8,128)S(1)} %get-tuple-element.31), channel_id=1, source_target_pairs={{0,248},{2,250},{4,252},{6,254},{8,0},{10,2},{12,4},{14,6},{16,8},... | collective-permute-start | bytes 196616 | tf_op jit(solution)/shard_map/ppermute | solution.py:16
  34.2 6.0 %collective-permute-start.9 = (f32[2,1024]{1,0:T(2,128)S(1)}, f32[2,1024]{1,0:T(2,128)S(1)}, u32[]{:S(2)}, u32[]{:S(2)}) collective-permute-start(f32[2,1024]{1,0:T(2,128)S(1)} %get-tuple-element.33), channel_id=1, source_target_pairs={{0,254},{2,0},{4,2},{6,4},{8,6},{10,8},{12,10},{14,12},{16,14},{18... | collective-permute-start | bytes 24584 | tf_op jit(solution)/shard_map/ppermute | solution.py:16
  40.2 2.9 %update.1 = (f32[1024,128]{1,0:T(8,128)}, f32[1024,128]{1,0:T(8,128)}, f32[1024,128]{1,0:T(8,128)}) custom-call(f32[1024,128]{1,0:T(8,128)S(1)} %bitcast.33, f32[1024,128]{1,0:T(8,128)S(1)} %bitcast.35, f32[1024,128]{1,0:T(8,128)S(1)} %bitcast.37, f32[1024,128]{1,0:T(8,128)S(1)} %bitcast.40, f32[1024,128]{1,0:T(8,128)S(1)} %bitcast.39, ...), custom_call_target="tpu_custom_call" | custom-call | bytes 4489216 | tf_op jit(solution)/shard_map/update/pallas_call | solution.py:34
  43.1 0.8 %add.3 = f32[1024,128]{1,0:T(8,128)} add(f32[1024,128]{1,0:T(8,128)S(1)} %get-tuple-element.26, f32[1024,128]{1,0:T(8,128)S(1)} %collective-permute-done.4) | non-fusion elementwise | flops 131072 | bytes 1572864 | tf_op jit(solution)/shard_map/add | solution.py:289
  44.0 1.7 %theta_finish.1 = f32[1024,128]{1,0:T(8,128)} custom-call(f32[16,64,128]{2,1,0:T(8,128)S(1)} %get-tuple-element.29.refs_0_, f32[1024,128]{1,0:T(8,128)S(1)} %bitcast.29, f32[1024,128]{1,0:T(8,128)S(1)} %bitcast.31, f32[2,64,128]{2,1,0:T(8,128)S(1)} %collective-permute-done.6.refs_3_, f32[2,64,128]{2,1,0:T(8,128)S(1)} %collective-permute-done.7.refs_4_, ...), custom_call_target="tpu_custom_call" | custom-call | bytes 2244608 | tf_op jit(solution)/shard_map/theta_finish/pallas_call | solution.py:34
  (23 shorter events, 0.1 us)
Async XLA Ops:
  0.6 1.0 %copy-start = (f32[64,1,16,128]{3,2,1,0:T(8,128)S(1)}, f32[64,1,16,128]{3,2,1,0:T(8,128)}, u32[]{:S(2)}) copy-start(f32[64,1,16,128]{3,2,1,0:T(8,128)} %param.12) | copy-start | bytes 1572868
  1.7 1.0 %copy-start.1 = (f32[64,1,16,128]{3,2,1,0:T(8,128)S(1)}, f32[64,1,16,128]{3,2,1,0:T(8,128)}, u32[]{:S(2)}) copy-start(f32[64,1,16,128]{3,2,1,0:T(8,128)} %param.13) | copy-start | bytes 1572868
  2.7 0.9 %copy-start.8 = (f32[256,256]{1,0:T(8,128)S(1)}, f32[256,256]{1,0:T(8,128)}, u32[]{:S(2)}) copy-start(f32[256,256]{1,0:T(8,128)} %refs_2_.3) | copy-start | bytes 786436
  3.7 5.1 %copy-start.6 = (f32[64,1,16,128]{3,2,1,0:T(8,128)S(1)}, f32[64,1,16,128]{3,2,1,0:T(8,128)}, u32[]{:S(2)}) copy-start(f32[64,1,16,128]{3,2,1,0:T(8,128)} %param.14) | copy-start | bytes 1572868
  3.7 5.1 %copy-start.7 = (f32[64,1,16,128]{3,2,1,0:T(8,128)S(1)}, f32[64,1,16,128]{3,2,1,0:T(8,128)}, u32[]{:S(2)}) copy-start(f32[64,1,16,128]{3,2,1,0:T(8,128)} %param.16) | copy-start | bytes 1572868
  4.2 4.6 %copy-start.4 = (f32[64,1,16,128]{3,2,1,0:T(8,128)S(1)}, f32[64,1,16,128]{3,2,1,0:T(8,128)}, u32[]{:S(2)}) copy-start(f32[64,1,16,128]{3,2,1,0:T(8,128)} %param.10) | copy-start | bytes 1572868
  4.2 4.6 %copy-start.5 = (f32[64,1,16,128]{3,2,1,0:T(8,128)S(1)}, f32[64,1,16,128]{3,2,1,0:T(8,128)}, u32[]{:S(2)}) copy-start(f32[64,1,16,128]{3,2,1,0:T(8,128)} %param.11) | copy-start | bytes 1572868
  4.3 16.4 %collective-permute-start.5 = (f32[16,64,128]{2,1,0:T(8,128)S(1)}, f32[16,64,128]{2,1,0:T(8,128)S(1)}, u32[]{:S(2)}, u32[]{:S(2)}) collective-permute-start(f32[16,64,128]{2,1,0:T(8,128)S(1)} %solve_first.1), channel_id=1, source_target_pairs={{0,1},{1,0},{2,3},{3,2},{4,5},{5,4},{6,7},{7,6},{8,9},{9,8},{10,11... | collective-permute-start | bytes 1572872 | tf_op jit(solution)/shard_map/ppermute | solution.py:16
  7.4 35.7 %collective-permute-start.4 = (f32[1024,128]{1,0:T(8,128)S(1)}, f32[1024,128]{1,0:T(8,128)S(1)}, u32[]{:S(2)}, u32[]{:S(2)}) collective-permute-start(f32[1024,128]{1,0:T(8,128)S(1)} %get-tuple-element.27), channel_id=1, source_target_pairs={{0,1},{1,0},{2,3},{3,2},{4,5},{5,4},{6,7},{7,6},{8,9},{9,8},{10,11... | collective-permute-start | bytes 1572872 | tf_op jit(solution)/shard_map/ppermute | solution.py:16
  8.8 18.2 %copy-start.2 = (f32[64,1,16,128]{3,2,1,0:T(8,128)S(1)}, f32[64,1,16,128]{3,2,1,0:T(8,128)}, u32[]{:S(2)}) copy-start(f32[64,1,16,128]{3,2,1,0:T(8,128)} %param.17) | copy-start | bytes 1572868
  8.8 18.2 %copy-start.3 = (f32[64,1,16,128]{3,2,1,0:T(8,128)S(1)}, f32[64,1,16,128]{3,2,1,0:T(8,128)}, u32[]{:S(2)}) copy-start(f32[64,1,16,128]{3,2,1,0:T(8,128)} %param.18) | copy-start | bytes 1572868
  9.5 24.7 %collective-permute-start = (f32[2,2,64,128]{3,2,1,0:T(8,128)S(1)}, f32[2,2,64,128]{3,2,1,0:T(8,128)S(1)}, u32[]{:S(2)}, u32[]{:S(2)}) collective-permute-start(f32[2,2,64,128]{3,2,1,0:T(8,128)S(1)} %get-tuple-element.20), channel_id=1, source_target_pairs={{0,8},{2,10},{4,12},{6,14},{8,16},{10,18},{12,20},{14,22},{16,24},... | collective-permute-start | bytes 393224 | tf_op jit(solution)/shard_map/ppermute | solution.py:16
  12.7 21.5 %collective-permute-start.1 = (f32[2,2,64,128]{3,2,1,0:T(8,128)S(1)}, f32[2,2,64,128]{3,2,1,0:T(8,128)S(1)}, u32[]{:S(2)}, u32[]{:S(2)}) collective-permute-start(f32[2,2,64,128]{3,2,1,0:T(8,128)S(1)} %get-tuple-element.21), channel_id=1, source_target_pairs={{0,248},{2,250},{4,252},{6,254},{8,0},{10,2},{12,4},{14,6},{16,8},... | collective-permute-start | bytes 393224 | tf_op jit(solution)/shard_map/ppermute | solution.py:16
  18.7 8.9 %collective-permute-start.2 = (f32[4,1024]{1,0:T(4,128)S(1)}, f32[4,1024]{1,0:T(4,128)S(1)}, u32[]{:S(2)}, u32[]{:S(2)}) collective-permute-start(f32[4,1024]{1,0:T(4,128)S(1)} %get-tuple-element.22), channel_id=1, source_target_pairs={{0,2},{2,4},{4,6},{6,8},{8,10},{10,12},{12,14},{14,16},{16,18},{18... | collective-permute-start | bytes 49160 | tf_op jit(solution)/shard_map/ppermute | solution.py:16
  20.7 7.8 %collective-permute-start.3 = (f32[4,1024]{1,0:T(4,128)S(1)}, f32[4,1024]{1,0:T(4,128)S(1)}, u32[]{:S(2)}, u32[]{:S(2)}) collective-permute-start(f32[4,1024]{1,0:T(4,128)S(1)} %get-tuple-element.23), channel_id=1, source_target_pairs={{0,254},{2,0},{4,2},{6,4},{8,6},{10,8},{12,10},{14,12},{16,14},{18... | collective-permute-start | bytes 49160 | tf_op jit(solution)/shard_map/ppermute | solution.py:16
  27.0 13.2 %copy-start.9 = (f32[64,1,16,128]{3,2,1,0:T(8,128)S(1)}, f32[64,1,16,128]{3,2,1,0:T(8,128)}, u32[]{:S(2)}) copy-start(f32[64,1,16,128]{3,2,1,0:T(8,128)} %param.15) | copy-start | bytes 1572868
  27.6 16.4 %collective-permute-start.6 = (f32[2,64,128]{2,1,0:T(8,128)S(1)}, f32[2,64,128]{2,1,0:T(8,128)S(1)}, u32[]{:S(2)}, u32[]{:S(2)}) collective-permute-start(f32[2,64,128]{2,1,0:T(8,128)S(1)} %get-tuple-element.30), channel_id=1, source_target_pairs={{0,8},{2,10},{4,12},{6,14},{8,16},{10,18},{12,20},{14,22},{16,24},... | collective-permute-start | bytes 196616 | tf_op jit(solution)/shard_map/ppermute | solution.py:16
  28.5 15.5 %collective-permute-start.7 = (f32[2,64,128]{2,1,0:T(8,128)S(1)}, f32[2,64,128]{2,1,0:T(8,128)S(1)}, u32[]{:S(2)}, u32[]{:S(2)}) collective-permute-start(f32[2,64,128]{2,1,0:T(8,128)S(1)} %get-tuple-element.31), channel_id=1, source_target_pairs={{0,248},{2,250},{4,252},{6,254},{8,0},{10,2},{12,4},{14,6},{16,8},... | collective-permute-start | bytes 196616 | tf_op jit(solution)/shard_map/ppermute | solution.py:16
  34.2 9.7 %collective-permute-start.8 = (f32[2,1024]{1,0:T(2,128)S(1)}, f32[2,1024]{1,0:T(2,128)S(1)}, u32[]{:S(2)}, u32[]{:S(2)}) collective-permute-start(f32[2,1024]{1,0:T(2,128)S(1)} %get-tuple-element.32), channel_id=1, source_target_pairs={{0,2},{2,4},{4,6},{6,8},{8,10},{10,12},{12,14},{14,16},{16,18},{18... | collective-permute-start | bytes 24584 | tf_op jit(solution)/shard_map/ppermute | solution.py:16
  34.2 9.7 %collective-permute-start.9 = (f32[2,1024]{1,0:T(2,128)S(1)}, f32[2,1024]{1,0:T(2,128)S(1)}, u32[]{:S(2)}, u32[]{:S(2)}) collective-permute-start(f32[2,1024]{1,0:T(2,128)S(1)} %get-tuple-element.33), channel_id=1, source_target_pairs={{0,254},{2,0},{4,2},{6,4},{8,6},{10,8},{12,10},{14,12},{16,14},{18... | collective-permute-start | bytes 24584 | tf_op jit(solution)/shard_map/ppermute | solution.py:16

commit v2 on v1

v2 whole, which is shorter than its diff:
```python
import jax
import jax.numpy as jnp
from jax import lax
from jax.experimental import pallas as pl
from jax.experimental.pallas import tpu as pltpu
from jax.sharding import PartitionSpec as P

TW = 4
FIRST_LIMIT = (53 << 20) + (640 << 10)
LONG = 12_000_000_000
W_COST = 0
T_COST = 0
F_COST = 0
f32 = jnp.float32
bf16 = jnp.bfloat16
VMEM = pl.BlockSpec(memory_space=pltpu.VMEM)


def passed_along(array, axis, by):
    devices = lax.axis_size(axis)
    return lax.ppermute(array, axis, [(i, (i + by) % devices) for i in range(devices)])


def split(x):
    high = x.astype(bf16)
    return high, (x - high.astype(f32)).astype(bf16)


def split3(x):
    high = x.astype(bf16)
    rest = x - high.astype(f32)
    middle = rest.astype(bf16)
    return high, middle, (rest - middle.astype(f32)).astype(bf16)


HBM = pl.BlockSpec(memory_space=pl.ANY)


def call(kernel, name, outs, scratch, *args, flops=0, in_space=VMEM, out_space=VMEM, limit=32 << 20, after=()):
    shapes = tuple(jax.ShapeDtypeStruct(s, f32) for s in outs)
    size = sum(a.size for a in args) + sum(s.size for s in shapes)

    def body(*refs):
        kernel(*refs[: len(args)], *refs[len(args) + len(after) :])

    return pl.pallas_call(
        body,
        out_shape=shapes,
        in_specs=[in_space] * len(args) + [HBM] * len(after),
        out_specs=out_space if isinstance(out_space, tuple) else (out_space,) * len(shapes),
        scratch_shapes=scratch,
        name=name,
        cost_estimate=pl.CostEstimate(flops=flops, bytes_accessed=4 * size, transcendentals=0),
        compiler_params=pltpu.CompilerParams(vmem_limit_bytes=limit),
    )(*args, *after)


def row(ref, i, levels, px):
    return ref[pl.ds(i, levels, stride=px), :]


def own_rows_transposed(a_ref, at_ref, me, levels):
    rows = jnp.concatenate(
        [a_ref[pl.ds(me * levels, levels), :], a_ref[pl.ds((2 + me) * levels, levels), :]], axis=0
    )
    at_ref[...] = rows.T


def left_factor(blocks):
    high, low = split(jnp.concatenate(blocks, axis=0))
    return jnp.concatenate(
        [jnp.concatenate([high, high], axis=1), jnp.concatenate([low, low], axis=1)], axis=0
    )


def paired(pieces):
    halves = []
    for w_part, t_part in pieces:
        halves.append(jnp.concatenate(split(jnp.concatenate([w_part, t_part], axis=0)), axis=0))
    return jnp.concatenate(halves, axis=1)


def iota2(shape, dim):
    return lax.broadcasted_iota(jnp.int32, shape, dim)


def rim_selector(py):
    k = iota2((8, py), 0)
    j = iota2((8, py), 1)
    want = jnp.where(k < 2, k, py - 4 + k)
    return jnp.where((j == want) & (k < 4), 1.0, 0.0).astype(bf16)


def rims(field, selector):
    total = 0.0
    for piece in split3(field):
        total = total + lax.dot_general(
            selector, piece, (((1,), (1,)), ((), ())), preferred_element_type=f32
        )
    return total


def rim_slot(i, px):
    return i if i < 2 else i - px + 4


def sender(sems):
    copies = []

    def send(source, target):
        copy = pltpu.make_async_copy(source, target, sems.at[len(copies)])
        copy.start()
        copies.append(copy)

    return copies, send


def solve_theta(px, w_hbm, t_hbm, a_hbm, rim_ref, inner_hbm, w_ref, t_ref, a_ref, at_ref, full_ref,
                inner_ref, sems):
    cells, py = w_hbm.shape
    levels = cells // px
    copies, send = sender(sems)
    send(a_hbm, a_ref)
    send(w_hbm, w_ref)
    send(t_hbm, t_ref)
    me = lax.axis_index("lev")
    copies[0].wait()
    own_rows_transposed(a_ref, at_ref, me, levels)
    left = left_factor([at_ref[pl.ds((3 - me) * levels, levels), :]])
    copies[1].wait()
    copies[2].wait()
    for i in [*range(2, px - 2, 2), 0, px - 2]:
        if i == 0:
            send(inner_ref, inner_hbm)
        right = paired([(row(w_ref, i + d, levels, px), row(t_ref, i + d, levels, px)) for d in range(2)])
        r = jnp.dot(left, right, preferred_element_type=f32)
        r = r[:levels] + r[levels:]
        for d in range(2):
            part = r[:, d * py : (d + 1) * py]
            full_ref[pl.ds(i + d, levels, stride=px), :] = part
            if 2 <= i < px - 2:
                inner_ref[i + d - 2] = part
            else:
                rim_ref[pl.ds(rim_slot(i + d, px) * levels, levels), :] = part
    edges = rims(full_ref[...], rim_selector(py))
    for k in range(levels * px // py):
        rim_ref[pl.ds(4 * levels + 4 * k, 4), :] = edges[0:4, k * py : (k + 1) * py]
    copies[3].wait()


def solve_rest(px, w_ref, t_ref, a_ref, ow_ref, mw_ref, mt_ref, at_ref):
    levels = w_ref.shape[0] // px
    py = w_ref.shape[1]
    me = lax.axis_index("lev")
    own_rows_transposed(a_ref, at_ref, me, levels)
    left = left_factor(
        [
            at_ref[pl.ds((1 - me) * levels, levels), :],
            at_ref[pl.ds(me * levels, levels), :],
            at_ref[pl.ds((2 + me) * levels, levels), :],
        ]
    )
    for i in range(0, px, 2):
        right = paired([(row(w_ref, i + d, levels, px), row(t_ref, i + d, levels, px)) for d in range(2)])
        r = jnp.dot(left, right, preferred_element_type=f32)
        r = r[: 3 * levels] + r[3 * levels :]
        for d in range(2):
            part = r[:, d * py : (d + 1) * py]
            here = pl.ds(i + d, levels, stride=px)
            ow_ref[here, :] = part[:levels]
            mw_ref[here, :] = part[levels : 2 * levels]
            mt_ref[here, :] = part[2 * levels :]


def pack_rows(px, first, u_ref, p_ref, q_ref, wf_ref, mt_ref, got_ref, out):
    levels = out.shape[2]
    start = (1 - first) * (px - 2)
    for d in range(2):
        i = start + d
        out[0, d] = row(u_ref, i, levels, px)
        out[1, d] = row(p_ref, i, levels, px) * row(q_ref, i, levels, px)
        star = row(mt_ref, i, levels, px) + got_ref[pl.ds(((1 - first) * 2 + d) * levels, levels), :]
        out[2, d] = row(wf_ref, i, levels, px) * star


def pack_even(px, u_ref, p_ref, q_ref, wf_ref, mt_ref, got_ref, e4_ref):
    odd4 = lax.rem(lax.div(lax.axis_index("cols"), TW), 2)
    pack_rows(px, odd4, u_ref, p_ref, q_ref, wf_ref, mt_ref, got_ref, e4_ref)


def pack(px, u_ref, v_ref, p_ref, q_ref, wf_ref, ws_ref, mt_ref, got_ref, o4_ref, e1_ref, o1_ref):
    levels = o4_ref.shape[2]
    py = o4_ref.shape[3]
    cols = lax.axis_index("cols")
    odd4 = lax.rem(lax.div(cols, TW), 2)
    odd1 = lax.rem(cols, 2)
    pack_rows(px, 1 - odd4, u_ref, p_ref, q_ref, wf_ref, mt_ref, got_ref, o4_ref)
    selector = rim_selector(py)
    got_rims = jnp.concatenate(
        [got_ref[pl.ds(4 * levels + 4 * k, 4), :] for k in range(levels * px // py)], axis=1
    )
    v_rims = rims(v_ref[...], selector)[0:4]
    p_rims = rims(p_ref[...] * q_ref[...], selector)[0:4]
    t_rims = rims(ws_ref[...], selector)[0:4] * (rims(mt_ref[...], selector)[0:4] + got_rims)
    first = jnp.concatenate([v_rims[0:2], p_rims[0:2], t_rims[0:2], t_rims[0:2]], axis=0)
    last = jnp.concatenate([v_rims[2:4], p_rims[2:4], t_rims[2:4], t_rims[2:4]], axis=0)
    is_odd = odd1 == 1
    e1_ref[...] = jnp.where(is_odd, first, last)
    o1_ref[...] = jnp.where(is_odd, last, first)


def band(py):
    k = iota2((py, py), 0)
    j = iota2((py, py), 1)
    d = k - j
    one = jnp.where(d == 1, 8.0, jnp.where(d == -1, -8.0, 0.0))
    two = jnp.where(d == 2, -1.0, jnp.where(d == -2, 1.0, 0.0))
    return (one + two).astype(bf16)


def rim_band(py):
    k = iota2((4, py), 0)
    j = iota2((4, py), 1)
    d = jnp.where(k < 2, k - 2, py - 2 + k) - j
    one = jnp.where(d == 1, 8.0, jnp.where(d == -1, -8.0, 0.0))
    two = jnp.where(d == 2, -1.0, jnp.where(d == -2, 1.0, 0.0))
    return (one + two).astype(bf16)


def second_inner(field):
    center = band(field.shape[1])
    total = 0.0
    for piece in split(field):
        total = total + jnp.dot(piece, center, preferred_element_type=f32)
    return total * (1.0 / 12.0)


def second_rim(rim, py):
    edge = rim_band(py)
    total = 0.0
    for piece in split(rim):
        total = total + lax.dot_general(
            piece, edge, (((0,), (0,)), ((), ())), preferred_element_type=f32
        )
    return total * (1.0 / 12.0)


def first_inner(rows, i, px):
    one = rows(i + 1) if i + 1 < px else 0.0
    one = one - rows(i - 1) if i >= 1 else one
    two = rows(i + 2) if i + 2 < px else 0.0
    two = two - rows(i - 2) if i >= 2 else two
    return (8.0 * one - two) * (1.0 / 12.0)


def first_rim(i, before, after, px):
    if i == 0:
        return (before[0] - 8.0 * before[1]) * (1.0 / 12.0)
    if i == 1:
        return before[1] * (1.0 / 12.0)
    if i == px - 2:
        return after[0] * (-1.0 / 12.0)
    return (8.0 * after[0] - after[1]) * (1.0 / 12.0)


def first_inner(rows, i, px):
    one = rows(i + 1) if i + 1 < px else 0.0
    one = one - rows(i - 1) if i >= 1 else one
    two = rows(i + 2) if i + 2 < px else 0.0
    two = two - rows(i - 2) if i >= 2 else two
    return (8.0 * one - two) * (1.0 / 12.0)


def first_rim(i, before, after, px):
    if i == 0:
        return (before[0] - 8.0 * before[1]) * (1.0 / 12.0)
    if i == 1:
        return before[1] * (1.0 / 12.0)
    if i == px - 2:
        return after[0] * (-1.0 / 12.0)
    return (8.0 * after[0] - after[1]) * (1.0 / 12.0)


def winds_inner(px, u_ref, v_ref, p_ref, g_ref, q_ref, uo_ref, vo_ref, po_ref, pr_ref, gv_ref):
    levels = u_ref.shape[0] // px
    pressure = p_ref[...] * q_ref[...]
    pr_ref[...] = pressure
    vo_ref[...] = v_ref[...] + second_inner(pressure)
    gv_ref[...] = second_inner(v_ref[...])

    def u_rows(i):
        return row(u_ref, i, levels, px)

    def p_rows(i):
        return row(pr_ref, i, levels, px)

    for i in range(px):
        here = pl.ds(i, levels, stride=px)
        uo_ref[here, :] = u_ref[here, :] + first_inner(p_rows, i, px)
        po_ref[here, :] = p_ref[here, :] + g_ref[here, :] * (
            first_inner(u_rows, i, px) + gv_ref[here, :]
        )


def theta_inner(px, rim_ref, inner_ref, mt_ref, wf_ref, ws_ref, o_ref, star_ref, first_ref):
    levels = inner_ref.shape[1]
    for i in range(px):
        if 2 <= i < px - 2:
            got = inner_ref[i - 2]
        else:
            got = rim_ref[pl.ds(rim_slot(i, px) * levels, levels), :]
        star = got + row(mt_ref, i, levels, px)
        star_ref[pl.ds(i, levels, stride=px), :] = star
        first_ref[i] = row(wf_ref, i, levels, px) * star
    star = star_ref[...]
    star_ref[...] = star + second_inner(ws_ref[...] * star)

    def rows(i):
        return first_ref[i]

    for i in range(px):
        here = pl.ds(i, levels, stride=px)
        o_ref[here, :] = star_ref[here, :] + first_inner(rows, i, px)


def halo_rows(e4_ref, o4_ref, at, odd):
    before = [jnp.where(odd, e4_ref[at, d], o4_ref[at, d]) for d in range(2)]
    after = [jnp.where(odd, o4_ref[at, d], e4_ref[at, d]) for d in range(2)]
    return before, after


def halo_columns(e1_ref, o1_ref, at, odd):
    e1 = e1_ref[2 * at : 2 * at + 2]
    o1 = o1_ref[2 * at : 2 * at + 2]
    return jnp.concatenate([jnp.where(odd, e1, o1), jnp.where(odd, o1, e1)], axis=0)


def parities():
    cols = lax.axis_index("cols")
    return lax.rem(lax.div(cols, TW), 2) == 1, lax.rem(cols, 2) == 1


def finish(px, ub_ref, vb_ref, pb_ref, g_ref, tb_ref, e4_ref, o4_ref, e1_ref, o1_ref,
           u_hbm, v_hbm, t_hbm, p_hbm, u_ref, v_ref, t_ref, p_ref, sems):
    cells, py = ub_ref.shape
    levels = cells // px
    odd4, odd1 = parities()
    copies, send = sender(sems)
    edge_rows = (0, 1, px - 2, px - 1)
    u_ref[...] = ub_ref[...]
    before, after = halo_rows(e4_ref, o4_ref, 1, odd4)
    for i in edge_rows:
        here = pl.ds(i, levels, stride=px)
        u_ref[here, :] = ub_ref[here, :] + first_rim(i, before, after, px)
    send(u_ref, u_hbm)
    v_ref[...] = vb_ref[...] + second_rim(halo_columns(e1_ref, o1_ref, 1, odd1), py)
    send(v_ref, v_hbm)
    t_ref[...] = tb_ref[...] + second_rim(halo_columns(e1_ref, o1_ref, 2, odd1), py)
    before, after = halo_rows(e4_ref, o4_ref, 2, odd4)
    for i in edge_rows:
        here = pl.ds(i, levels, stride=px)
        t_ref[here, :] = t_ref[here, :] + first_rim(i, before, after, px)
    send(t_ref, t_hbm)
    p_ref[...] = pb_ref[...] + g_ref[...] * second_rim(halo_columns(e1_ref, o1_ref, 0, odd1), py)
    before, after = halo_rows(e4_ref, o4_ref, 0, odd4)
    for i in edge_rows:
        here = pl.ds(i, levels, stride=px)
        p_ref[here, :] = p_ref[here, :] + g_ref[here, :] * first_rim(i, before, after, px)
    send(p_ref, p_hbm)
    for copy in copies:
        copy.wait()


def kernel_for(px, body):
    def kernel(*refs):
        body(px, *refs)

    return kernel


def exchange(array, step, odd_pairs):
    devices = lax.axis_size("cols")
    pairs = []
    for c in range(devices):
        up = ((c // step) % 2 == 1) == odd_pairs
        pairs.append((c, (c + step if up else c - step) % devices))
    return lax.ppermute(array, "cols", pairs)


def on_device(u, v, w, t, p, grad, squeeze, wind_first, wind_second, a):
    levels, _, px, py = u.shape
    cells = levels * px
    u2, v2, w2, t2, p2, g2, q2, wf2, ws2 = (
        x.reshape(cells, py) for x in (u, v, w, t, p, grad, squeeze, wind_first, wind_second)
    )
    at = pltpu.VMEM((4 * levels, 2 * levels), f32)
    flat = (cells, py)
    rim_rows = 4 * levels + 4 * (cells // py)
    rim_shape = (rim_rows, py)
    inner_shape = (px - 4, levels, py)
    rim_t, inner_t = call(
        kernel_for(px, solve_theta), "solve_theta", [rim_shape, inner_shape],
        [pltpu.VMEM(flat, f32), pltpu.VMEM(flat, f32), pltpu.VMEM(a.shape, f32), at,
         pltpu.VMEM(flat, f32), pltpu.VMEM(inner_shape, f32), pltpu.SemaphoreType.DMA((4,))],
        w2, t2, a, in_space=HBM, out_space=(VMEM, HBM), limit=FIRST_LIMIT, flops=LONG)
    got_rim = passed_along(rim_t, "lev", 1)
    got_inner = passed_along(inner_t, "lev", 1)
    other_w, mine_w, mine_t = call(
        kernel_for(px, solve_rest), "solve_rest", [flat] * 3, [at], w2, t2, a, flops=LONG, after=(rim_t,))
    o4, e1, o1 = call(
        kernel_for(px, pack), "pack", [(3, 2, levels, py)] + [(8, cells)] * 2, [],
        u2, v2, p2, q2, wf2, ws2, mine_t, got_rim, flops=LONG, after=(other_w,))
    (e4,) = call(
        kernel_for(px, pack_even), "pack_even", [(3, 2, levels, py)], [],
        u2, p2, q2, wf2, mine_t, got_rim, flops=LONG, after=(o1,))
    got_w = passed_along(other_w, "lev", 1)
    halos = (exchange(e4, TW, False), exchange(o4, TW, True), exchange(e1, 1, False), exchange(o1, 1, True))
    u_in, v_in, p_in = call(
        kernel_for(px, winds_inner), "winds_inner", [flat] * 3, [pltpu.VMEM(flat, f32)] * 2,
        u2, v2, p2, g2, q2, after=(e4,), flops=W_COST)
    (t_in,) = call(
        kernel_for(px, theta_inner), "theta_inner", [flat],
        [pltpu.VMEM(flat, f32), pltpu.VMEM((px, levels, py), f32)],
        got_rim, got_inner, mine_t, wf2, ws2, flops=T_COST)
    w_out = mine_w + got_w
    u_out, v_out, theta_out, p_out = call(
        kernel_for(px, finish), "finish", [flat] * 4,
        [pltpu.VMEM(flat, f32)] * 4 + [pltpu.SemaphoreType.DMA((4,))],
        u_in, v_in, p_in, g2, t_in, *halos, out_space=HBM, flops=F_COST)
    outs = (u_out, v_out, w_out, theta_out, p_out)
    return tuple(x.reshape(u.shape) for x in outs)


def solution(mesh):
    spread = P("lev", "cols", None, None)
    return jax.shard_map(
        on_device,
        mesh=mesh,
        in_specs=(spread,) * 9 + (P(),),
        out_specs=(spread,) * 5,
        check_vma=False,
    )
```

time: 45.9 us -> 35.7 us (0.78)
  the two profiles are of different devices: /device:TPU:4 before, /device:TPU:24 now
where the time goes in v2:
time: 35.7 us; the launch traced here: 35.6 us
  starting transfers between devices  17.1 us (48%)
  Pallas kernels  9.54 us (27%)
  waiting for transfers between devices  7.27 us (20%)
  other arithmetic  0.85 us (2%)
  between operations  0.78 us (2%)
    ppermute x4, starting transfers between devices, exchange(): return lax.ppermute(array, 'cols', pairs)  10.3 us
    pallas_call x7, Pallas kernels, call(): pl.pallas_call(body, out_shape=shapes, in_specs=[in_space] * len(args) +...  9.54 us
    ppermute x3, starting transfers between devices, passed_along(): lax.ppermute(array, axis, [(i, (i + by) % devices) for i in range(devices)])  6.81 us
    ppermute x3, waiting for transfers between devices, passed_along(): lax.ppermute(array, axis, [(i, (i + by) % devices) for i in range(devices)])  6.06 us
    ppermute x4, waiting for transfers between devices, exchange(): return lax.ppermute(array, 'cols', pairs)  1.21 us
    add x1, other arithmetic, on_device(): w_out = mine_w + got_w  0.85 us
  transfers between devices with their start and end apart: 7, of which 3 were waited for; matrix products, arithmetic and copies ran while one was open for 0% of the time, Pallas kernels for 19%

profile of v2, /device:TPU:24, one launch (start us, length us, event | category | flops | bytes accessed | tf_op | source)
XLA Modules:
  0.0 35.6 jit_solution(9024399199794672804)
XLA Ops:
  0.7 2.7 %solve_theta.1 = (f32[288,128]{1,0:T(8,128)S(1)}, f32[12,64,128]{2,1,0:T(8,128)}) custom-call(f32[1024,128]{1,0:T(8,128)} %bitcast.42, f32[1024,128]{1,0:T(8,128)} %bitcast.44, f32[256,256]{1,0:T(8,128)} %refs_2_.3), custom_call_target="tpu_custom_call" | custom-call | flops 12000000000 | bytes 1851392 | tf_op jit(solution)/shard_map/solve_theta/pallas_call | solution.py:46
  3.4 3.1 %collective-permute-start = (f32[288,128]{1,0:T(8,128)S(1)}, f32[288,128]{1,0:T(8,128)S(1)}, u32[]{:S(2)}, u32[]{:S(2)}) collective-permute-start(f32[288,128]{1,0:T(8,128)S(1)} %get-tuple-element.20.refs_3_), channel_id=1, source_target_pairs={{0,1},{1,0},{2,3},{3,2},{4,5},{5,4},{6,7},{7,6},{8,9},{9,8},{10,11... | collective-permute-start | bytes 442376 | tf_op jit(solution)/shard_map/ppermute | solution.py:21
  6.5 0.0 copy-start.5
  6.5 0.0 copy-start.6
  6.5 0.6 %collective-permute-start.1 = (f32[12,64,128]{2,1,0:T(8,128)}, f32[12,64,128]{2,1,0:T(8,128)S(1)}, u32[]{:S(2)}, u32[]{:S(2)}) collective-permute-start(f32[12,64,128]{2,1,0:T(8,128)} %get-tuple-element.27), channel_id=1, source_target_pairs={{0,1},{1,0},{2,3},{3,2},{4,5},{5,4},{6,7},{7,6},{8,9},{9,8},{10,11... | collective-permute-start | bytes 1179656 | tf_op jit(solution)/shard_map/ppermute | solution.py:21
  7.1 0.9 %solve_rest.1 = (f32[1024,128]{1,0:T(8,128)S(1)}, f32[1024,128]{1,0:T(8,128)S(1)}, f32[1024,128]{1,0:T(8,128)S(1)}) custom-call(f32[1024,128]{1,0:T(8,128)S(1)} %bitcast.43, f32[1024,128]{1,0:T(8,128)S(1)} %bitcast.45, f32[256,256]{1,0:T(8,128)S(1)} %copy-done.9, f32[288,128]{1,0:T(8,128)S(1)} %get-tuple-element.20.refs_3_), custom_call_target="tpu_custom_call" | custom-call | flops 12000000000 | bytes 2883584 | tf_op jit(solution)/shard_map/solve_rest/pallas_call | solution.py:46
  8.0 3.1 %collective-permute-start.6 = (f32[1024,128]{1,0:T(8,128)S(1)}, f32[1024,128]{1,0:T(8,128)S(1)}, u32[]{:S(2)}, u32[]{:S(2)}) collective-permute-start(f32[1024,128]{1,0:T(8,128)S(1)} %get-tuple-element.22.refs_8_), channel_id=1, source_target_pairs={{0,1},{1,0},{2,3},{3,2},{4,5},{5,4},{6,7},{7,6},{8,9},{9,8},{10,11... | collective-permute-start | bytes 1572872 | tf_op jit(solution)/shard_map/ppermute | solution.py:21
  11.1 0.0 collective-permute-done.refs_7_.refs_5_.refs_0_
  11.2 1.0 %pack.1 = (f32[3,2,64,128]{3,2,1,0:T(8,128)S(1)}, f32[8,1024]{1,0:T(8,128)S(1)}, f32[8,1024]{1,0:T(8,128)S(1)}) custom-call(f32[1024,128]{1,0:T(8,128)S(1)} %bitcast.31, f32[1024,128]{1,0:T(8,128)S(1)} %bitcast.34, f32[1024,128]{1,0:T(8,128)S(1)} %bitcast.36, f32[1024,128]{1,0:T(8,128)S(1)} %bitcast.39, f32[1024,128]{1,0:T(8,128)S(1)} %bitcast.26, ...), custom_call_target="tpu_custom_call" | custom-call | flops 12000000000 | bytes 4079616 | tf_op jit(solution)/shard_map/pack/pallas_call | solution.py:46
  12.2 2.7 %collective-permute-start.3 = (f32[3,2,64,128]{3,2,1,0:T(8,128)S(1)}, f32[3,2,64,128]{3,2,1,0:T(8,128)S(1)}, u32[]{:S(2)}, u32[]{:S(2)}) collective-permute-start(f32[3,2,64,128]{3,2,1,0:T(8,128)S(1)} %get-tuple-element.28), channel_id=1, source_target_pairs={{0,248},{2,250},{4,252},{6,254},{8,16},{10,18},{12,20},{14,22},{16... | collective-permute-start | bytes 589832 | tf_op jit(solution)/shard_map/ppermute | solution.py:387
  14.8 0.2 pack_even.1.refs_5_
  15.0 7.6 %collective-permute-start.2 = (f32[3,2,64,128]{3,2,1,0:T(8,128)S(1)}, f32[3,2,64,128]{3,2,1,0:T(8,128)S(1)}, u32[]{:S(2)}, u32[]{:S(2)}) collective-permute-start(f32[3,2,64,128]{3,2,1,0:T(8,128)S(1)} %pack_even.1.refs_5_), channel_id=1, source_target_pairs={{0,8},{2,10},{4,12},{6,14},{8,0},{10,2},{12,4},{14,6},{16,24},{18,... | collective-permute-start | bytes 589832 | tf_op jit(solution)/shard_map/ppermute | solution.py:387
  22.6 0.0 collective-permute-start.4
  22.6 0.8 %collective-permute-done.1.refs_1_ = f32[12,64,128]{2,1,0:T(8,128)S(1)} collective-permute-done((f32[12,64,128]{2,1,0:T(8,128)}, f32[12,64,128]{2,1,0:T(8,128)S(1)}, u32[]{:S(2)}, u32[]{:S(2)}) %collective-permute-start.1) | collective-permute-done | bytes 393248 | tf_op jit(solution)/shard_map/ppermute | solution.py:21
  23.5 0.0 collective-permute-start.5
  23.5 1.5 %winds_inner.1 = (f32[1024,128]{1,0:T(8,128)S(1)}, f32[1024,128]{1,0:T(8,128)S(1)}, f32[1024,128]{1,0:T(8,128)S(1)}) custom-call(f32[1024,128]{1,0:T(8,128)S(1)} %bitcast.33, f32[1024,128]{1,0:T(8,128)S(1)} %bitcast.35, f32[1024,128]{1,0:T(8,128)S(1)} %bitcast.38, f32[1024,128]{1,0:T(8,128)S(1)} %bitcast.24, f32[1024,128]{1,0:T(8,128)S(1)} %bitcast.41, ...), custom_call_target="tpu_custom_call" | custom-call | bytes 4194304 | tf_op jit(solution)/shard_map/winds_inner/pallas_call | solution.py:46
  25.0 1.0 %theta_inner.1.refs_4_ = f32[1024,128]{1,0:T(8,128)S(1)} custom-call(f32[288,128]{1,0:T(8,128)S(1)} %collective-permute-done.refs_7_.refs_5_.refs_0_, f32[12,64,128]{2,1,0:T(8,128)S(1)} %collective-permute-done.1.refs_1_, f32[1024,128]{1,0:T(8,128)S(1)} %get-tuple-element.21.refs_6_.refs_4_.refs_2_, f32[1024,128]{1,0:T(8,128)S(1)} %bitcast.28, ...), custom_call_target="tpu_custom_call" | custom-call | bytes 2637824 | tf_op jit(solution)/shard_map/theta_inner/pallas_call | solution.py:46
  26.0 0.0 collective-permute-done.4.refs_7_
  26.0 1.2 %collective-permute-done.5.refs_8_ = f32[8,1024]{1,0:T(8,128)S(1)} collective-permute-done((f32[8,1024]{1,0:T(8,128)S(1)}, f32[8,1024]{1,0:T(8,128)S(1)}, u32[]{:S(2)}, u32[]{:S(2)}) %collective-permute-start.5) | collective-permute-done | bytes 32800 | tf_op jit(solution)/shard_map/ppermute | solution.py:387
  27.2 0.0 collective-permute-done.3.refs_6_
  27.2 0.0 collective-permute-done.2.refs_5_
  27.2 2.3 %finish.1 = (f32[1024,128]{1,0:T(8,128)}, f32[1024,128]{1,0:T(8,128)}, f32[1024,128]{1,0:T(8,128)}, f32[1024,128]{1,0:T(8,128)}) custom-call(f32[1024,128]{1,0:T(8,128)S(1)} %get-tuple-element.24.refs_0_, f32[1024,128]{1,0:T(8,128)S(1)} %get-tuple-element.25.refs_1_, f32[1024,128]{1,0:T(8,128)S(1)} %get-tuple-element.26.refs_2_, f32[1024,128]{1,0:T(8,128)S(1)} %bitcast.25, ...), custom_call_target="tpu_custom_call" | custom-call | bytes 5177344 | tf_op jit(solution)/shard_map/finish/pallas_call | solution.py:46
  29.5 5.2 %collective-permute-done.6 = f32[1024,128]{1,0:T(8,128)S(1)} collective-permute-done((f32[1024,128]{1,0:T(8,128)S(1)}, f32[1024,128]{1,0:T(8,128)S(1)}, u32[]{:S(2)}, u32[]{:S(2)}) %collective-permute-start.6) | collective-permute-done | bytes 524320 | tf_op jit(solution)/shard_map/ppermute | solution.py:21
  34.8 0.8 %add.3 = f32[1024,128]{1,0:T(8,128)} add(f32[1024,128]{1,0:T(8,128)S(1)} %get-tuple-element.32, f32[1024,128]{1,0:T(8,128)S(1)} %collective-permute-done.6) | non-fusion elementwise | flops 131072 | bytes 1572864 | tf_op jit(solution)/shard_map/add | solution.py:425
  (18 shorter events, 0.0 us)
Async XLA Ops:
  0.6 6.5 %copy-start.7 = (f32[64,1,16,128]{3,2,1,0:T(8,128)S(1)}, f32[64,1,16,128]{3,2,1,0:T(8,128)}, u32[]{:S(2)}) copy-start(f32[64,1,16,128]{3,2,1,0:T(8,128)} %param.12) | copy-start | bytes 1572868
  0.6 6.5 %copy-start.8 = (f32[64,1,16,128]{3,2,1,0:T(8,128)S(1)}, f32[64,1,16,128]{3,2,1,0:T(8,128)}, u32[]{:S(2)}) copy-start(f32[64,1,16,128]{3,2,1,0:T(8,128)} %param.13) | copy-start | bytes 1572868
  0.7 6.4 %copy-start.9 = (f32[256,256]{1,0:T(8,128)S(1)}, f32[256,256]{1,0:T(8,128)}, u32[]{:S(2)}) copy-start(f32[256,256]{1,0:T(8,128)} %refs_2_.3) | copy-start | bytes 786436
  3.4 7.8 %collective-permute-start = (f32[288,128]{1,0:T(8,128)S(1)}, f32[288,128]{1,0:T(8,128)S(1)}, u32[]{:S(2)}, u32[]{:S(2)}) collective-permute-start(f32[288,128]{1,0:T(8,128)S(1)} %get-tuple-element.20.refs_3_), channel_id=1, source_target_pairs={{0,1},{1,0},{2,3},{3,2},{4,5},{5,4},{6,7},{7,6},{8,9},{9,8},{10,11... | collective-permute-start | bytes 442376 | tf_op jit(solution)/shard_map/ppermute | solution.py:21
  6.5 4.7 %copy-start.1 = (f32[64,1,16,128]{3,2,1,0:T(8,128)S(1)}, f32[64,1,16,128]{3,2,1,0:T(8,128)}, u32[]{:S(2)}) copy-start(f32[64,1,16,128]{3,2,1,0:T(8,128)} %param.17) | copy-start | bytes 1572868
  6.5 4.7 %copy-start.2 = (f32[64,1,16,128]{3,2,1,0:T(8,128)S(1)}, f32[64,1,16,128]{3,2,1,0:T(8,128)}, u32[]{:S(2)}) copy-start(f32[64,1,16,128]{3,2,1,0:T(8,128)} %param.18) | copy-start | bytes 1572868
  6.5 4.7 %copy-start.3 = (f32[64,1,16,128]{3,2,1,0:T(8,128)S(1)}, f32[64,1,16,128]{3,2,1,0:T(8,128)}, u32[]{:S(2)}) copy-start(f32[64,1,16,128]{3,2,1,0:T(8,128)} %param.10) | copy-start | bytes 1572868
  6.5 4.7 %copy-start.4 = (f32[64,1,16,128]{3,2,1,0:T(8,128)S(1)}, f32[64,1,16,128]{3,2,1,0:T(8,128)}, u32[]{:S(2)}) copy-start(f32[64,1,16,128]{3,2,1,0:T(8,128)} %param.11) | copy-start | bytes 1572868
  6.5 4.7 %copy-start.5 = (f32[64,1,16,128]{3,2,1,0:T(8,128)S(1)}, f32[64,1,16,128]{3,2,1,0:T(8,128)}, u32[]{:S(2)}) copy-start(f32[64,1,16,128]{3,2,1,0:T(8,128)} %param.14) | copy-start | bytes 1572868
  6.5 4.7 %copy-start.6 = (f32[64,1,16,128]{3,2,1,0:T(8,128)S(1)}, f32[64,1,16,128]{3,2,1,0:T(8,128)}, u32[]{:S(2)}) copy-start(f32[64,1,16,128]{3,2,1,0:T(8,128)} %param.16) | copy-start | bytes 1572868
  6.5 17.0 %collective-permute-start.1 = (f32[12,64,128]{2,1,0:T(8,128)}, f32[12,64,128]{2,1,0:T(8,128)S(1)}, u32[]{:S(2)}, u32[]{:S(2)}) collective-permute-start(f32[12,64,128]{2,1,0:T(8,128)} %get-tuple-element.27), channel_id=1, source_target_pairs={{0,1},{1,0},{2,3},{3,2},{4,5},{5,4},{6,7},{7,6},{8,9},{9,8},{10,11... | collective-permute-start | bytes 1179656 | tf_op jit(solution)/shard_map/ppermute | solution.py:21
  8.0 26.7 %collective-permute-start.6 = (f32[1024,128]{1,0:T(8,128)S(1)}, f32[1024,128]{1,0:T(8,128)S(1)}, u32[]{:S(2)}, u32[]{:S(2)}) collective-permute-start(f32[1024,128]{1,0:T(8,128)S(1)} %get-tuple-element.22.refs_8_), channel_id=1, source_target_pairs={{0,1},{1,0},{2,3},{3,2},{4,5},{5,4},{6,7},{7,6},{8,9},{9,8},{10,11... | collective-permute-start | bytes 1572872 | tf_op jit(solution)/shard_map/ppermute | solution.py:21
  12.2 15.1 %collective-permute-start.3 = (f32[3,2,64,128]{3,2,1,0:T(8,128)S(1)}, f32[3,2,64,128]{3,2,1,0:T(8,128)S(1)}, u32[]{:S(2)}, u32[]{:S(2)}) collective-permute-start(f32[3,2,64,128]{3,2,1,0:T(8,128)S(1)} %get-tuple-element.28), channel_id=1, source_target_pairs={{0,248},{2,250},{4,252},{6,254},{8,16},{10,18},{12,20},{14,22},{16... | collective-permute-start | bytes 589832 | tf_op jit(solution)/shard_map/ppermute | solution.py:387
  14.8 8.7 %copy-start = (f32[64,1,16,128]{3,2,1,0:T(8,128)S(1)}, f32[64,1,16,128]{3,2,1,0:T(8,128)}, u32[]{:S(2)}) copy-start(f32[64,1,16,128]{3,2,1,0:T(8,128)} %param.15) | copy-start | bytes 1572868
  15.0 12.2 %collective-permute-start.2 = (f32[3,2,64,128]{3,2,1,0:T(8,128)S(1)}, f32[3,2,64,128]{3,2,1,0:T(8,128)S(1)}, u32[]{:S(2)}, u32[]{:S(2)}) collective-permute-start(f32[3,2,64,128]{3,2,1,0:T(8,128)S(1)} %pack_even.1.refs_5_), channel_id=1, source_target_pairs={{0,8},{2,10},{4,12},{6,14},{8,0},{10,2},{12,4},{14,6},{16,24},{18,... | collective-permute-start | bytes 589832 | tf_op jit(solution)/shard_map/ppermute | solution.py:387
  22.6 3.4 %collective-permute-start.4 = (f32[8,1024]{1,0:T(8,128)S(1)}, f32[8,1024]{1,0:T(8,128)S(1)}, u32[]{:S(2)}, u32[]{:S(2)}) collective-permute-start(f32[8,1024]{1,0:T(8,128)S(1)} %get-tuple-element.29), channel_id=1, source_target_pairs={{0,2},{2,0},{4,6},{6,4},{8,10},{10,8},{12,14},{14,12},{16,18},{18,... | collective-permute-start | bytes 98312 | tf_op jit(solution)/shard_map/ppermute | solution.py:387
  23.5 3.8 %collective-permute-start.5 = (f32[8,1024]{1,0:T(8,128)S(1)}, f32[8,1024]{1,0:T(8,128)S(1)}, u32[]{:S(2)}, u32[]{:S(2)}) collective-permute-start(f32[8,1024]{1,0:T(8,128)S(1)} %get-tuple-element.23.refs_6_), channel_id=1, source_target_pairs={{0,254},{2,4},{4,2},{6,8},{8,6},{10,12},{12,10},{14,16},{16,14},{1... | collective-permute-start | bytes 98312 | tf_op jit(solution)/shard_map/ppermute | solution.py:387

commit v3 on v2

--- a/solution.py
+++ b/solution.py
@@ -9,6 +9,7 @@
 FIRST_LIMIT = (53 << 20) + (640 << 10)
 LONG = 12_000_000_000
 W_COST = 0
+I_COST = 0
 T_COST = 0
 F_COST = 0
 f32 = jnp.float32
@@ -115,8 +116,7 @@
     return copies, send
 
 
-def solve_theta(px, w_hbm, t_hbm, a_hbm, rim_ref, inner_hbm, w_ref, t_ref, a_ref, at_ref, full_ref,
-                inner_ref, sems):
+def solve_rim(px, w_hbm, t_hbm, a_hbm, rim_ref, w_ref, t_ref, a_ref, at_ref, full_ref, sems):
     cells, py = w_hbm.shape
     levels = cells // px
     copies, send = sender(sems)
@@ -129,47 +129,47 @@
     left = left_factor([at_ref[pl.ds((3 - me) * levels, levels), :]])
     copies[1].wait()
     copies[2].wait()
-    for i in [*range(2, px - 2, 2), 0, px - 2]:
-        if i == 0:
-            send(inner_ref, inner_hbm)
-        right = paired([(row(w_ref, i + d, levels, px), row(t_ref, i + d, levels, px)) for d in range(2)])
-        r = jnp.dot(left, right, preferred_element_type=f32)
-        r = r[:levels] + r[levels:]
-        for d in range(2):
-            part = r[:, d * py : (d + 1) * py]
-            full_ref[pl.ds(i + d, levels, stride=px), :] = part
-            if 2 <= i < px - 2:
-                inner_ref[i + d - 2] = part
-            else:
-                rim_ref[pl.ds(rim_slot(i + d, px) * levels, levels), :] = part
+    for i, part in solved(px, left, w_ref, t_ref):
+        full_ref[pl.ds(i, levels, stride=px), :] = part
+        if not 2 <= i < px - 2:
+            rim_ref[pl.ds(rim_slot(i, px) * levels, levels), :] = part
     edges = rims(full_ref[...], rim_selector(py))
     for k in range(levels * px // py):
         rim_ref[pl.ds(4 * levels + 4 * k, 4), :] = edges[0:4, k * py : (k + 1) * py]
-    copies[3].wait()
-
-
-def solve_rest(px, w_ref, t_ref, a_ref, ow_ref, mw_ref, mt_ref, at_ref):
+
+
+def solved(px, left, w_ref, t_ref):
     levels = w_ref.shape[0] // px
     py = w_ref.shape[1]
-    me = lax.axis_index("lev")
-    own_rows_transposed(a_ref, at_ref, me, levels)
-    left = left_factor(
-        [
-            at_ref[pl.ds((1 - me) * levels, levels), :],
-            at_ref[pl.ds(me * levels, levels), :],
-            at_ref[pl.ds((2 + me) * levels, levels), :],
-        ]
-    )
+    half = left.shape[0] // 2
     for i in range(0, px, 2):
         right = paired([(row(w_ref, i + d, levels, px), row(t_ref, i + d, levels, px)) for d in range(2)])
         r = jnp.dot(left, right, preferred_element_type=f32)
-        r = r[: 3 * levels] + r[3 * levels :]
-        for d in range(2):
-            part = r[:, d * py : (d + 1) * py]
-            here = pl.ds(i + d, levels, stride=px)
-            ow_ref[here, :] = part[:levels]
-            mw_ref[here, :] = part[levels : 2 * levels]
-            mt_ref[here, :] = part[2 * levels :]
+        r = r[:half] + r[half:]
+        yield i, r[:, :py]
+        yield i + 1, r[:, py:]
+
+
+def solve_inner(px, w_ref, t_ref, a_ref, inner_ref, mt_ref, at_ref):
+    levels = w_ref.shape[0] // px
+    me = lax.axis_index("lev")
+    own_rows_transposed(a_ref, at_ref, me, levels)
+    left = left_factor([at_ref[pl.ds((3 - me) * levels, levels), :], at_ref[pl.ds((2 + me) * levels, levels), :]])
+    for i, part in solved(px, left, w_ref, t_ref):
+        if 2 <= i < px - 2:
+            inner_ref[i - 2] = part[:levels]
+        mt_ref[pl.ds(i, levels, stride=px), :] = part[levels:]
+
+
+def solve_w(px, w_ref, t_ref, a_ref, ow_ref, mw_ref, at_ref):
+    levels = w_ref.shape[0] // px
+    me = lax.axis_index("lev")
+    own_rows_transposed(a_ref, at_ref, me, levels)
+    left = left_factor([at_ref[pl.ds((1 - me) * levels, levels), :], at_ref[pl.ds(me * levels, levels), :]])
+    for i, part in solved(px, left, w_ref, t_ref):
+        here = pl.ds(i, levels, stride=px)
+        ow_ref[here, :] = part[:levels]
+        mw_ref[here, :] = part[levels:]
 
 
 def pack_rows(px, first, u_ref, p_ref, q_ref, wf_ref, mt_ref, got_ref, out):
@@ -398,15 +398,18 @@
     rim_rows = 4 * levels + 4 * (cells // py)
     rim_shape = (rim_rows, py)
     inner_shape = (px - 4, levels, py)
-    rim_t, inner_t = call(
-        kernel_for(px, solve_theta), "solve_theta", [rim_shape, inner_shape],
+    (rim_t,) = call(
+        kernel_for(px, solve_rim), "solve_rim", [rim_shape],
         [pltpu.VMEM(flat, f32), pltpu.VMEM(flat, f32), pltpu.VMEM(a.shape, f32), at,
-         pltpu.VMEM(flat, f32), pltpu.VMEM(inner_shape, f32), pltpu.SemaphoreType.DMA((4,))],
-        w2, t2, a, in_space=HBM, out_space=(VMEM, HBM), limit=FIRST_LIMIT, flops=LONG)
+         pltpu.VMEM(flat, f32), pltpu.SemaphoreType.DMA((3,))],
+        w2, t2, a, in_space=HBM, limit=FIRST_LIMIT, flops=LONG)
+    inner_t, mine_t = call(
+        kernel_for(px, solve_inner), "solve_inner", [inner_shape, flat], [at], w2, t2, a,
+        after=(rim_t,), flops=I_COST)
     got_rim = passed_along(rim_t, "lev", 1)
     got_inner = passed_along(inner_t, "lev", 1)
-    other_w, mine_w, mine_t = call(
-        kernel_for(px, solve_rest), "solve_rest", [flat] * 3, [at], w2, t2, a, flops=LONG, after=(rim_t,))
+    other_w, mine_w = call(
+        kernel_for(px, solve_w), "solve_w", [flat] * 2, [at], w2, t2, a, flops=LONG, after=(inner_t,))
     o4, e1, o1 = call(
         kernel_for(px, pack), "pack", [(3, 2, levels, py)] + [(8, cells)] * 2, [],
         u2, v2, p2, q2, wf2, ws2, mine_t, got_rim, flops=LONG, after=(other_w,))

time: 35.7 us -> 35.8 us (level)
  starting transfers between devices: 17.1 us -> 16.1 us
  waiting for transfers between devices: 7.27 us -> 8.24 us
    ppermute x3, waiting for transfers between devices: 6.06 us -> 7.42 us  [passed_along(): lax.ppermute(array, axis, [(i, (i + by) % devices) for i in range(devices)])]
    ppermute x4, starting transfers between devices: 10.3 us -> 9.25 us  [exchange(): return lax.ppermute(array, 'cols', pairs)]
    ppermute x4, waiting for transfers between devices: 1.21 us -> 0.82 us  [exchange(): return lax.ppermute(array, 'cols', pairs)]
    pallas_call x7 -> x8, Pallas kernels: 9.54 us -> 9.64 us  [call(): pl.pallas_call(body, out_shape=shapes, in_specs=[in_space] * len(args) +...]
  transfers between devices with their start and end apart: 7 -> 7, of which waited for: 3 -> 3; matrix products, arithmetic and copies ran while one was open for 0% -> 0% of each run, Pallas kernels for 19% -> 20%
where the time goes in v3:
time: 35.8 us; the launch traced here: 35.7 us
  starting transfers between devices  16.1 us (45%)
  Pallas kernels  9.64 us (27%)
  waiting for transfers between devices  8.24 us (23%)
  other arithmetic  0.85 us (2%)
  between operations  0.81 us (2%)
    pallas_call x8, Pallas kernels, call(): pl.pallas_call(body, out_shape=shapes, in_specs=[in_space] * len(args) +...  9.64 us
    ppermute x4, starting transfers between devices, exchange(): return lax.ppermute(array, 'cols', pairs)  9.25 us
    ppermute x3, waiting for transfers between devices, passed_along(): lax.ppermute(array, axis, [(i, (i + by) % devices) for i in range(devices)])  7.42 us
    ppermute x3, starting transfers between devices, passed_along(): lax.ppermute(array, axis, [(i, (i + by) % devices) for i in range(devices)])  6.82 us
    add x1, other arithmetic, on_device(): w_out = mine_w + got_w  0.85 us
    ppermute x4, waiting for transfers between devices, exchange(): return lax.ppermute(array, 'cols', pairs)  0.82 us
  transfers between devices with their start and end apart: 7, of which 3 were waited for; matrix products, arithmetic and copies ran while one was open for 0% of the time, Pallas kernels for 20%

profile of v3, /device:TPU:24, one launch (start us, length us, event | category | flops | bytes accessed | tf_op | source)
XLA Modules:
  0.0 35.7 jit_solution(9263638407263568337)
XLA Ops:
  0.7 2.3 %solve_rim.1.refs_3_ = f32[288,128]{1,0:T(8,128)S(1)} custom-call(f32[1024,128]{1,0:T(8,128)} %bitcast.31, f32[1024,128]{1,0:T(8,128)} %bitcast.34, f32[256,256]{1,0:T(8,128)} %refs_2_.5), custom_call_target="tpu_custom_call" | custom-call | flops 12000000000 | bytes 1458176 | tf_op jit(solution)/shard_map/solve_rim/pallas_call | solution.py:47
  3.0 3.1 %collective-permute-start = (f32[288,128]{1,0:T(8,128)S(1)}, f32[288,128]{1,0:T(8,128)S(1)}, u32[]{:S(2)}, u32[]{:S(2)}) collective-permute-start(f32[288,128]{1,0:T(8,128)S(1)} %solve_rim.1.refs_3_), channel_id=1, source_target_pairs={{0,1},{1,0},{2,3},{3,2},{4,5},{5,4},{6,7},{7,6},{8,9},{9,8},{10,11... | collective-permute-start | bytes 442376 | tf_op jit(solution)/shard_map/ppermute | solution.py:22
  6.1 0.6 %solve_inner.1 = (f32[12,64,128]{2,1,0:T(8,128)S(1)}, f32[1024,128]{1,0:T(8,128)S(1)}) custom-call(f32[1024,128]{1,0:T(8,128)S(1)} %bitcast.32, f32[1024,128]{1,0:T(8,128)S(1)} %bitcast.35, f32[256,256]{1,0:T(8,128)S(1)} %copy-done.9, f32[288,128]{1,0:T(8,128)S(1)} %solve_rim.1.refs_3_), custom_call_target="tpu_custom_call" | custom-call | bytes 2228224 | tf_op jit(solution)/shard_map/solve_inner/pallas_call | solution.py:47
  6.8 0.0 copy-start.1
  6.8 0.0 copy-start.2
  6.8 0.0 copy-start.5
  6.8 0.0 copy-start.6
  6.8 0.0 copy-start.7
  6.8 0.0 copy-start.8
  6.8 0.6 %collective-permute-start.1 = (f32[12,64,128]{2,1,0:T(8,128)S(1)}, f32[12,64,128]{2,1,0:T(8,128)S(1)}, u32[]{:S(2)}, u32[]{:S(2)}) collective-permute-start(f32[12,64,128]{2,1,0:T(8,128)S(1)} %get-tuple-element.20.refs_3_), channel_id=1, source_target_pairs={{0,1},{1,0},{2,3},{3,2},{4,5},{5,4},{6,7},{7,6},{8,9},{9,8},{10,11... | collective-permute-start | bytes 1179656 | tf_op jit(solution)/shard_map/ppermute | solution.py:22
  7.4 0.7 %solve_w.1 = (f32[1024,128]{1,0:T(8,128)S(1)}, f32[1024,128]{1,0:T(8,128)S(1)}) custom-call(f32[1024,128]{1,0:T(8,128)S(1)} %bitcast.33, f32[1024,128]{1,0:T(8,128)S(1)} %bitcast.36, f32[256,256]{1,0:T(8,128)S(1)} %copy-done.9, f32[12,64,128]{2,1,0:T(8,128)S(1)} %get-tuple-element.20.refs_3_), custom_call_target="tpu_custom_call" | custom-call | flops 12000000000 | bytes 2359296 | tf_op jit(solution)/shard_map/solve_w/pallas_call | solution.py:47
  8.2 3.1 %collective-permute-start.6 = (f32[1024,128]{1,0:T(8,128)S(1)}, f32[1024,128]{1,0:T(8,128)S(1)}, u32[]{:S(2)}, u32[]{:S(2)}) collective-permute-start(f32[1024,128]{1,0:T(8,128)S(1)} %get-tuple-element.21.refs_8_), channel_id=1, source_target_pairs={{0,1},{1,0},{2,3},{3,2},{4,5},{5,4},{6,7},{7,6},{8,9},{9,8},{10,11... | collective-permute-start | bytes 1572872 | tf_op jit(solution)/shard_map/ppermute | solution.py:22
  11.3 0.0 collective-permute-done.refs_7_.refs_5_.refs_0_
  11.3 1.0 %pack.1 = (f32[3,2,64,128]{3,2,1,0:T(8,128)S(1)}, f32[8,1024]{1,0:T(8,128)S(1)}, f32[8,1024]{1,0:T(8,128)S(1)}) custom-call(f32[1024,128]{1,0:T(8,128)S(1)} %bitcast.37, f32[1024,128]{1,0:T(8,128)S(1)} %bitcast.40, f32[1024,128]{1,0:T(8,128)S(1)} %bitcast.42, f32[1024,128]{1,0:T(8,128)S(1)} %bitcast.45, f32[1024,128]{1,0:T(8,128)S(1)} %bitcast.26, ...), custom_call_target="tpu_custom_call" | custom-call | flops 12000000000 | bytes 4079616 | tf_op jit(solution)/shard_map/pack/pallas_call | solution.py:47
  12.3 2.7 %collective-permute-start.3 = (f32[3,2,64,128]{3,2,1,0:T(8,128)S(1)}, f32[3,2,64,128]{3,2,1,0:T(8,128)S(1)}, u32[]{:S(2)}, u32[]{:S(2)}) collective-permute-start(f32[3,2,64,128]{3,2,1,0:T(8,128)S(1)} %get-tuple-element.26), channel_id=1, source_target_pairs={{0,248},{2,250},{4,252},{6,254},{8,16},{10,18},{12,20},{14,22},{16... | collective-permute-start | bytes 589832 | tf_op jit(solution)/shard_map/ppermute | solution.py:387
  15.0 0.2 pack_even.1.refs_5_
  15.2 6.6 %collective-permute-start.2 = (f32[3,2,64,128]{3,2,1,0:T(8,128)S(1)}, f32[3,2,64,128]{3,2,1,0:T(8,128)S(1)}, u32[]{:S(2)}, u32[]{:S(2)}) collective-permute-start(f32[3,2,64,128]{3,2,1,0:T(8,128)S(1)} %pack_even.1.refs_5_), channel_id=1, source_target_pairs={{0,8},{2,10},{4,12},{6,14},{8,0},{10,2},{12,4},{14,6},{16,24},{18,... | collective-permute-start | bytes 589832 | tf_op jit(solution)/shard_map/ppermute | solution.py:387
  21.7 3.0 %collective-permute-done.1.refs_1_ = f32[12,64,128]{2,1,0:T(8,128)S(1)} collective-permute-done((f32[12,64,128]{2,1,0:T(8,128)S(1)}, f32[12,64,128]{2,1,0:T(8,128)S(1)}, u32[]{:S(2)}, u32[]{:S(2)}) %collective-permute-start.1) | collective-permute-done | bytes 393248 | tf_op jit(solution)/shard_map/ppermute | solution.py:22
  24.7 1.5 %winds_inner.1 = (f32[1024,128]{1,0:T(8,128)S(1)}, f32[1024,128]{1,0:T(8,128)S(1)}, f32[1024,128]{1,0:T(8,128)S(1)}) custom-call(f32[1024,128]{1,0:T(8,128)S(1)} %bitcast.39, f32[1024,128]{1,0:T(8,128)S(1)} %bitcast.41, f32[1024,128]{1,0:T(8,128)S(1)} %bitcast.44, f32[1024,128]{1,0:T(8,128)S(1)} %bitcast.24, f32[1024,128]{1,0:T(8,128)S(1)} %bitcast.47, ...), custom_call_target="tpu_custom_call" | custom-call | bytes 4194304 | tf_op jit(solution)/shard_map/winds_inner/pallas_call | solution.py:47
  26.2 1.0 %theta_inner.1.refs_4_ = f32[1024,128]{1,0:T(8,128)S(1)} custom-call(f32[288,128]{1,0:T(8,128)S(1)} %collective-permute-done.refs_7_.refs_5_.refs_0_, f32[12,64,128]{2,1,0:T(8,128)S(1)} %collective-permute-done.1.refs_1_, f32[1024,128]{1,0:T(8,128)S(1)} %get-tuple-element.19.refs_6_.refs_4_.refs_2_, f32[1024,128]{1,0:T(8,128)S(1)} %bitcast.28, ...), custom_call_target="tpu_custom_call" | custom-call | bytes 2637824 | tf_op jit(solution)/shard_map/theta_inner/pallas_call | solution.py:47
  27.2 0.8 %collective-permute-done.5.refs_8_ = f32[8,1024]{1,0:T(8,128)S(1)} collective-permute-done((f32[8,1024]{1,0:T(8,128)S(1)}, f32[8,1024]{1,0:T(8,128)S(1)}, u32[]{:S(2)}, u32[]{:S(2)}) %collective-permute-start.5) | collective-permute-done | bytes 32800 | tf_op jit(solution)/shard_map/ppermute | solution.py:387
  28.0 2.3 %finish.1 = (f32[1024,128]{1,0:T(8,128)}, f32[1024,128]{1,0:T(8,128)}, f32[1024,128]{1,0:T(8,128)}, f32[1024,128]{1,0:T(8,128)}) custom-call(f32[1024,128]{1,0:T(8,128)S(1)} %get-tuple-element.23.refs_0_, f32[1024,128]{1,0:T(8,128)S(1)} %get-tuple-element.24.refs_1_, f32[1024,128]{1,0:T(8,128)S(1)} %get-tuple-element.25.refs_2_, f32[1024,128]{1,0:T(8,128)S(1)} %bitcast.25, ...), custom_call_target="tpu_custom_call" | custom-call | bytes 5177344 | tf_op jit(solution)/shard_map/finish/pallas_call | solution.py:47
  30.3 4.5 %collective-permute-done.6 = f32[1024,128]{1,0:T(8,128)S(1)} collective-permute-done((f32[1024,128]{1,0:T(8,128)S(1)}, f32[1024,128]{1,0:T(8,128)S(1)}, u32[]{:S(2)}, u32[]{:S(2)}) %collective-permute-start.6) | collective-permute-done | bytes 524320 | tf_op jit(solution)/shard_map/ppermute | solution.py:22
  34.8 0.8 %add.3 = f32[1024,128]{1,0:T(8,128)} add(f32[1024,128]{1,0:T(8,128)S(1)} %get-tuple-element.30, f32[1024,128]{1,0:T(8,128)S(1)} %collective-permute-done.6) | non-fusion elementwise | flops 131072 | bytes 1572864 | tf_op jit(solution)/shard_map/add | solution.py:428
  (19 shorter events, 0.0 us)
Async XLA Ops:
  0.6 5.5 %copy-start.3 = (f32[64,1,16,128]{3,2,1,0:T(8,128)S(1)}, f32[64,1,16,128]{3,2,1,0:T(8,128)}, u32[]{:S(2)}) copy-start(f32[64,1,16,128]{3,2,1,0:T(8,128)} %param.12) | copy-start | bytes 1572868
  0.6 5.5 %copy-start.4 = (f32[64,1,16,128]{3,2,1,0:T(8,128)S(1)}, f32[64,1,16,128]{3,2,1,0:T(8,128)}, u32[]{:S(2)}) copy-start(f32[64,1,16,128]{3,2,1,0:T(8,128)} %param.13) | copy-start | bytes 1572868
  0.7 5.5 %copy-start.9 = (f32[256,256]{1,0:T(8,128)S(1)}, f32[256,256]{1,0:T(8,128)}, u32[]{:S(2)}) copy-start(f32[256,256]{1,0:T(8,128)} %refs_2_.5) | copy-start | bytes 786436
  3.0 8.3 %collective-permute-start = (f32[288,128]{1,0:T(8,128)S(1)}, f32[288,128]{1,0:T(8,128)S(1)}, u32[]{:S(2)}, u32[]{:S(2)}) collective-permute-start(f32[288,128]{1,0:T(8,128)S(1)} %solve_rim.1.refs_3_), channel_id=1, source_target_pairs={{0,1},{1,0},{2,3},{3,2},{4,5},{5,4},{6,7},{7,6},{8,9},{9,8},{10,11... | collective-permute-start | bytes 442376 | tf_op jit(solution)/shard_map/ppermute | solution.py:22
  6.8 4.5 %copy-start.1 = (f32[64,1,16,128]{3,2,1,0:T(8,128)S(1)}, f32[64,1,16,128]{3,2,1,0:T(8,128)}, u32[]{:S(2)}) copy-start(f32[64,1,16,128]{3,2,1,0:T(8,128)} %param.17) | copy-start | bytes 1572868
  6.8 4.5 %copy-start.2 = (f32[64,1,16,128]{3,2,1,0:T(8,128)S(1)}, f32[64,1,16,128]{3,2,1,0:T(8,128)}, u32[]{:S(2)}) copy-start(f32[64,1,16,128]{3,2,1,0:T(8,128)} %param.18) | copy-start | bytes 1572868
  6.8 4.5 %copy-start.5 = (f32[64,1,16,128]{3,2,1,0:T(8,128)S(1)}, f32[64,1,16,128]{3,2,1,0:T(8,128)}, u32[]{:S(2)}) copy-start(f32[64,1,16,128]{3,2,1,0:T(8,128)} %param.10) | copy-start | bytes 1572868
  6.8 4.5 %copy-start.6 = (f32[64,1,16,128]{3,2,1,0:T(8,128)S(1)}, f32[64,1,16,128]{3,2,1,0:T(8,128)}, u32[]{:S(2)}) copy-start(f32[64,1,16,128]{3,2,1,0:T(8,128)} %param.11) | copy-start | bytes 1572868
  6.8 4.5 %copy-start.7 = (f32[64,1,16,128]{3,2,1,0:T(8,128)S(1)}, f32[64,1,16,128]{3,2,1,0:T(8,128)}, u32[]{:S(2)}) copy-start(f32[64,1,16,128]{3,2,1,0:T(8,128)} %param.14) | copy-start | bytes 1572868
  6.8 4.5 %copy-start.8 = (f32[64,1,16,128]{3,2,1,0:T(8,128)S(1)}, f32[64,1,16,128]{3,2,1,0:T(8,128)}, u32[]{:S(2)}) copy-start(f32[64,1,16,128]{3,2,1,0:T(8,128)} %param.16) | copy-start | bytes 1572868
  6.8 17.8 %collective-permute-start.1 = (f32[12,64,128]{2,1,0:T(8,128)S(1)}, f32[12,64,128]{2,1,0:T(8,128)S(1)}, u32[]{:S(2)}, u32[]{:S(2)}) collective-permute-start(f32[12,64,128]{2,1,0:T(8,128)S(1)} %get-tuple-element.20.refs_3_), channel_id=1, source_target_pairs={{0,1},{1,0},{2,3},{3,2},{4,5},{5,4},{6,7},{7,6},{8,9},{9,8},{10,11... | collective-permute-start | bytes 1179656 | tf_op jit(solution)/shard_map/ppermute | solution.py:22
  8.2 26.7 %collective-permute-start.6 = (f32[1024,128]{1,0:T(8,128)S(1)}, f32[1024,128]{1,0:T(8,128)S(1)}, u32[]{:S(2)}, u32[]{:S(2)}) collective-permute-start(f32[1024,128]{1,0:T(8,128)S(1)} %get-tuple-element.21.refs_8_), channel_id=1, source_target_pairs={{0,1},{1,0},{2,3},{3,2},{4,5},{5,4},{6,7},{7,6},{8,9},{9,8},{10,11... | collective-permute-start | bytes 1572872 | tf_op jit(solution)/shard_map/ppermute | solution.py:22
  12.3 15.7 %collective-permute-start.3 = (f32[3,2,64,128]{3,2,1,0:T(8,128)S(1)}, f32[3,2,64,128]{3,2,1,0:T(8,128)S(1)}, u32[]{:S(2)}, u32[]{:S(2)}) collective-permute-start(f32[3,2,64,128]{3,2,1,0:T(8,128)S(1)} %get-tuple-element.26), channel_id=1, source_target_pairs={{0,248},{2,250},{4,252},{6,254},{8,16},{10,18},{12,20},{14,22},{16... | collective-permute-start | bytes 589832 | tf_op jit(solution)/shard_map/ppermute | solution.py:387
  15.0 9.7 %copy-start = (f32[64,1,16,128]{3,2,1,0:T(8,128)S(1)}, f32[64,1,16,128]{3,2,1,0:T(8,128)}, u32[]{:S(2)}) copy-start(f32[64,1,16,128]{3,2,1,0:T(8,128)} %param.15) | copy-start | bytes 1572868
  15.2 12.9 %collective-permute-start.2 = (f32[3,2,64,128]{3,2,1,0:T(8,128)S(1)}, f32[3,2,64,128]{3,2,1,0:T(8,128)S(1)}, u32[]{:S(2)}, u32[]{:S(2)}) collective-permute-start(f32[3,2,64,128]{3,2,1,0:T(8,128)S(1)} %pack_even.1.refs_5_), channel_id=1, source_target_pairs={{0,8},{2,10},{4,12},{6,14},{8,0},{10,2},{12,4},{14,6},{16,24},{18,... | collective-permute-start | bytes 589832 | tf_op jit(solution)/shard_map/ppermute | solution.py:387
  21.7 5.5 %collective-permute-start.4 = (f32[8,1024]{1,0:T(8,128)S(1)}, f32[8,1024]{1,0:T(8,128)S(1)}, u32[]{:S(2)}, u32[]{:S(2)}) collective-permute-start(f32[8,1024]{1,0:T(8,128)S(1)} %get-tuple-element.27), channel_id=1, source_target_pairs={{0,2},{2,0},{4,6},{6,4},{8,10},{10,8},{12,14},{14,12},{16,18},{18,... | collective-permute-start | bytes 98312 | tf_op jit(solution)/shard_map/ppermute | solution.py:387
  24.7 3.3 %collective-permute-start.5 = (f32[8,1024]{1,0:T(8,128)S(1)}, f32[8,1024]{1,0:T(8,128)S(1)}, u32[]{:S(2)}, u32[]{:S(2)}) collective-permute-start(f32[8,1024]{1,0:T(8,128)S(1)} %get-tuple-element.22.refs_6_), channel_id=1, source_target_pairs={{0,254},{2,4},{4,2},{6,8},{8,6},{10,12},{12,10},{14,16},{16,14},{1... | collective-permute-start | bytes 98312 | tf_op jit(solution)/shard_map/ppermute | solution.py:387

commit v4 on v3

--- a/solution.py
+++ b/solution.py
@@ -60,13 +60,6 @@
     return ref[pl.ds(i, levels, stride=px), :]
 
 
-def own_rows_transposed(a_ref, at_ref, me, levels):
-    rows = jnp.concatenate(
-        [a_ref[pl.ds(me * levels, levels), :], a_ref[pl.ds((2 + me) * levels, levels), :]], axis=0
-    )
-    at_ref[...] = rows.T
-
-
 def left_factor(blocks):
     high, low = split(jnp.concatenate(blocks, axis=0))
     return jnp.concatenate(
@@ -116,7 +109,7 @@
     return copies, send
 
 
-def solve_rim(px, w_hbm, t_hbm, a_hbm, rim_ref, w_ref, t_ref, a_ref, at_ref, full_ref, sems):
+def solve_first(px, w_hbm, t_hbm, a_hbm, rim_ref, at_ref, w_ref, t_ref, a_ref, full_ref, sems):
     cells, py = w_hbm.shape
     levels = cells // px
     copies, send = sender(sems)
@@ -125,7 +118,10 @@
     send(t_hbm, t_ref)
     me = lax.axis_index("lev")
     copies[0].wait()
-    own_rows_transposed(a_ref, at_ref, me, levels)
+    rows = jnp.concatenate(
+        [a_ref[pl.ds(me * levels, levels), :], a_ref[pl.ds((2 + me) * levels, levels), :]], axis=0
+    )
+    at_ref[...] = rows.T
     left = left_factor([at_ref[pl.ds((3 - me) * levels, levels), :]])
     copies[1].wait()
     copies[2].wait()
@@ -138,11 +134,11 @@
         rim_ref[pl.ds(4 * levels + 4 * k, 4), :] = edges[0:4, k * py : (k + 1) * py]
 
 
-def solved(px, left, w_ref, t_ref):
+def solved(px, left, w_ref, t_ref, skip=0):
     levels = w_ref.shape[0] // px
     py = w_ref.shape[1]
     half = left.shape[0] // 2
-    for i in range(0, px, 2):
+    for i in range(skip, px - skip, 2):
         right = paired([(row(w_ref, i + d, levels, px), row(t_ref, i + d, levels, px)) for d in range(2)])
         r = jnp.dot(left, right, preferred_element_type=f32)
         r = r[:half] + r[half:]
@@ -150,26 +146,29 @@
         yield i + 1, r[:, py:]
 
 
-def solve_inner(px, w_ref, t_ref, a_ref, inner_ref, mt_ref, at_ref):
+def solve_inner(px, w_ref, t_ref, at_ref, inner_ref):
     levels = w_ref.shape[0] // px
     me = lax.axis_index("lev")
-    own_rows_transposed(a_ref, at_ref, me, levels)
-    left = left_factor([at_ref[pl.ds((3 - me) * levels, levels), :], at_ref[pl.ds((2 + me) * levels, levels), :]])
-    for i, part in solved(px, left, w_ref, t_ref):
-        if 2 <= i < px - 2:
-            inner_ref[i - 2] = part[:levels]
-        mt_ref[pl.ds(i, levels, stride=px), :] = part[levels:]
-
-
-def solve_w(px, w_ref, t_ref, a_ref, ow_ref, mw_ref, at_ref):
+    left = left_factor([at_ref[pl.ds((3 - me) * levels, levels), :]])
+    for i, part in solved(px, left, w_ref, t_ref, 2):
+        inner_ref[i - 2] = part
+
+
+def solve_rest(px, w_ref, t_ref, at_ref, ow_ref, mw_ref, mt_ref):
     levels = w_ref.shape[0] // px
     me = lax.axis_index("lev")
-    own_rows_transposed(a_ref, at_ref, me, levels)
-    left = left_factor([at_ref[pl.ds((1 - me) * levels, levels), :], at_ref[pl.ds(me * levels, levels), :]])
+    left = left_factor(
+        [
+            at_ref[pl.ds((1 - me) * levels, levels), :],
+            at_ref[pl.ds(me * levels, levels), :],
+            at_ref[pl.ds((2 + me) * levels, levels), :],
+        ]
+    )
     for i, part in solved(px, left, w_ref, t_ref):
         here = pl.ds(i, levels, stride=px)
         ow_ref[here, :] = part[:levels]
-        mw_ref[here, :] = part[levels:]
+        mw_ref[here, :] = part[levels : 2 * levels]
+        mt_ref[here, :] = part[2 * levels :]
 
 
 def pack_rows(px, first, u_ref, p_ref, q_ref, wf_ref, mt_ref, got_ref, out):
@@ -393,23 +392,21 @@
     u2, v2, w2, t2, p2, g2, q2, wf2, ws2 = (
         x.reshape(cells, py) for x in (u, v, w, t, p, grad, squeeze, wind_first, wind_second)
     )
-    at = pltpu.VMEM((4 * levels, 2 * levels), f32)
     flat = (cells, py)
     rim_rows = 4 * levels + 4 * (cells // py)
     rim_shape = (rim_rows, py)
     inner_shape = (px - 4, levels, py)
-    (rim_t,) = call(
-        kernel_for(px, solve_rim), "solve_rim", [rim_shape],
-        [pltpu.VMEM(flat, f32), pltpu.VMEM(flat, f32), pltpu.VMEM(a.shape, f32), at,
+    rim_t, at = call(
+        kernel_for(px, solve_first), "solve_first", [rim_shape, (4 * levels, 2 * levels)],
+        [pltpu.VMEM(flat, f32), pltpu.VMEM(flat, f32), pltpu.VMEM(a.shape, f32),
          pltpu.VMEM(flat, f32), pltpu.SemaphoreType.DMA((3,))],
         w2, t2, a, in_space=HBM, limit=FIRST_LIMIT, flops=LONG)
-    inner_t, mine_t = call(
-        kernel_for(px, solve_inner), "solve_inner", [inner_shape, flat], [at], w2, t2, a,
-        after=(rim_t,), flops=I_COST)
+    (inner_t,) = call(
+        kernel_for(px, solve_inner), "solve_inner", [inner_shape], [], w2, t2, at, flops=I_COST)
     got_rim = passed_along(rim_t, "lev", 1)
     got_inner = passed_along(inner_t, "lev", 1)
-    other_w, mine_w = call(
-        kernel_for(px, solve_w), "solve_w", [flat] * 2, [at], w2, t2, a, flops=LONG, after=(inner_t,))
+    other_w, mine_w, mine_t = call(
+        kernel_for(px, solve_rest), "solve_rest", [flat] * 3, [], w2, t2, at, flops=LONG, after=(inner_t,))
     o4, e1, o1 = call(
         kernel_for(px, pack), "pack", [(3, 2, levels, py)] + [(8, cells)] * 2, [],
         u2, v2, p2, q2, wf2, ws2, mine_t, got_rim, flops=LONG, after=(other_w,))

time: 35.8 us -> 35.5 us (level)
  waiting for transfers between devices: 8.24 us -> 7.81 us
    ppermute x3, waiting for transfers between devices: 7.42 us -> 6.58 us  [passed_along(): lax.ppermute(array, axis, [(i, (i + by) % devices) for i in range(devices)])]
    ppermute x4, waiting for transfers between devices: 0.82 us -> 1.23 us  [exchange(): return lax.ppermute(array, 'cols', pairs)]
  transfers between devices with their start and end apart: 7 -> 7, of which waited for: 3 -> 3; matrix products, arithmetic and copies ran while one was open for 0% -> 0% of each run, Pallas kernels for 20% -> 21%
where the time goes in v4:
time: 35.5 us; the launch traced here: 35.4 us
  starting transfers between devices  16.3 us (46%)
  Pallas kernels  9.64 us (27%)
  waiting for transfers between devices  7.81 us (22%)
  other arithmetic  0.85 us (2%)
  between operations  0.8 us (2%)
    pallas_call x8, Pallas kernels, call(): pl.pallas_call(body, out_shape=shapes, in_specs=[in_space] * len(args) +...  9.64 us
    ppermute x4, starting transfers between devices, exchange(): return lax.ppermute(array, 'cols', pairs)  9.46 us
    ppermute x3, starting transfers between devices, passed_along(): lax.ppermute(array, axis, [(i, (i + by) % devices) for i in range(devices)])  6.82 us
    ppermute x3, waiting for transfers between devices, passed_along(): lax.ppermute(array, axis, [(i, (i + by) % devices) for i in range(devices)])  6.58 us
    ppermute x4, waiting for transfers between devices, exchange(): return lax.ppermute(array, 'cols', pairs)  1.23 us
    add x1, other arithmetic, on_device(): w_out = mine_w + got_w  0.85 us
  transfers between devices with their start and end apart: 7, of which 3 were waited for; matrix products, arithmetic and copies ran while one was open for 0% of the time, Pallas kernels for 21%

profile of v4, /device:TPU:24, one launch (start us, length us, event | category | flops | bytes accessed | tf_op | source)
XLA Modules:
  0.0 35.4 jit_solution(16780575242351944601)
XLA Ops:
  0.7 2.3 %solve_first.1 = (f32[288,128]{1,0:T(8,128)S(1)}, f32[256,128]{1,0:T(8,128)S(1)}) custom-call(f32[1024,128]{1,0:T(8,128)} %bitcast.26, f32[1024,128]{1,0:T(8,128)} %bitcast.29, f32[256,256]{1,0:T(8,128)} %refs_2_.1), custom_call_target="tpu_custom_call" | custom-call | flops 12000000000 | bytes 1589248 | tf_op jit(solution)/shard_map/solve_first/pallas_call | solution.py:47
  3.0 3.1 %collective-permute-start = (f32[288,128]{1,0:T(8,128)S(1)}, f32[288,128]{1,0:T(8,128)S(1)}, u32[]{:S(2)}, u32[]{:S(2)}) collective-permute-start(f32[288,128]{1,0:T(8,128)S(1)} %get-tuple-element.22), channel_id=1, source_target_pairs={{0,1},{1,0},{2,3},{3,2},{4,5},{5,4},{6,7},{7,6},{8,9},{9,8},{10,11... | collective-permute-start | bytes 442376 | tf_op jit(solution)/shard_map/ppermute | solution.py:22
  6.1 0.4 %solve_inner.1.refs_3_ = f32[12,64,128]{2,1,0:T(8,128)S(1)} custom-call(f32[1024,128]{1,0:T(8,128)S(1)} %bitcast.27, f32[1024,128]{1,0:T(8,128)S(1)} %bitcast.30, f32[256,128]{1,0:T(8,128)S(1)} %get-tuple-element.20.refs_2_), custom_call_target="tpu_custom_call" | custom-call | bytes 1572864 | tf_op jit(solution)/shard_map/solve_inner/pallas_call | solution.py:47
  6.5 0.0 copy-start.3
  6.6 0.0 copy-start.4
  6.6 0.0 copy-start.5
  6.6 0.0 copy-start.6
  6.6 0.0 copy-start.7
  6.6 0.0 copy-start.8
  6.6 0.6 %collective-permute-start.1 = (f32[12,64,128]{2,1,0:T(8,128)S(1)}, f32[12,64,128]{2,1,0:T(8,128)S(1)}, u32[]{:S(2)}, u32[]{:S(2)}) collective-permute-start(f32[12,64,128]{2,1,0:T(8,128)S(1)} %solve_inner.1.refs_3_), channel_id=1, source_target_pairs={{0,1},{1,0},{2,3},{3,2},{4,5},{5,4},{6,7},{7,6},{8,9},{9,8},{10,11... | collective-permute-start | bytes 1179656 | tf_op jit(solution)/shard_map/ppermute | solution.py:22
  7.2 0.9 %solve_rest.1 = (f32[1024,128]{1,0:T(8,128)S(1)}, f32[1024,128]{1,0:T(8,128)S(1)}, f32[1024,128]{1,0:T(8,128)S(1)}) custom-call(f32[1024,128]{1,0:T(8,128)S(1)} %bitcast.28, f32[1024,128]{1,0:T(8,128)S(1)} %bitcast.31, f32[256,128]{1,0:T(8,128)S(1)} %get-tuple-element.20.refs_2_, f32[12,64,128]{2,1,0:T(8,128)S(1)} %solve_inner.1.refs_3_), custom_call_target="tpu_custom_call" | custom-call | flops 12000000000 | bytes 2752512 | tf_op jit(solution)/shard_map/solve_rest/pallas_call | solution.py:47
  8.1 3.1 %collective-permute-start.6 = (f32[1024,128]{1,0:T(8,128)S(1)}, f32[1024,128]{1,0:T(8,128)S(1)}, u32[]{:S(2)}, u32[]{:S(2)}) collective-permute-start(f32[1024,128]{1,0:T(8,128)S(1)} %get-tuple-element.23.refs_8_), channel_id=1, source_target_pairs={{0,1},{1,0},{2,3},{3,2},{4,5},{5,4},{6,7},{7,6},{8,9},{9,8},{10,11... | collective-permute-start | bytes 1572872 | tf_op jit(solution)/shard_map/ppermute | solution.py:22
  11.3 1.0 %pack.1 = (f32[3,2,64,128]{3,2,1,0:T(8,128)S(1)}, f32[8,1024]{1,0:T(8,128)S(1)}, f32[8,1024]{1,0:T(8,128)S(1)}) custom-call(f32[1024,128]{1,0:T(8,128)S(1)} %bitcast.37, f32[1024,128]{1,0:T(8,128)S(1)} %bitcast.40, f32[1024,128]{1,0:T(8,128)S(1)} %bitcast.42, f32[1024,128]{1,0:T(8,128)S(1)} %bitcast.45, f32[1024,128]{1,0:T(8,128)S(1)} %bitcast.32, ...), custom_call_target="tpu_custom_call" | custom-call | flops 12000000000 | bytes 4079616 | tf_op jit(solution)/shard_map/pack/pallas_call | solution.py:47
  12.3 2.7 %collective-permute-start.3 = (f32[3,2,64,128]{3,2,1,0:T(8,128)S(1)}, f32[3,2,64,128]{3,2,1,0:T(8,128)S(1)}, u32[]{:S(2)}, u32[]{:S(2)}) collective-permute-start(f32[3,2,64,128]{3,2,1,0:T(8,128)S(1)} %get-tuple-element.28), channel_id=1, source_target_pairs={{0,248},{2,250},{4,252},{6,254},{8,16},{10,18},{12,20},{14,22},{16... | collective-permute-start | bytes 589832 | tf_op jit(solution)/shard_map/ppermute | solution.py:386
  15.0 0.2 pack_even.1.refs_5_
  15.1 6.8 %collective-permute-start.2 = (f32[3,2,64,128]{3,2,1,0:T(8,128)S(1)}, f32[3,2,64,128]{3,2,1,0:T(8,128)S(1)}, u32[]{:S(2)}, u32[]{:S(2)}) collective-permute-start(f32[3,2,64,128]{3,2,1,0:T(8,128)S(1)} %pack_even.1.refs_5_), channel_id=1, source_target_pairs={{0,8},{2,10},{4,12},{6,14},{8,0},{10,2},{12,4},{14,6},{16,24},{18,... | collective-permute-start | bytes 589832 | tf_op jit(solution)/shard_map/ppermute | solution.py:386
  21.9 0.0 collective-permute-start.4
  21.9 1.0 %collective-permute-done.1.refs_1_ = f32[12,64,128]{2,1,0:T(8,128)S(1)} collective-permute-done((f32[12,64,128]{2,1,0:T(8,128)S(1)}, f32[12,64,128]{2,1,0:T(8,128)S(1)}, u32[]{:S(2)}, u32[]{:S(2)}) %collective-permute-start.1) | collective-permute-done | bytes 393248 | tf_op jit(solution)/shard_map/ppermute | solution.py:22
  23.0 1.5 %winds_inner.1 = (f32[1024,128]{1,0:T(8,128)S(1)}, f32[1024,128]{1,0:T(8,128)S(1)}, f32[1024,128]{1,0:T(8,128)S(1)}) custom-call(f32[1024,128]{1,0:T(8,128)S(1)} %bitcast.39, f32[1024,128]{1,0:T(8,128)S(1)} %bitcast.41, f32[1024,128]{1,0:T(8,128)S(1)} %bitcast.44, f32[1024,128]{1,0:T(8,128)S(1)} %bitcast.24, f32[1024,128]{1,0:T(8,128)S(1)} %bitcast.47, ...), custom_call_target="tpu_custom_call" | custom-call | bytes 4194304 | tf_op jit(solution)/shard_map/winds_inner/pallas_call | solution.py:47
  24.5 1.0 %theta_inner.1.refs_4_ = f32[1024,128]{1,0:T(8,128)S(1)} custom-call(f32[288,128]{1,0:T(8,128)S(1)} %collective-permute-done.refs_7_.refs_5_.refs_0_, f32[12,64,128]{2,1,0:T(8,128)S(1)} %collective-permute-done.1.refs_1_, f32[1024,128]{1,0:T(8,128)S(1)} %get-tuple-element.21.refs_6_.refs_4_.refs_2_, f32[1024,128]{1,0:T(8,128)S(1)} %bitcast.34, ...), custom_call_target="tpu_custom_call" | custom-call | bytes 2637824 | tf_op jit(solution)/shard_map/theta_inner/pallas_call | solution.py:47
  25.5 1.2 %collective-permute-done.5.refs_8_ = f32[8,1024]{1,0:T(8,128)S(1)} collective-permute-done((f32[8,1024]{1,0:T(8,128)S(1)}, f32[8,1024]{1,0:T(8,128)S(1)}, u32[]{:S(2)}, u32[]{:S(2)}) %collective-permute-start.5) | collective-permute-done | bytes 32800 | tf_op jit(solution)/shard_map/ppermute | solution.py:386
  26.7 2.3 %finish.1 = (f32[1024,128]{1,0:T(8,128)}, f32[1024,128]{1,0:T(8,128)}, f32[1024,128]{1,0:T(8,128)}, f32[1024,128]{1,0:T(8,128)}) custom-call(f32[1024,128]{1,0:T(8,128)S(1)} %get-tuple-element.25.refs_0_, f32[1024,128]{1,0:T(8,128)S(1)} %get-tuple-element.26.refs_1_, f32[1024,128]{1,0:T(8,128)S(1)} %get-tuple-element.27.refs_2_, f32[1024,128]{1,0:T(8,128)S(1)} %bitcast.25, ...), custom_call_target="tpu_custom_call" | custom-call | bytes 5177344 | tf_op jit(solution)/shard_map/finish/pallas_call | solution.py:47
  29.0 5.5 %collective-permute-done.6 = f32[1024,128]{1,0:T(8,128)S(1)} collective-permute-done((f32[1024,128]{1,0:T(8,128)S(1)}, f32[1024,128]{1,0:T(8,128)S(1)}, u32[]{:S(2)}, u32[]{:S(2)}) %collective-permute-start.6) | collective-permute-done | bytes 524320 | tf_op jit(solution)/shard_map/ppermute | solution.py:22
  34.6 0.8 %add.3 = f32[1024,128]{1,0:T(8,128)} add(f32[1024,128]{1,0:T(8,128)S(1)} %get-tuple-element.32, f32[1024,128]{1,0:T(8,128)S(1)} %collective-permute-done.6) | non-fusion elementwise | flops 131072 | bytes 1572864 | tf_op jit(solution)/shard_map/add | solution.py:425
  (17 shorter events, 0.0 us)
Async XLA Ops:
  0.6 5.5 %copy-start.1 = (f32[64,1,16,128]{3,2,1,0:T(8,128)S(1)}, f32[64,1,16,128]{3,2,1,0:T(8,128)}, u32[]{:S(2)}) copy-start(f32[64,1,16,128]{3,2,1,0:T(8,128)} %param.12) | copy-start | bytes 1572868
  0.6 5.4 %copy-start.2 = (f32[64,1,16,128]{3,2,1,0:T(8,128)S(1)}, f32[64,1,16,128]{3,2,1,0:T(8,128)}, u32[]{:S(2)}) copy-start(f32[64,1,16,128]{3,2,1,0:T(8,128)} %param.13) | copy-start | bytes 1572868
  3.0 8.3 %collective-permute-start = (f32[288,128]{1,0:T(8,128)S(1)}, f32[288,128]{1,0:T(8,128)S(1)}, u32[]{:S(2)}, u32[]{:S(2)}) collective-permute-start(f32[288,128]{1,0:T(8,128)S(1)} %get-tuple-element.22), channel_id=1, source_target_pairs={{0,1},{1,0},{2,3},{3,2},{4,5},{5,4},{6,7},{7,6},{8,9},{9,8},{10,11... | collective-permute-start | bytes 442376 | tf_op jit(solution)/shard_map/ppermute | solution.py:22
  6.5 4.7 %copy-start.3 = (f32[64,1,16,128]{3,2,1,0:T(8,128)S(1)}, f32[64,1,16,128]{3,2,1,0:T(8,128)}, u32[]{:S(2)}) copy-start(f32[64,1,16,128]{3,2,1,0:T(8,128)} %param.17) | copy-start | bytes 1572868
  6.6 4.7 %copy-start.4 = (f32[64,1,16,128]{3,2,1,0:T(8,128)S(1)}, f32[64,1,16,128]{3,2,1,0:T(8,128)}, u32[]{:S(2)}) copy-start(f32[64,1,16,128]{3,2,1,0:T(8,128)} %param.18) | copy-start | bytes 1572868
  6.6 4.7 %copy-start.5 = (f32[64,1,16,128]{3,2,1,0:T(8,128)S(1)}, f32[64,1,16,128]{3,2,1,0:T(8,128)}, u32[]{:S(2)}) copy-start(f32[64,1,16,128]{3,2,1,0:T(8,128)} %param.10) | copy-start | bytes 1572868
  6.6 4.7 %copy-start.6 = (f32[64,1,16,128]{3,2,1,0:T(8,128)S(1)}, f32[64,1,16,128]{3,2,1,0:T(8,128)}, u32[]{:S(2)}) copy-start(f32[64,1,16,128]{3,2,1,0:T(8,128)} %param.11) | copy-start | bytes 1572868
  6.6 4.7 %copy-start.7 = (f32[64,1,16,128]{3,2,1,0:T(8,128)S(1)}, f32[64,1,16,128]{3,2,1,0:T(8,128)}, u32[]{:S(2)}) copy-start(f32[64,1,16,128]{3,2,1,0:T(8,128)} %param.14) | copy-start | bytes 1572868
  6.6 4.7 %copy-start.8 = (f32[64,1,16,128]{3,2,1,0:T(8,128)S(1)}, f32[64,1,16,128]{3,2,1,0:T(8,128)}, u32[]{:S(2)}) copy-start(f32[64,1,16,128]{3,2,1,0:T(8,128)} %param.16) | copy-start | bytes 1572868
  6.6 16.4 %collective-permute-start.1 = (f32[12,64,128]{2,1,0:T(8,128)S(1)}, f32[12,64,128]{2,1,0:T(8,128)S(1)}, u32[]{:S(2)}, u32[]{:S(2)}) collective-permute-start(f32[12,64,128]{2,1,0:T(8,128)S(1)} %solve_inner.1.refs_3_), channel_id=1, source_target_pairs={{0,1},{1,0},{2,3},{3,2},{4,5},{5,4},{6,7},{7,6},{8,9},{9,8},{10,11... | collective-permute-start | bytes 1179656 | tf_op jit(solution)/shard_map/ppermute | solution.py:22
  8.1 26.4 %collective-permute-start.6 = (f32[1024,128]{1,0:T(8,128)S(1)}, f32[1024,128]{1,0:T(8,128)S(1)}, u32[]{:S(2)}, u32[]{:S(2)}) collective-permute-start(f32[1024,128]{1,0:T(8,128)S(1)} %get-tuple-element.23.refs_8_), channel_id=1, source_target_pairs={{0,1},{1,0},{2,3},{3,2},{4,5},{5,4},{6,7},{7,6},{8,9},{9,8},{10,11... | collective-permute-start | bytes 1572872 | tf_op jit(solution)/shard_map/ppermute | solution.py:22
  12.3 14.4 %collective-permute-start.3 = (f32[3,2,64,128]{3,2,1,0:T(8,128)S(1)}, f32[3,2,64,128]{3,2,1,0:T(8,128)S(1)}, u32[]{:S(2)}, u32[]{:S(2)}) collective-permute-start(f32[3,2,64,128]{3,2,1,0:T(8,128)S(1)} %get-tuple-element.28), channel_id=1, source_target_pairs={{0,248},{2,250},{4,252},{6,254},{8,16},{10,18},{12,20},{14,22},{16... | collective-permute-start | bytes 589832 | tf_op jit(solution)/shard_map/ppermute | solution.py:386
  15.0 8.0 %copy-start = (f32[64,1,16,128]{3,2,1,0:T(8,128)S(1)}, f32[64,1,16,128]{3,2,1,0:T(8,128)}, u32[]{:S(2)}) copy-start(f32[64,1,16,128]{3,2,1,0:T(8,128)} %param.15) | copy-start | bytes 1572868
  15.1 11.6 %collective-permute-start.2 = (f32[3,2,64,128]{3,2,1,0:T(8,128)S(1)}, f32[3,2,64,128]{3,2,1,0:T(8,128)S(1)}, u32[]{:S(2)}, u32[]{:S(2)}) collective-permute-start(f32[3,2,64,128]{3,2,1,0:T(8,128)S(1)} %pack_even.1.refs_5_), channel_id=1, source_target_pairs={{0,8},{2,10},{4,12},{6,14},{8,0},{10,2},{12,4},{14,6},{16,24},{18,... | collective-permute-start | bytes 589832 | tf_op jit(solution)/shard_map/ppermute | solution.py:386
  21.9 3.6 %collective-permute-start.4 = (f32[8,1024]{1,0:T(8,128)S(1)}, f32[8,1024]{1,0:T(8,128)S(1)}, u32[]{:S(2)}, u32[]{:S(2)}) collective-permute-start(f32[8,1024]{1,0:T(8,128)S(1)} %get-tuple-element.29), channel_id=1, source_target_pairs={{0,2},{2,0},{4,6},{6,4},{8,10},{10,8},{12,14},{14,12},{16,18},{18,... | collective-permute-start | bytes 98312 | tf_op jit(solution)/shard_map/ppermute | solution.py:386
  23.0 3.8 %collective-permute-start.5 = (f32[8,1024]{1,0:T(8,128)S(1)}, f32[8,1024]{1,0:T(8,128)S(1)}, u32[]{:S(2)}, u32[]{:S(2)}) collective-permute-start(f32[8,1024]{1,0:T(8,128)S(1)} %get-tuple-element.24.refs_6_), channel_id=1, source_target_pairs={{0,254},{2,4},{4,2},{6,8},{8,6},{10,12},{12,10},{14,16},{16,14},{1... | collective-permute-start | bytes 98312 | tf_op jit(solution)/shard_map/ppermute | solution.py:386

commit v5 on v4

--- a/solution.py
+++ b/solution.py
@@ -110,12 +110,14 @@
 
 
 def solve_first(px, w_hbm, t_hbm, a_hbm, rim_ref, at_ref, w_ref, t_ref, a_ref, full_ref, sems):
-    cells, py = w_hbm.shape
-    levels = cells // px
+    levels, _, py = w_hbm.shape
+    half = px // 2
     copies, send = sender(sems)
     send(a_hbm, a_ref)
-    send(w_hbm, w_ref)
-    send(t_hbm, t_ref)
+    for h in range(2):
+        here = pl.ds(h * half, half)
+        send(w_hbm.at[:, here, :], w_ref.at[h])
+        send(t_hbm.at[:, here, :], t_ref.at[h])
     me = lax.axis_index("lev")
     copies[0].wait()
     rows = jnp.concatenate(
@@ -123,12 +125,16 @@
     )
     at_ref[...] = rows.T
     left = left_factor([at_ref[pl.ds((3 - me) * levels, levels), :]])
-    copies[1].wait()
-    copies[2].wait()
-    for i, part in solved(px, left, w_ref, t_ref):
-        full_ref[pl.ds(i, levels, stride=px), :] = part
-        if not 2 <= i < px - 2:
-            rim_ref[pl.ds(rim_slot(i, px) * levels, levels), :] = part
+    for h in range(2):
+        copies[1 + 2 * h].wait()
+        copies[2 + 2 * h].wait()
+        w_half = w_ref.at[h].reshape(levels * half, py)
+        t_half = t_ref.at[h].reshape(levels * half, py)
+        for k, part in solved(half, left, w_half, t_half):
+            i = h * half + k
+            full_ref[pl.ds(i, levels, stride=px), :] = part
+            if not 2 <= i < px - 2:
+                rim_ref[pl.ds(rim_slot(i, px) * levels, levels), :] = part
     edges = rims(full_ref[...], rim_selector(py))
     for k in range(levels * px // py):
         rim_ref[pl.ds(4 * levels + 4 * k, 4), :] = edges[0:4, k * py : (k + 1) * py]
@@ -201,8 +207,8 @@
     v_rims = rims(v_ref[...], selector)[0:4]
     p_rims = rims(p_ref[...] * q_ref[...], selector)[0:4]
     t_rims = rims(ws_ref[...], selector)[0:4] * (rims(mt_ref[...], selector)[0:4] + got_rims)
-    first = jnp.concatenate([v_rims[0:2], p_rims[0:2], t_rims[0:2], t_rims[0:2]], axis=0)
-    last = jnp.concatenate([v_rims[2:4], p_rims[2:4], t_rims[2:4], t_rims[2:4]], axis=0)
+    first = jnp.concatenate([v_rims[0:2], p_rims[0:2], t_rims[0:2]], axis=1)
+    last = jnp.concatenate([v_rims[2:4], p_rims[2:4], t_rims[2:4]], axis=1)
     is_odd = odd1 == 1
     e1_ref[...] = jnp.where(is_odd, first, last)
     o1_ref[...] = jnp.where(is_odd, last, first)
@@ -329,8 +335,9 @@
 
 
 def halo_columns(e1_ref, o1_ref, at, odd):
-    e1 = e1_ref[2 * at : 2 * at + 2]
-    o1 = o1_ref[2 * at : 2 * at + 2]
+    cells = e1_ref.shape[1] // 3
+    e1 = e1_ref[:, at * cells : (at + 1) * cells]
+    o1 = o1_ref[:, at * cells : (at + 1) * cells]
     return jnp.concatenate([jnp.where(odd, e1, o1), jnp.where(odd, o1, e1)], axis=0)
 
 
@@ -398,9 +405,9 @@
     inner_shape = (px - 4, levels, py)
     rim_t, at = call(
         kernel_for(px, solve_first), "solve_first", [rim_shape, (4 * levels, 2 * levels)],
-        [pltpu.VMEM(flat, f32), pltpu.VMEM(flat, f32), pltpu.VMEM(a.shape, f32),
-         pltpu.VMEM(flat, f32), pltpu.SemaphoreType.DMA((3,))],
-        w2, t2, a, in_space=HBM, limit=FIRST_LIMIT, flops=LONG)
+        [pltpu.VMEM((2, levels, px // 2, py), f32)] * 2
+        + [pltpu.VMEM(a.shape, f32), pltpu.VMEM(flat, f32), pltpu.SemaphoreType.DMA((5,))],
+        w.reshape(levels, px, py), t.reshape(levels, px, py), a, in_space=HBM, limit=FIRST_LIMIT, flops=LONG)
     (inner_t,) = call(
         kernel_for(px, solve_inner), "solve_inner", [inner_shape], [], w2, t2, at, flops=I_COST)
     got_rim = passed_along(rim_t, "lev", 1)
@@ -408,7 +415,7 @@
     other_w, mine_w, mine_t = call(
         kernel_for(px, solve_rest), "solve_rest", [flat] * 3, [], w2, t2, at, flops=LONG, after=(inner_t,))
     o4, e1, o1 = call(
-        kernel_for(px, pack), "pack", [(3, 2, levels, py)] + [(8, cells)] * 2, [],
+        kernel_for(px, pack), "pack", [(3, 2, levels, py)] + [(2, 3 * cells)] * 2, [],
         u2, v2, p2, q2, wf2, ws2, mine_t, got_rim, flops=LONG, after=(other_w,))
     (e4,) = call(
         kernel_for(px, pack_even), "pack_even", [(3, 2, levels, py)], [],

time: 35.5 us -> 35.3 us (level)
  no operation moved by 1% of the time
where the time goes in v5:
time: 35.3 us; the launch traced here: 35.2 us
  starting transfers between devices  16.3 us (46%)
  Pallas kernels  9.5 us (27%)
  waiting for transfers between devices  7.72 us (22%)
  other arithmetic  0.85 us (2%)
  between operations  0.8 us (2%)
    pallas_call x8, Pallas kernels, call(): pl.pallas_call(body, out_shape=shapes, in_specs=[in_space] * len(args) +...  9.5 us
    ppermute x4, starting transfers between devices, exchange(): return lax.ppermute(array, 'cols', pairs)  9.46 us
    ppermute x3, starting transfers between devices, passed_along(): lax.ppermute(array, axis, [(i, (i + by) % devices) for i in range(devices)])  6.83 us
    ppermute x3, waiting for transfers between devices, passed_along(): lax.ppermute(array, axis, [(i, (i + by) % devices) for i in range(devices)])  6.66 us
    ppermute x4, waiting for transfers between devices, exchange(): return lax.ppermute(array, 'cols', pairs)  1.06 us
    add x1, other arithmetic, on_device(): w_out = mine_w + got_w  0.85 us
  transfers between devices with their start and end apart: 7, of which 3 were waited for; matrix products, arithmetic and copies ran while one was open for 0% of the time, Pallas kernels for 21%

profile of v5, /device:TPU:24, one launch (start us, length us, event | category | flops | bytes accessed | tf_op | source)
XLA Modules:
  0.0 35.2 jit_solution(16004930837670713300)
XLA Ops:
  0.7 2.2 %solve_first.1 = (f32[288,128]{1,0:T(8,128)S(1)}, f32[256,128]{1,0:T(8,128)S(1)}) custom-call(f32[64,16,128]{2,1,0:T(8,128)} %bitcast.28, f32[64,16,128]{2,1,0:T(8,128)} %bitcast.31, f32[256,256]{1,0:T(8,128)} %refs_2_.1), custom_call_target="tpu_custom_call" | custom-call | flops 12000000000 | bytes 1589248 | tf_op jit(solution)/shard_map/solve_first/pallas_call | solution.py:47
  2.8 3.1 %collective-permute-start = (f32[288,128]{1,0:T(8,128)S(1)}, f32[288,128]{1,0:T(8,128)S(1)}, u32[]{:S(2)}, u32[]{:S(2)}) collective-permute-start(f32[288,128]{1,0:T(8,128)S(1)} %get-tuple-element.22), channel_id=1, source_target_pairs={{0,1},{1,0},{2,3},{3,2},{4,5},{5,4},{6,7},{7,6},{8,9},{9,8},{10,11... | collective-permute-start | bytes 442376 | tf_op jit(solution)/shard_map/ppermute | solution.py:22
  6.0 0.4 %solve_inner.1.refs_3_ = f32[12,64,128]{2,1,0:T(8,128)S(1)} custom-call(f32[1024,128]{1,0:T(8,128)S(1)} %bitcast.29, f32[1024,128]{1,0:T(8,128)S(1)} %bitcast.32, f32[256,128]{1,0:T(8,128)S(1)} %get-tuple-element.20.refs_2_), custom_call_target="tpu_custom_call" | custom-call | bytes 1572864 | tf_op jit(solution)/shard_map/solve_inner/pallas_call | solution.py:47
  6.4 0.0 copy-start.3
  6.4 0.0 copy-start.4
  6.4 0.0 copy-start.5
  6.4 0.0 copy-start.6
  6.5 0.0 copy-start.7
  6.5 0.0 copy-start.8
  6.5 0.6 %collective-permute-start.1 = (f32[12,64,128]{2,1,0:T(8,128)S(1)}, f32[12,64,128]{2,1,0:T(8,128)S(1)}, u32[]{:S(2)}, u32[]{:S(2)}) collective-permute-start(f32[12,64,128]{2,1,0:T(8,128)S(1)} %solve_inner.1.refs_3_), channel_id=1, source_target_pairs={{0,1},{1,0},{2,3},{3,2},{4,5},{5,4},{6,7},{7,6},{8,9},{9,8},{10,11... | collective-permute-start | bytes 1179656 | tf_op jit(solution)/shard_map/ppermute | solution.py:22
  7.1 0.9 %solve_rest.1 = (f32[1024,128]{1,0:T(8,128)S(1)}, f32[1024,128]{1,0:T(8,128)S(1)}, f32[1024,128]{1,0:T(8,128)S(1)}) custom-call(f32[1024,128]{1,0:T(8,128)S(1)} %bitcast.30, f32[1024,128]{1,0:T(8,128)S(1)} %bitcast.33, f32[256,128]{1,0:T(8,128)S(1)} %get-tuple-element.20.refs_2_, f32[12,64,128]{2,1,0:T(8,128)S(1)} %solve_inner.1.refs_3_), custom_call_target="tpu_custom_call" | custom-call | flops 12000000000 | bytes 2752512 | tf_op jit(solution)/shard_map/solve_rest/pallas_call | solution.py:47
  8.0 3.1 %collective-permute-start.6 = (f32[1024,128]{1,0:T(8,128)S(1)}, f32[1024,128]{1,0:T(8,128)S(1)}, u32[]{:S(2)}, u32[]{:S(2)}) collective-permute-start(f32[1024,128]{1,0:T(8,128)S(1)} %get-tuple-element.23.refs_8_), channel_id=1, source_target_pairs={{0,1},{1,0},{2,3},{3,2},{4,5},{5,4},{6,7},{7,6},{8,9},{9,8},{10,11... | collective-permute-start | bytes 1572872 | tf_op jit(solution)/shard_map/ppermute | solution.py:22
  11.1 0.0 collective-permute-done.refs_7_.refs_5_.refs_0_
  11.2 1.0 %pack.1 = (f32[3,2,64,128]{3,2,1,0:T(8,128)S(1)}, f32[2,3072]{1,0:T(2,128)S(1)}, f32[2,3072]{1,0:T(2,128)S(1)}) custom-call(f32[1024,128]{1,0:T(8,128)S(1)} %bitcast.39, f32[1024,128]{1,0:T(8,128)S(1)} %bitcast.42, f32[1024,128]{1,0:T(8,128)S(1)} %bitcast.44, f32[1024,128]{1,0:T(8,128)S(1)} %bitcast.47, f32[1024,128]{1,0:T(8,128)S(1)} %bitcast.34, ...), custom_call_target="tpu_custom_call" | custom-call | flops 12000000000 | bytes 4063232 | tf_op jit(solution)/shard_map/pack/pallas_call | solution.py:47
  12.2 2.7 %collective-permute-start.3 = (f32[3,2,64,128]{3,2,1,0:T(8,128)S(1)}, f32[3,2,64,128]{3,2,1,0:T(8,128)S(1)}, u32[]{:S(2)}, u32[]{:S(2)}) collective-permute-start(f32[3,2,64,128]{3,2,1,0:T(8,128)S(1)} %get-tuple-element.28), channel_id=1, source_target_pairs={{0,248},{2,250},{4,252},{6,254},{8,16},{10,18},{12,20},{14,22},{16... | collective-permute-start | bytes 589832 | tf_op jit(solution)/shard_map/ppermute | solution.py:393
  14.8 0.2 pack_even.1.refs_5_
  15.0 6.8 %collective-permute-start.2 = (f32[3,2,64,128]{3,2,1,0:T(8,128)S(1)}, f32[3,2,64,128]{3,2,1,0:T(8,128)S(1)}, u32[]{:S(2)}, u32[]{:S(2)}) collective-permute-start(f32[3,2,64,128]{3,2,1,0:T(8,128)S(1)} %pack_even.1.refs_5_), channel_id=1, source_target_pairs={{0,8},{2,10},{4,12},{6,14},{8,0},{10,2},{12,4},{14,6},{16,24},{18,... | collective-permute-start | bytes 589832 | tf_op jit(solution)/shard_map/ppermute | solution.py:393
  21.8 1.1 %collective-permute-done.1.refs_1_ = f32[12,64,128]{2,1,0:T(8,128)S(1)} collective-permute-done((f32[12,64,128]{2,1,0:T(8,128)S(1)}, f32[12,64,128]{2,1,0:T(8,128)S(1)}, u32[]{:S(2)}, u32[]{:S(2)}) %collective-permute-start.1) | collective-permute-done | bytes 393248 | tf_op jit(solution)/shard_map/ppermute | solution.py:22
  22.8 1.5 %winds_inner.1 = (f32[1024,128]{1,0:T(8,128)S(1)}, f32[1024,128]{1,0:T(8,128)S(1)}, f32[1024,128]{1,0:T(8,128)S(1)}) custom-call(f32[1024,128]{1,0:T(8,128)S(1)} %bitcast.41, f32[1024,128]{1,0:T(8,128)S(1)} %bitcast.43, f32[1024,128]{1,0:T(8,128)S(1)} %bitcast.46, f32[1024,128]{1,0:T(8,128)S(1)} %bitcast.26, f32[1024,128]{1,0:T(8,128)S(1)} %bitcast.49, ...), custom_call_target="tpu_custom_call" | custom-call | bytes 4194304 | tf_op jit(solution)/shard_map/winds_inner/pallas_call | solution.py:47
  24.3 1.0 %theta_inner.1.refs_4_ = f32[1024,128]{1,0:T(8,128)S(1)} custom-call(f32[288,128]{1,0:T(8,128)S(1)} %collective-permute-done.refs_7_.refs_5_.refs_0_, f32[12,64,128]{2,1,0:T(8,128)S(1)} %collective-permute-done.1.refs_1_, f32[1024,128]{1,0:T(8,128)S(1)} %get-tuple-element.21.refs_6_.refs_4_.refs_2_, f32[1024,128]{1,0:T(8,128)S(1)} %bitcast.36, ...), custom_call_target="tpu_custom_call" | custom-call | bytes 2637824 | tf_op jit(solution)/shard_map/theta_inner/pallas_call | solution.py:47
  25.4 1.0 %collective-permute-done.5.refs_8_ = f32[2,3072]{1,0:T(2,128)S(1)} collective-permute-done((f32[2,3072]{1,0:T(2,128)S(1)}, f32[2,3072]{1,0:T(2,128)S(1)}, u32[]{:S(2)}, u32[]{:S(2)}) %collective-permute-start.5) | collective-permute-done | bytes 24608 | tf_op jit(solution)/shard_map/ppermute | solution.py:393
  26.4 2.3 %finish.1 = (f32[1024,128]{1,0:T(8,128)}, f32[1024,128]{1,0:T(8,128)}, f32[1024,128]{1,0:T(8,128)}, f32[1024,128]{1,0:T(8,128)}) custom-call(f32[1024,128]{1,0:T(8,128)S(1)} %get-tuple-element.25.refs_0_, f32[1024,128]{1,0:T(8,128)S(1)} %get-tuple-element.26.refs_1_, f32[1024,128]{1,0:T(8,128)S(1)} %get-tuple-element.27.refs_2_, f32[1024,128]{1,0:T(8,128)S(1)} %bitcast.27, ...), custom_call_target="tpu_custom_call" | custom-call | bytes 5160960 | tf_op jit(solution)/shard_map/finish/pallas_call | solution.py:47
  28.7 5.6 %collective-permute-done.6 = f32[1024,128]{1,0:T(8,128)S(1)} collective-permute-done((f32[1024,128]{1,0:T(8,128)S(1)}, f32[1024,128]{1,0:T(8,128)S(1)}, u32[]{:S(2)}, u32[]{:S(2)}) %collective-permute-start.6) | collective-permute-done | bytes 524320 | tf_op jit(solution)/shard_map/ppermute | solution.py:22
  34.4 0.8 %add.3 = f32[1024,128]{1,0:T(8,128)} add(f32[1024,128]{1,0:T(8,128)S(1)} %get-tuple-element.32, f32[1024,128]{1,0:T(8,128)S(1)} %collective-permute-done.6) | non-fusion elementwise | flops 131072 | bytes 1572864 | tf_op jit(solution)/shard_map/add | solution.py:432
  (17 shorter events, 0.0 us)
Async XLA Ops:
  0.6 5.3 %copy-start.1 = (f32[64,1,16,128]{3,2,1,0:T(8,128)S(1)}, f32[64,1,16,128]{3,2,1,0:T(8,128)}, u32[]{:S(2)}) copy-start(f32[64,1,16,128]{3,2,1,0:T(8,128)} %param.12) | copy-start | bytes 1572868
  0.6 5.3 %copy-start.2 = (f32[64,1,16,128]{3,2,1,0:T(8,128)S(1)}, f32[64,1,16,128]{3,2,1,0:T(8,128)}, u32[]{:S(2)}) copy-start(f32[64,1,16,128]{3,2,1,0:T(8,128)} %param.13) | copy-start | bytes 1572868
  2.8 8.3 %collective-permute-start = (f32[288,128]{1,0:T(8,128)S(1)}, f32[288,128]{1,0:T(8,128)S(1)}, u32[]{:S(2)}, u32[]{:S(2)}) collective-permute-start(f32[288,128]{1,0:T(8,128)S(1)} %get-tuple-element.22), channel_id=1, source_target_pairs={{0,1},{1,0},{2,3},{3,2},{4,5},{5,4},{6,7},{7,6},{8,9},{9,8},{10,11... | collective-permute-start | bytes 442376 | tf_op jit(solution)/shard_map/ppermute | solution.py:22
  6.4 4.7 %copy-start.3 = (f32[64,1,16,128]{3,2,1,0:T(8,128)S(1)}, f32[64,1,16,128]{3,2,1,0:T(8,128)}, u32[]{:S(2)}) copy-start(f32[64,1,16,128]{3,2,1,0:T(8,128)} %param.17) | copy-start | bytes 1572868
  6.4 4.7 %copy-start.4 = (f32[64,1,16,128]{3,2,1,0:T(8,128)S(1)}, f32[64,1,16,128]{3,2,1,0:T(8,128)}, u32[]{:S(2)}) copy-start(f32[64,1,16,128]{3,2,1,0:T(8,128)} %param.18) | copy-start | bytes 1572868
  6.4 4.7 %copy-start.5 = (f32[64,1,16,128]{3,2,1,0:T(8,128)S(1)}, f32[64,1,16,128]{3,2,1,0:T(8,128)}, u32[]{:S(2)}) copy-start(f32[64,1,16,128]{3,2,1,0:T(8,128)} %param.10) | copy-start | bytes 1572868
  6.4 4.7 %copy-start.6 = (f32[64,1,16,128]{3,2,1,0:T(8,128)S(1)}, f32[64,1,16,128]{3,2,1,0:T(8,128)}, u32[]{:S(2)}) copy-start(f32[64,1,16,128]{3,2,1,0:T(8,128)} %param.11) | copy-start | bytes 1572868
  6.5 4.7 %copy-start.7 = (f32[64,1,16,128]{3,2,1,0:T(8,128)S(1)}, f32[64,1,16,128]{3,2,1,0:T(8,128)}, u32[]{:S(2)}) copy-start(f32[64,1,16,128]{3,2,1,0:T(8,128)} %param.14) | copy-start | bytes 1572868
  6.5 4.7 %copy-start.8 = (f32[64,1,16,128]{3,2,1,0:T(8,128)S(1)}, f32[64,1,16,128]{3,2,1,0:T(8,128)}, u32[]{:S(2)}) copy-start(f32[64,1,16,128]{3,2,1,0:T(8,128)} %param.16) | copy-start | bytes 1572868
  6.5 16.4 %collective-permute-start.1 = (f32[12,64,128]{2,1,0:T(8,128)S(1)}, f32[12,64,128]{2,1,0:T(8,128)S(1)}, u32[]{:S(2)}, u32[]{:S(2)}) collective-permute-start(f32[12,64,128]{2,1,0:T(8,128)S(1)} %solve_inner.1.refs_3_), channel_id=1, source_target_pairs={{0,1},{1,0},{2,3},{3,2},{4,5},{5,4},{6,7},{7,6},{8,9},{9,8},{10,11... | collective-permute-start | bytes 1179656 | tf_op jit(solution)/shard_map/ppermute | solution.py:22
  8.0 26.4 %collective-permute-start.6 = (f32[1024,128]{1,0:T(8,128)S(1)}, f32[1024,128]{1,0:T(8,128)S(1)}, u32[]{:S(2)}, u32[]{:S(2)}) collective-permute-start(f32[1024,128]{1,0:T(8,128)S(1)} %get-tuple-element.23.refs_8_), channel_id=1, source_target_pairs={{0,1},{1,0},{2,3},{3,2},{4,5},{5,4},{6,7},{7,6},{8,9},{9,8},{10,11... | collective-permute-start | bytes 1572872 | tf_op jit(solution)/shard_map/ppermute | solution.py:22
  12.2 14.3 %collective-permute-start.3 = (f32[3,2,64,128]{3,2,1,0:T(8,128)S(1)}, f32[3,2,64,128]{3,2,1,0:T(8,128)S(1)}, u32[]{:S(2)}, u32[]{:S(2)}) collective-permute-start(f32[3,2,64,128]{3,2,1,0:T(8,128)S(1)} %get-tuple-element.28), channel_id=1, source_target_pairs={{0,248},{2,250},{4,252},{6,254},{8,16},{10,18},{12,20},{14,22},{16... | collective-permute-start | bytes 589832 | tf_op jit(solution)/shard_map/ppermute | solution.py:393
  14.8 8.0 %copy-start = (f32[64,1,16,128]{3,2,1,0:T(8,128)S(1)}, f32[64,1,16,128]{3,2,1,0:T(8,128)}, u32[]{:S(2)}) copy-start(f32[64,1,16,128]{3,2,1,0:T(8,128)} %param.15) | copy-start | bytes 1572868
  15.0 11.4 %collective-permute-start.2 = (f32[3,2,64,128]{3,2,1,0:T(8,128)S(1)}, f32[3,2,64,128]{3,2,1,0:T(8,128)S(1)}, u32[]{:S(2)}, u32[]{:S(2)}) collective-permute-start(f32[3,2,64,128]{3,2,1,0:T(8,128)S(1)} %pack_even.1.refs_5_), channel_id=1, source_target_pairs={{0,8},{2,10},{4,12},{6,14},{8,0},{10,2},{12,4},{14,6},{16,24},{18,... | collective-permute-start | bytes 589832 | tf_op jit(solution)/shard_map/ppermute | solution.py:393
  21.8 3.6 %collective-permute-start.4 = (f32[2,3072]{1,0:T(2,128)S(1)}, f32[2,3072]{1,0:T(2,128)S(1)}, u32[]{:S(2)}, u32[]{:S(2)}) collective-permute-start(f32[2,3072]{1,0:T(2,128)S(1)} %get-tuple-element.29), channel_id=1, source_target_pairs={{0,2},{2,0},{4,6},{6,4},{8,10},{10,8},{12,14},{14,12},{16,18},{18,... | collective-permute-start | bytes 73736 | tf_op jit(solution)/shard_map/ppermute | solution.py:393
  22.8 3.6 %collective-permute-start.5 = (f32[2,3072]{1,0:T(2,128)S(1)}, f32[2,3072]{1,0:T(2,128)S(1)}, u32[]{:S(2)}, u32[]{:S(2)}) collective-permute-start(f32[2,3072]{1,0:T(2,128)S(1)} %get-tuple-element.24.refs_6_), channel_id=1, source_target_pairs={{0,254},{2,4},{4,2},{6,8},{8,6},{10,12},{12,10},{14,16},{16,14},{1... | collective-permute-start | bytes 73736 | tf_op jit(solution)/shard_map/ppermute | solution.py:393

commit v6 on v5

--- a/solution.py
+++ b/solution.py
@@ -6,7 +6,8 @@
 from jax.sharding import PartitionSpec as P
 
 TW = 4
-FIRST_LIMIT = (53 << 20) + (640 << 10)
+EDGE = 3
+FIRST_LIMIT = (53 << 20) + (560 << 10)
 LONG = 12_000_000_000
 W_COST = 0
 I_COST = 0
@@ -95,7 +96,7 @@
 
 
 def rim_slot(i, px):
-    return i if i < 2 else i - px + 4
+    return i if i < EDGE else i - px + 2 * EDGE
 
 
 def sender(sems):
@@ -133,11 +134,11 @@
         for k, part in solved(half, left, w_half, t_half):
             i = h * half + k
             full_ref[pl.ds(i, levels, stride=px), :] = part
-            if not 2 <= i < px - 2:
+            if not EDGE <= i < px - EDGE:
                 rim_ref[pl.ds(rim_slot(i, px) * levels, levels), :] = part
     edges = rims(full_ref[...], rim_selector(py))
     for k in range(levels * px // py):
-        rim_ref[pl.ds(4 * levels + 4 * k, 4), :] = edges[0:4, k * py : (k + 1) * py]
+        rim_ref[pl.ds(2 * EDGE * levels + 4 * k, 4), :] = edges[0:4, k * py : (k + 1) * py]
 
 
 def solved(px, left, w_ref, t_ref, skip=0):
@@ -156,8 +157,9 @@
     levels = w_ref.shape[0] // px
     me = lax.axis_index("lev")
     left = left_factor([at_ref[pl.ds((3 - me) * levels, levels), :]])
-    for i, part in solved(px, left, w_ref, t_ref, 2):
-        inner_ref[i - 2] = part
+    for i, part in solved(px, left, w_ref, t_ref, EDGE // 2 * 2):
+        if EDGE <= i < px - EDGE:
+            inner_ref[i - EDGE] = part
 
 
 def solve_rest(px, w_ref, t_ref, at_ref, ow_ref, mw_ref, mt_ref):
@@ -184,7 +186,7 @@
         i = start + d
         out[0, d] = row(u_ref, i, levels, px)
         out[1, d] = row(p_ref, i, levels, px) * row(q_ref, i, levels, px)
-        star = row(mt_ref, i, levels, px) + got_ref[pl.ds(((1 - first) * 2 + d) * levels, levels), :]
+        star = row(mt_ref, i, levels, px) + got_ref[pl.ds(((1 - first) * (2 * EDGE - 2) + d) * levels, levels), :]
         out[2, d] = row(wf_ref, i, levels, px) * star
 
 
@@ -202,7 +204,7 @@
     pack_rows(px, 1 - odd4, u_ref, p_ref, q_ref, wf_ref, mt_ref, got_ref, o4_ref)
     selector = rim_selector(py)
     got_rims = jnp.concatenate(
-        [got_ref[pl.ds(4 * levels + 4 * k, 4), :] for k in range(levels * px // py)], axis=1
+        [got_ref[pl.ds(2 * EDGE * levels + 4 * k, 4), :] for k in range(levels * px // py)], axis=1
     )
     v_rims = rims(v_ref[...], selector)[0:4]
     p_rims = rims(p_ref[...] * q_ref[...], selector)[0:4]
@@ -310,8 +312,8 @@
 def theta_inner(px, rim_ref, inner_ref, mt_ref, wf_ref, ws_ref, o_ref, star_ref, first_ref):
     levels = inner_ref.shape[1]
     for i in range(px):
-        if 2 <= i < px - 2:
-            got = inner_ref[i - 2]
+        if EDGE <= i < px - EDGE:
+            got = inner_ref[i - EDGE]
         else:
             got = rim_ref[pl.ds(rim_slot(i, px) * levels, levels), :]
         star = got + row(mt_ref, i, levels, px)
@@ -400,9 +402,9 @@
         x.reshape(cells, py) for x in (u, v, w, t, p, grad, squeeze, wind_first, wind_second)
     )
     flat = (cells, py)
-    rim_rows = 4 * levels + 4 * (cells // py)
+    rim_rows = 2 * EDGE * levels + 4 * (cells // py)
     rim_shape = (rim_rows, py)
-    inner_shape = (px - 4, levels, py)
+    inner_shape = (px - 2 * EDGE, levels, py)
     rim_t, at = call(
         kernel_for(px, solve_first), "solve_first", [rim_shape, (4 * levels, 2 * levels)],
         [pltpu.VMEM((2, levels, px // 2, py), f32)] * 2

time: 35.3 us -> 35.1 us (level)
  waiting for transfers between devices: 7.72 us -> 6.22 us
  starting transfers between devices: 16.3 us -> 17.6 us
    ppermute x4, starting transfers between devices: 9.46 us -> 10.8 us  [exchange(): return lax.ppermute(array, 'cols', pairs)]
    ppermute x3, waiting for transfers between devices: 6.66 us -> 5.58 us  [passed_along(): lax.ppermute(array, axis, [(i, (i + by) % devices) for i in range(devices)])]
    ppermute x4, waiting for transfers between devices: 1.06 us -> 0.64 us  [exchange(): return lax.ppermute(array, 'cols', pairs)]
where the time goes in v6:
time: 35.1 us; the launch traced here: 35 us
  starting transfers between devices  17.6 us (50%)
  Pallas kernels  9.5 us (27%)
  waiting for transfers between devices  6.22 us (18%)
  other arithmetic  0.85 us (2%)
  between operations  0.79 us (2%)
    ppermute x4, starting transfers between devices, exchange(): return lax.ppermute(array, 'cols', pairs)  10.8 us
    pallas_call x8, Pallas kernels, call(): pl.pallas_call(body, out_shape=shapes, in_specs=[in_space] * len(args) +...  9.5 us
    ppermute x3, starting transfers between devices, passed_along(): lax.ppermute(array, axis, [(i, (i + by) % devices) for i in range(devices)])  6.81 us
    ppermute x3, waiting for transfers between devices, passed_along(): lax.ppermute(array, axis, [(i, (i + by) % devices) for i in range(devices)])  5.58 us
    add x1, other arithmetic, on_device(): w_out = mine_w + got_w  0.85 us
  transfers between devices with their start and end apart: 7, of which 3 were waited for; matrix products, arithmetic and copies ran while one was open for 0% of the time, Pallas kernels for 21%

profile of v6, /device:TPU:24, one launch (start us, length us, event | category | flops | bytes accessed | tf_op | source)
XLA Modules:
  0.0 35.0 jit_solution(16717871246821395201)
XLA Ops:
  0.7 2.2 %solve_first.1 = (f32[416,128]{1,0:T(8,128)S(1)}, f32[256,128]{1,0:T(8,128)S(1)}) custom-call(f32[64,16,128]{2,1,0:T(8,128)} %bitcast.28, f32[64,16,128]{2,1,0:T(8,128)} %bitcast.31, f32[256,256]{1,0:T(8,128)} %refs_2_.1), custom_call_target="tpu_custom_call" | custom-call | flops 12000000000 | bytes 1654784 | tf_op jit(solution)/shard_map/solve_first/pallas_call | solution.py:48
  2.8 3.1 %collective-permute-start = (f32[416,128]{1,0:T(8,128)S(1)}, f32[416,128]{1,0:T(8,128)S(1)}, u32[]{:S(2)}, u32[]{:S(2)}) collective-permute-start(f32[416,128]{1,0:T(8,128)S(1)} %get-tuple-element.22), channel_id=1, source_target_pairs={{0,1},{1,0},{2,3},{3,2},{4,5},{5,4},{6,7},{7,6},{8,9},{9,8},{10,11... | collective-permute-start | bytes 638984 | tf_op jit(solution)/shard_map/ppermute | solution.py:23
  5.9 0.4 %solve_inner.1.refs_3_ = f32[10,64,128]{2,1,0:T(8,128)S(1)} custom-call(f32[1024,128]{1,0:T(8,128)S(1)} %bitcast.29, f32[1024,128]{1,0:T(8,128)S(1)} %bitcast.32, f32[256,128]{1,0:T(8,128)S(1)} %get-tuple-element.20.refs_2_), custom_call_target="tpu_custom_call" | custom-call | bytes 1507328 | tf_op jit(solution)/shard_map/solve_inner/pallas_call | solution.py:48
  6.4 0.0 copy-start.3
  6.4 0.0 copy-start.4
  6.4 0.0 copy-start.5
  6.4 0.0 copy-start.6
  6.5 0.0 copy-start.7
  6.5 0.0 copy-start.8
  6.5 0.6 %collective-permute-start.1 = (f32[10,64,128]{2,1,0:T(8,128)S(1)}, f32[10,64,128]{2,1,0:T(8,128)S(1)}, u32[]{:S(2)}, u32[]{:S(2)}) collective-permute-start(f32[10,64,128]{2,1,0:T(8,128)S(1)} %solve_inner.1.refs_3_), channel_id=1, source_target_pairs={{0,1},{1,0},{2,3},{3,2},{4,5},{5,4},{6,7},{7,6},{8,9},{9,8},{10,11... | collective-permute-start | bytes 983048 | tf_op jit(solution)/shard_map/ppermute | solution.py:23
  7.1 0.9 %solve_rest.1 = (f32[1024,128]{1,0:T(8,128)S(1)}, f32[1024,128]{1,0:T(8,128)S(1)}, f32[1024,128]{1,0:T(8,128)S(1)}) custom-call(f32[1024,128]{1,0:T(8,128)S(1)} %bitcast.30, f32[1024,128]{1,0:T(8,128)S(1)} %bitcast.33, f32[256,128]{1,0:T(8,128)S(1)} %get-tuple-element.20.refs_2_, f32[10,64,128]{2,1,0:T(8,128)S(1)} %solve_inner.1.refs_3_), custom_call_target="tpu_custom_call" | custom-call | flops 12000000000 | bytes 2752512 | tf_op jit(solution)/shard_map/solve_rest/pallas_call | solution.py:48
  8.0 3.1 %collective-permute-start.6 = (f32[1024,128]{1,0:T(8,128)S(1)}, f32[1024,128]{1,0:T(8,128)S(1)}, u32[]{:S(2)}, u32[]{:S(2)}) collective-permute-start(f32[1024,128]{1,0:T(8,128)S(1)} %get-tuple-element.23.refs_8_), channel_id=1, source_target_pairs={{0,1},{1,0},{2,3},{3,2},{4,5},{5,4},{6,7},{7,6},{8,9},{9,8},{10,11... | collective-permute-start | bytes 1572872 | tf_op jit(solution)/shard_map/ppermute | solution.py:23
  11.1 1.5 %collective-permute-done.refs_7_.refs_5_.refs_0_ = f32[416,128]{1,0:T(8,128)S(1)} collective-permute-done((f32[416,128]{1,0:T(8,128)S(1)}, f32[416,128]{1,0:T(8,128)S(1)}, u32[]{:S(2)}, u32[]{:S(2)}) %collective-permute-start) | collective-permute-done | bytes 213024 | tf_op jit(solution)/shard_map/ppermute | solution.py:23
  12.6 1.0 %pack.1 = (f32[3,2,64,128]{3,2,1,0:T(8,128)S(1)}, f32[2,3072]{1,0:T(2,128)S(1)}, f32[2,3072]{1,0:T(2,128)S(1)}) custom-call(f32[1024,128]{1,0:T(8,128)S(1)} %bitcast.39, f32[1024,128]{1,0:T(8,128)S(1)} %bitcast.42, f32[1024,128]{1,0:T(8,128)S(1)} %bitcast.44, f32[1024,128]{1,0:T(8,128)S(1)} %bitcast.47, f32[1024,128]{1,0:T(8,128)S(1)} %bitcast.34, ...), custom_call_target="tpu_custom_call" | custom-call | flops 12000000000 | bytes 4128768 | tf_op jit(solution)/shard_map/pack/pallas_call | solution.py:48
  13.6 2.7 %collective-permute-start.3 = (f32[3,2,64,128]{3,2,1,0:T(8,128)S(1)}, f32[3,2,64,128]{3,2,1,0:T(8,128)S(1)}, u32[]{:S(2)}, u32[]{:S(2)}) collective-permute-start(f32[3,2,64,128]{3,2,1,0:T(8,128)S(1)} %get-tuple-element.28), channel_id=1, source_target_pairs={{0,248},{2,250},{4,252},{6,254},{8,16},{10,18},{12,20},{14,22},{16... | collective-permute-start | bytes 589832 | tf_op jit(solution)/shard_map/ppermute | solution.py:395
  16.3 0.2 pack_even.1.refs_5_
  16.4 7.3 %collective-permute-start.2 = (f32[3,2,64,128]{3,2,1,0:T(8,128)S(1)}, f32[3,2,64,128]{3,2,1,0:T(8,128)S(1)}, u32[]{:S(2)}, u32[]{:S(2)}) collective-permute-start(f32[3,2,64,128]{3,2,1,0:T(8,128)S(1)} %pack_even.1.refs_5_), channel_id=1, source_target_pairs={{0,8},{2,10},{4,12},{6,14},{8,0},{10,2},{12,4},{14,6},{16,24},{18,... | collective-permute-start | bytes 589832 | tf_op jit(solution)/shard_map/ppermute | solution.py:395
  23.7 0.9 %collective-permute-start.5 = (f32[2,3072]{1,0:T(2,128)S(1)}, f32[2,3072]{1,0:T(2,128)S(1)}, u32[]{:S(2)}, u32[]{:S(2)}) collective-permute-start(f32[2,3072]{1,0:T(2,128)S(1)} %get-tuple-element.24.refs_6_), channel_id=1, source_target_pairs={{0,254},{2,4},{4,2},{6,8},{8,6},{10,12},{12,10},{14,16},{16,14},{1... | collective-permute-start | bytes 73736 | tf_op jit(solution)/shard_map/ppermute | solution.py:395
  24.6 1.5 %winds_inner.1 = (f32[1024,128]{1,0:T(8,128)S(1)}, f32[1024,128]{1,0:T(8,128)S(1)}, f32[1024,128]{1,0:T(8,128)S(1)}) custom-call(f32[1024,128]{1,0:T(8,128)S(1)} %bitcast.41, f32[1024,128]{1,0:T(8,128)S(1)} %bitcast.43, f32[1024,128]{1,0:T(8,128)S(1)} %bitcast.46, f32[1024,128]{1,0:T(8,128)S(1)} %bitcast.26, f32[1024,128]{1,0:T(8,128)S(1)} %bitcast.49, ...), custom_call_target="tpu_custom_call" | custom-call | bytes 4194304 | tf_op jit(solution)/shard_map/winds_inner/pallas_call | solution.py:48
  26.1 1.0 %theta_inner.1.refs_4_ = f32[1024,128]{1,0:T(8,128)S(1)} custom-call(f32[416,128]{1,0:T(8,128)S(1)} %collective-permute-done.refs_7_.refs_5_.refs_0_, f32[10,64,128]{2,1,0:T(8,128)S(1)} %collective-permute-done.1.refs_1_, f32[1024,128]{1,0:T(8,128)S(1)} %get-tuple-element.21.refs_6_.refs_4_.refs_2_, f32[1024,128]{1,0:T(8,128)S(1)} %bitcast.36, ...), custom_call_target="tpu_custom_call" | custom-call | bytes 2637824 | tf_op jit(solution)/shard_map/theta_inner/pallas_call | solution.py:48
  27.1 0.6 %collective-permute-done.5.refs_8_ = f32[2,3072]{1,0:T(2,128)S(1)} collective-permute-done((f32[2,3072]{1,0:T(2,128)S(1)}, f32[2,3072]{1,0:T(2,128)S(1)}, u32[]{:S(2)}, u32[]{:S(2)}) %collective-permute-start.5) | collective-permute-done | bytes 24608 | tf_op jit(solution)/shard_map/ppermute | solution.py:395
  27.7 2.3 %finish.1 = (f32[1024,128]{1,0:T(8,128)}, f32[1024,128]{1,0:T(8,128)}, f32[1024,128]{1,0:T(8,128)}, f32[1024,128]{1,0:T(8,128)}) custom-call(f32[1024,128]{1,0:T(8,128)S(1)} %get-tuple-element.25.refs_0_, f32[1024,128]{1,0:T(8,128)S(1)} %get-tuple-element.26.refs_1_, f32[1024,128]{1,0:T(8,128)S(1)} %get-tuple-element.27.refs_2_, f32[1024,128]{1,0:T(8,128)S(1)} %bitcast.27, ...), custom_call_target="tpu_custom_call" | custom-call | bytes 5160960 | tf_op jit(solution)/shard_map/finish/pallas_call | solution.py:48
  30.0 4.1 %collective-permute-done.6 = f32[1024,128]{1,0:T(8,128)S(1)} collective-permute-done((f32[1024,128]{1,0:T(8,128)S(1)}, f32[1024,128]{1,0:T(8,128)S(1)}, u32[]{:S(2)}, u32[]{:S(2)}) %collective-permute-start.6) | collective-permute-done | bytes 524320 | tf_op jit(solution)/shard_map/ppermute | solution.py:23
  34.2 0.8 %add.3 = f32[1024,128]{1,0:T(8,128)} add(f32[1024,128]{1,0:T(8,128)S(1)} %get-tuple-element.32, f32[1024,128]{1,0:T(8,128)S(1)} %collective-permute-done.6) | non-fusion elementwise | flops 131072 | bytes 1572864 | tf_op jit(solution)/shard_map/add | solution.py:434
  (17 shorter events, 0.0 us)
Async XLA Ops:
  0.6 5.3 %copy-start.1 = (f32[64,1,16,128]{3,2,1,0:T(8,128)S(1)}, f32[64,1,16,128]{3,2,1,0:T(8,128)}, u32[]{:S(2)}) copy-start(f32[64,1,16,128]{3,2,1,0:T(8,128)} %param.12) | copy-start | bytes 1572868
  0.6 5.3 %copy-start.2 = (f32[64,1,16,128]{3,2,1,0:T(8,128)S(1)}, f32[64,1,16,128]{3,2,1,0:T(8,128)}, u32[]{:S(2)}) copy-start(f32[64,1,16,128]{3,2,1,0:T(8,128)} %param.13) | copy-start | bytes 1572868
  2.8 9.7 %collective-permute-start = (f32[416,128]{1,0:T(8,128)S(1)}, f32[416,128]{1,0:T(8,128)S(1)}, u32[]{:S(2)}, u32[]{:S(2)}) collective-permute-start(f32[416,128]{1,0:T(8,128)S(1)} %get-tuple-element.22), channel_id=1, source_target_pairs={{0,1},{1,0},{2,3},{3,2},{4,5},{5,4},{6,7},{7,6},{8,9},{9,8},{10,11... | collective-permute-start | bytes 638984 | tf_op jit(solution)/shard_map/ppermute | solution.py:23
  6.4 6.2 %copy-start.3 = (f32[64,1,16,128]{3,2,1,0:T(8,128)S(1)}, f32[64,1,16,128]{3,2,1,0:T(8,128)}, u32[]{:S(2)}) copy-start(f32[64,1,16,128]{3,2,1,0:T(8,128)} %param.17) | copy-start | bytes 1572868
  6.4 6.2 %copy-start.4 = (f32[64,1,16,128]{3,2,1,0:T(8,128)S(1)}, f32[64,1,16,128]{3,2,1,0:T(8,128)}, u32[]{:S(2)}) copy-start(f32[64,1,16,128]{3,2,1,0:T(8,128)} %param.18) | copy-start | bytes 1572868
  6.4 6.1 %copy-start.5 = (f32[64,1,16,128]{3,2,1,0:T(8,128)S(1)}, f32[64,1,16,128]{3,2,1,0:T(8,128)}, u32[]{:S(2)}) copy-start(f32[64,1,16,128]{3,2,1,0:T(8,128)} %param.10) | copy-start | bytes 1572868
  6.4 6.1 %copy-start.6 = (f32[64,1,16,128]{3,2,1,0:T(8,128)S(1)}, f32[64,1,16,128]{3,2,1,0:T(8,128)}, u32[]{:S(2)}) copy-start(f32[64,1,16,128]{3,2,1,0:T(8,128)} %param.11) | copy-start | bytes 1572868
  6.5 6.1 %copy-start.7 = (f32[64,1,16,128]{3,2,1,0:T(8,128)S(1)}, f32[64,1,16,128]{3,2,1,0:T(8,128)}, u32[]{:S(2)}) copy-start(f32[64,1,16,128]{3,2,1,0:T(8,128)} %param.14) | copy-start | bytes 1572868
  6.5 6.1 %copy-start.8 = (f32[64,1,16,128]{3,2,1,0:T(8,128)S(1)}, f32[64,1,16,128]{3,2,1,0:T(8,128)}, u32[]{:S(2)}) copy-start(f32[64,1,16,128]{3,2,1,0:T(8,128)} %param.16) | copy-start | bytes 1572868
  6.5 17.2 %collective-permute-start.1 = (f32[10,64,128]{2,1,0:T(8,128)S(1)}, f32[10,64,128]{2,1,0:T(8,128)S(1)}, u32[]{:S(2)}, u32[]{:S(2)}) collective-permute-start(f32[10,64,128]{2,1,0:T(8,128)S(1)} %solve_inner.1.refs_3_), channel_id=1, source_target_pairs={{0,1},{1,0},{2,3},{3,2},{4,5},{5,4},{6,7},{7,6},{8,9},{9,8},{10,11... | collective-permute-start | bytes 983048 | tf_op jit(solution)/shard_map/ppermute | solution.py:23
  8.0 26.1 %collective-permute-start.6 = (f32[1024,128]{1,0:T(8,128)S(1)}, f32[1024,128]{1,0:T(8,128)S(1)}, u32[]{:S(2)}, u32[]{:S(2)}) collective-permute-start(f32[1024,128]{1,0:T(8,128)S(1)} %get-tuple-element.23.refs_8_), channel_id=1, source_target_pairs={{0,1},{1,0},{2,3},{3,2},{4,5},{5,4},{6,7},{7,6},{8,9},{9,8},{10,11... | collective-permute-start | bytes 1572872 | tf_op jit(solution)/shard_map/ppermute | solution.py:23
  13.6 14.1 %collective-permute-start.3 = (f32[3,2,64,128]{3,2,1,0:T(8,128)S(1)}, f32[3,2,64,128]{3,2,1,0:T(8,128)S(1)}, u32[]{:S(2)}, u32[]{:S(2)}) collective-permute-start(f32[3,2,64,128]{3,2,1,0:T(8,128)S(1)} %get-tuple-element.28), channel_id=1, source_target_pairs={{0,248},{2,250},{4,252},{6,254},{8,16},{10,18},{12,20},{14,22},{16... | collective-permute-start | bytes 589832 | tf_op jit(solution)/shard_map/ppermute | solution.py:395
  16.3 8.3 %copy-start = (f32[64,1,16,128]{3,2,1,0:T(8,128)S(1)}, f32[64,1,16,128]{3,2,1,0:T(8,128)}, u32[]{:S(2)}) copy-start(f32[64,1,16,128]{3,2,1,0:T(8,128)} %param.15) | copy-start | bytes 1572868
  16.4 11.3 %collective-permute-start.2 = (f32[3,2,64,128]{3,2,1,0:T(8,128)S(1)}, f32[3,2,64,128]{3,2,1,0:T(8,128)S(1)}, u32[]{:S(2)}, u32[]{:S(2)}) collective-permute-start(f32[3,2,64,128]{3,2,1,0:T(8,128)S(1)} %pack_even.1.refs_5_), channel_id=1, source_target_pairs={{0,8},{2,10},{4,12},{6,14},{8,0},{10,2},{12,4},{14,6},{16,24},{18,... | collective-permute-start | bytes 589832 | tf_op jit(solution)/shard_map/ppermute | solution.py:395
  23.7 3.4 %collective-permute-start.4 = (f32[2,3072]{1,0:T(2,128)S(1)}, f32[2,3072]{1,0:T(2,128)S(1)}, u32[]{:S(2)}, u32[]{:S(2)}) collective-permute-start(f32[2,3072]{1,0:T(2,128)S(1)} %get-tuple-element.29), channel_id=1, source_target_pairs={{0,2},{2,0},{4,6},{6,4},{8,10},{10,8},{12,14},{14,12},{16,18},{18,... | collective-permute-start | bytes 73736 | tf_op jit(solution)/shard_map/ppermute | solution.py:395
  23.7 4.0 %collective-permute-start.5 = (f32[2,3072]{1,0:T(2,128)S(1)}, f32[2,3072]{1,0:T(2,128)S(1)}, u32[]{:S(2)}, u32[]{:S(2)}) collective-permute-start(f32[2,3072]{1,0:T(2,128)S(1)} %get-tuple-element.24.refs_6_), channel_id=1, source_target_pairs={{0,254},{2,4},{4,2},{6,8},{8,6},{10,12},{12,10},{14,16},{16,14},{1... | collective-permute-start | bytes 73736 | tf_op jit(solution)/shard_map/ppermute | solution.py:395

commit v7 on v6

--- a/solution.py
+++ b/solution.py
@@ -86,9 +86,9 @@
     return jnp.where((j == want) & (k < 4), 1.0, 0.0).astype(bf16)
 
 
-def rims(field, selector):
+def rims(field, selector, parts=split3):
     total = 0.0
-    for piece in split3(field):
+    for piece in parts(field):
         total = total + lax.dot_general(
             selector, piece, (((1,), (1,)), ((), ())), preferred_element_type=f32
         )
@@ -136,7 +136,7 @@
             full_ref[pl.ds(i, levels, stride=px), :] = part
             if not EDGE <= i < px - EDGE:
                 rim_ref[pl.ds(rim_slot(i, px) * levels, levels), :] = part
-    edges = rims(full_ref[...], rim_selector(py))
+    edges = rims(full_ref[...], rim_selector(py), split)
     for k in range(levels * px // py):
         rim_ref[pl.ds(2 * EDGE * levels + 4 * k, 4), :] = edges[0:4, k * py : (k + 1) * py]
 

time: 35.1 us -> 35 us (level)
  no operation moved by 1% of the time
where the time goes in v7:
time: 35 us; the launch traced here: 34.9 us
  starting transfers between devices  17.6 us (50%)
  Pallas kernels  9.43 us (27%)
  waiting for transfers between devices  6.22 us (18%)
  other arithmetic  0.85 us (2%)
  between operations  0.79 us (2%)
    ppermute x4, starting transfers between devices, exchange(): return lax.ppermute(array, 'cols', pairs)  10.8 us
    pallas_call x8, Pallas kernels, call(): pl.pallas_call(body, out_shape=shapes, in_specs=[in_space] * len(args) +...  9.43 us
    ppermute x3, starting transfers between devices, passed_along(): lax.ppermute(array, axis, [(i, (i + by) % devices) for i in range(devices)])  6.81 us
    ppermute x3, waiting for transfers between devices, passed_along(): lax.ppermute(array, axis, [(i, (i + by) % devices) for i in range(devices)])  5.57 us
    add x1, other arithmetic, on_device(): w_out = mine_w + got_w  0.85 us
  transfers between devices with their start and end apart: 7, of which 3 were waited for; matrix products, arithmetic and copies ran while one was open for 0% of the time, Pallas kernels for 21%

profile of v7, /device:TPU:24, one launch (start us, length us, event | category | flops | bytes accessed | tf_op | source)
XLA Modules:
  0.0 34.9 jit_solution(16323682664785480216)
XLA Ops:
  0.7 2.1 %solve_first.1 = (f32[416,128]{1,0:T(8,128)S(1)}, f32[256,128]{1,0:T(8,128)S(1)}) custom-call(f32[64,16,128]{2,1,0:T(8,128)} %bitcast.28, f32[64,16,128]{2,1,0:T(8,128)} %bitcast.31, f32[256,256]{1,0:T(8,128)} %refs_2_.1), custom_call_target="tpu_custom_call" | custom-call | flops 12000000000 | bytes 1654784 | tf_op jit(solution)/shard_map/solve_first/pallas_call | solution.py:48
  2.8 3.1 %collective-permute-start = (f32[416,128]{1,0:T(8,128)S(1)}, f32[416,128]{1,0:T(8,128)S(1)}, u32[]{:S(2)}, u32[]{:S(2)}) collective-permute-start(f32[416,128]{1,0:T(8,128)S(1)} %get-tuple-element.22), channel_id=1, source_target_pairs={{0,1},{1,0},{2,3},{3,2},{4,5},{5,4},{6,7},{7,6},{8,9},{9,8},{10,11... | collective-permute-start | bytes 638984 | tf_op jit(solution)/shard_map/ppermute | solution.py:23
  5.9 0.4 %solve_inner.1.refs_3_ = f32[10,64,128]{2,1,0:T(8,128)S(1)} custom-call(f32[1024,128]{1,0:T(8,128)S(1)} %bitcast.29, f32[1024,128]{1,0:T(8,128)S(1)} %bitcast.32, f32[256,128]{1,0:T(8,128)S(1)} %get-tuple-element.20.refs_2_), custom_call_target="tpu_custom_call" | custom-call | bytes 1507328 | tf_op jit(solution)/shard_map/solve_inner/pallas_call | solution.py:48
  6.3 0.0 copy-start.3
  6.3 0.0 copy-start.4
  6.4 0.0 copy-start.5
  6.4 0.0 copy-start.6
  6.4 0.0 copy-start.7
  6.4 0.0 copy-start.8
  6.4 0.6 %collective-permute-start.1 = (f32[10,64,128]{2,1,0:T(8,128)S(1)}, f32[10,64,128]{2,1,0:T(8,128)S(1)}, u32[]{:S(2)}, u32[]{:S(2)}) collective-permute-start(f32[10,64,128]{2,1,0:T(8,128)S(1)} %solve_inner.1.refs_3_), channel_id=1, source_target_pairs={{0,1},{1,0},{2,3},{3,2},{4,5},{5,4},{6,7},{7,6},{8,9},{9,8},{10,11... | collective-permute-start | bytes 983048 | tf_op jit(solution)/shard_map/ppermute | solution.py:23
  7.0 0.9 %solve_rest.1 = (f32[1024,128]{1,0:T(8,128)S(1)}, f32[1024,128]{1,0:T(8,128)S(1)}, f32[1024,128]{1,0:T(8,128)S(1)}) custom-call(f32[1024,128]{1,0:T(8,128)S(1)} %bitcast.30, f32[1024,128]{1,0:T(8,128)S(1)} %bitcast.33, f32[256,128]{1,0:T(8,128)S(1)} %get-tuple-element.20.refs_2_, f32[10,64,128]{2,1,0:T(8,128)S(1)} %solve_inner.1.refs_3_), custom_call_target="tpu_custom_call" | custom-call | flops 12000000000 | bytes 2752512 | tf_op jit(solution)/shard_map/solve_rest/pallas_call | solution.py:48
  7.9 3.1 %collective-permute-start.6 = (f32[1024,128]{1,0:T(8,128)S(1)}, f32[1024,128]{1,0:T(8,128)S(1)}, u32[]{:S(2)}, u32[]{:S(2)}) collective-permute-start(f32[1024,128]{1,0:T(8,128)S(1)} %get-tuple-element.23.refs_8_), channel_id=1, source_target_pairs={{0,1},{1,0},{2,3},{3,2},{4,5},{5,4},{6,7},{7,6},{8,9},{9,8},{10,11... | collective-permute-start | bytes 1572872 | tf_op jit(solution)/shard_map/ppermute | solution.py:23
  11.0 1.5 %collective-permute-done.refs_7_.refs_5_.refs_0_ = f32[416,128]{1,0:T(8,128)S(1)} collective-permute-done((f32[416,128]{1,0:T(8,128)S(1)}, f32[416,128]{1,0:T(8,128)S(1)}, u32[]{:S(2)}, u32[]{:S(2)}) %collective-permute-start) | collective-permute-done | bytes 213024 | tf_op jit(solution)/shard_map/ppermute | solution.py:23
  12.5 1.0 %pack.1 = (f32[3,2,64,128]{3,2,1,0:T(8,128)S(1)}, f32[2,3072]{1,0:T(2,128)S(1)}, f32[2,3072]{1,0:T(2,128)S(1)}) custom-call(f32[1024,128]{1,0:T(8,128)S(1)} %bitcast.39, f32[1024,128]{1,0:T(8,128)S(1)} %bitcast.42, f32[1024,128]{1,0:T(8,128)S(1)} %bitcast.44, f32[1024,128]{1,0:T(8,128)S(1)} %bitcast.47, f32[1024,128]{1,0:T(8,128)S(1)} %bitcast.34, ...), custom_call_target="tpu_custom_call" | custom-call | flops 12000000000 | bytes 4128768 | tf_op jit(solution)/shard_map/pack/pallas_call | solution.py:48
  13.5 2.7 %collective-permute-start.3 = (f32[3,2,64,128]{3,2,1,0:T(8,128)S(1)}, f32[3,2,64,128]{3,2,1,0:T(8,128)S(1)}, u32[]{:S(2)}, u32[]{:S(2)}) collective-permute-start(f32[3,2,64,128]{3,2,1,0:T(8,128)S(1)} %get-tuple-element.28), channel_id=1, source_target_pairs={{0,248},{2,250},{4,252},{6,254},{8,16},{10,18},{12,20},{14,22},{16... | collective-permute-start | bytes 589832 | tf_op jit(solution)/shard_map/ppermute | solution.py:395
  16.2 0.2 pack_even.1.refs_5_
  16.4 7.3 %collective-permute-start.2 = (f32[3,2,64,128]{3,2,1,0:T(8,128)S(1)}, f32[3,2,64,128]{3,2,1,0:T(8,128)S(1)}, u32[]{:S(2)}, u32[]{:S(2)}) collective-permute-start(f32[3,2,64,128]{3,2,1,0:T(8,128)S(1)} %pack_even.1.refs_5_), channel_id=1, source_target_pairs={{0,8},{2,10},{4,12},{6,14},{8,0},{10,2},{12,4},{14,6},{16,24},{18,... | collective-permute-start | bytes 589832 | tf_op jit(solution)/shard_map/ppermute | solution.py:395
  23.6 0.9 %collective-permute-start.5 = (f32[2,3072]{1,0:T(2,128)S(1)}, f32[2,3072]{1,0:T(2,128)S(1)}, u32[]{:S(2)}, u32[]{:S(2)}) collective-permute-start(f32[2,3072]{1,0:T(2,128)S(1)} %get-tuple-element.24.refs_6_), channel_id=1, source_target_pairs={{0,254},{2,4},{4,2},{6,8},{8,6},{10,12},{12,10},{14,16},{16,14},{1... | collective-permute-start | bytes 73736 | tf_op jit(solution)/shard_map/ppermute | solution.py:395
  24.5 1.5 %winds_inner.1 = (f32[1024,128]{1,0:T(8,128)S(1)}, f32[1024,128]{1,0:T(8,128)S(1)}, f32[1024,128]{1,0:T(8,128)S(1)}) custom-call(f32[1024,128]{1,0:T(8,128)S(1)} %bitcast.41, f32[1024,128]{1,0:T(8,128)S(1)} %bitcast.43, f32[1024,128]{1,0:T(8,128)S(1)} %bitcast.46, f32[1024,128]{1,0:T(8,128)S(1)} %bitcast.26, f32[1024,128]{1,0:T(8,128)S(1)} %bitcast.49, ...), custom_call_target="tpu_custom_call" | custom-call | bytes 4194304 | tf_op jit(solution)/shard_map/winds_inner/pallas_call | solution.py:48
  26.0 1.0 %theta_inner.1.refs_4_ = f32[1024,128]{1,0:T(8,128)S(1)} custom-call(f32[416,128]{1,0:T(8,128)S(1)} %collective-permute-done.refs_7_.refs_5_.refs_0_, f32[10,64,128]{2,1,0:T(8,128)S(1)} %collective-permute-done.1.refs_1_, f32[1024,128]{1,0:T(8,128)S(1)} %get-tuple-element.21.refs_6_.refs_4_.refs_2_, f32[1024,128]{1,0:T(8,128)S(1)} %bitcast.36, ...), custom_call_target="tpu_custom_call" | custom-call | bytes 2637824 | tf_op jit(solution)/shard_map/theta_inner/pallas_call | solution.py:48
  27.0 0.6 %collective-permute-done.5.refs_8_ = f32[2,3072]{1,0:T(2,128)S(1)} collective-permute-done((f32[2,3072]{1,0:T(2,128)S(1)}, f32[2,3072]{1,0:T(2,128)S(1)}, u32[]{:S(2)}, u32[]{:S(2)}) %collective-permute-start.5) | collective-permute-done | bytes 24608 | tf_op jit(solution)/shard_map/ppermute | solution.py:395
  27.6 2.3 %finish.1 = (f32[1024,128]{1,0:T(8,128)}, f32[1024,128]{1,0:T(8,128)}, f32[1024,128]{1,0:T(8,128)}, f32[1024,128]{1,0:T(8,128)}) custom-call(f32[1024,128]{1,0:T(8,128)S(1)} %get-tuple-element.25.refs_0_, f32[1024,128]{1,0:T(8,128)S(1)} %get-tuple-element.26.refs_1_, f32[1024,128]{1,0:T(8,128)S(1)} %get-tuple-element.27.refs_2_, f32[1024,128]{1,0:T(8,128)S(1)} %bitcast.27, ...), custom_call_target="tpu_custom_call" | custom-call | bytes 5160960 | tf_op jit(solution)/shard_map/finish/pallas_call | solution.py:48
  30.0 4.1 %collective-permute-done.6 = f32[1024,128]{1,0:T(8,128)S(1)} collective-permute-done((f32[1024,128]{1,0:T(8,128)S(1)}, f32[1024,128]{1,0:T(8,128)S(1)}, u32[]{:S(2)}, u32[]{:S(2)}) %collective-permute-start.6) | collective-permute-done | bytes 524320 | tf_op jit(solution)/shard_map/ppermute | solution.py:23
  34.1 0.8 %add.3 = f32[1024,128]{1,0:T(8,128)} add(f32[1024,128]{1,0:T(8,128)S(1)} %get-tuple-element.32, f32[1024,128]{1,0:T(8,128)S(1)} %collective-permute-done.6) | non-fusion elementwise | flops 131072 | bytes 1572864 | tf_op jit(solution)/shard_map/add | solution.py:434
  (17 shorter events, 0.0 us)
Async XLA Ops:
  0.6 5.2 %copy-start.1 = (f32[64,1,16,128]{3,2,1,0:T(8,128)S(1)}, f32[64,1,16,128]{3,2,1,0:T(8,128)}, u32[]{:S(2)}) copy-start(f32[64,1,16,128]{3,2,1,0:T(8,128)} %param.12) | copy-start | bytes 1572868
  0.6 5.2 %copy-start.2 = (f32[64,1,16,128]{3,2,1,0:T(8,128)S(1)}, f32[64,1,16,128]{3,2,1,0:T(8,128)}, u32[]{:S(2)}) copy-start(f32[64,1,16,128]{3,2,1,0:T(8,128)} %param.13) | copy-start | bytes 1572868
  2.8 9.7 %collective-permute-start = (f32[416,128]{1,0:T(8,128)S(1)}, f32[416,128]{1,0:T(8,128)S(1)}, u32[]{:S(2)}, u32[]{:S(2)}) collective-permute-start(f32[416,128]{1,0:T(8,128)S(1)} %get-tuple-element.22), channel_id=1, source_target_pairs={{0,1},{1,0},{2,3},{3,2},{4,5},{5,4},{6,7},{7,6},{8,9},{9,8},{10,11... | collective-permute-start | bytes 638984 | tf_op jit(solution)/shard_map/ppermute | solution.py:23
  6.3 6.2 %copy-start.3 = (f32[64,1,16,128]{3,2,1,0:T(8,128)S(1)}, f32[64,1,16,128]{3,2,1,0:T(8,128)}, u32[]{:S(2)}) copy-start(f32[64,1,16,128]{3,2,1,0:T(8,128)} %param.17) | copy-start | bytes 1572868
  6.3 6.2 %copy-start.4 = (f32[64,1,16,128]{3,2,1,0:T(8,128)S(1)}, f32[64,1,16,128]{3,2,1,0:T(8,128)}, u32[]{:S(2)}) copy-start(f32[64,1,16,128]{3,2,1,0:T(8,128)} %param.18) | copy-start | bytes 1572868
  6.4 6.1 %copy-start.5 = (f32[64,1,16,128]{3,2,1,0:T(8,128)S(1)}, f32[64,1,16,128]{3,2,1,0:T(8,128)}, u32[]{:S(2)}) copy-start(f32[64,1,16,128]{3,2,1,0:T(8,128)} %param.10) | copy-start | bytes 1572868
  6.4 6.1 %copy-start.6 = (f32[64,1,16,128]{3,2,1,0:T(8,128)S(1)}, f32[64,1,16,128]{3,2,1,0:T(8,128)}, u32[]{:S(2)}) copy-start(f32[64,1,16,128]{3,2,1,0:T(8,128)} %param.11) | copy-start | bytes 1572868
  6.4 6.1 %copy-start.7 = (f32[64,1,16,128]{3,2,1,0:T(8,128)S(1)}, f32[64,1,16,128]{3,2,1,0:T(8,128)}, u32[]{:S(2)}) copy-start(f32[64,1,16,128]{3,2,1,0:T(8,128)} %param.14) | copy-start | bytes 1572868
  6.4 6.1 %copy-start.8 = (f32[64,1,16,128]{3,2,1,0:T(8,128)S(1)}, f32[64,1,16,128]{3,2,1,0:T(8,128)}, u32[]{:S(2)}) copy-start(f32[64,1,16,128]{3,2,1,0:T(8,128)} %param.16) | copy-start | bytes 1572868
  6.4 17.2 %collective-permute-start.1 = (f32[10,64,128]{2,1,0:T(8,128)S(1)}, f32[10,64,128]{2,1,0:T(8,128)S(1)}, u32[]{:S(2)}, u32[]{:S(2)}) collective-permute-start(f32[10,64,128]{2,1,0:T(8,128)S(1)} %solve_inner.1.refs_3_), channel_id=1, source_target_pairs={{0,1},{1,0},{2,3},{3,2},{4,5},{5,4},{6,7},{7,6},{8,9},{9,8},{10,11... | collective-permute-start | bytes 983048 | tf_op jit(solution)/shard_map/ppermute | solution.py:23
  7.9 26.1 %collective-permute-start.6 = (f32[1024,128]{1,0:T(8,128)S(1)}, f32[1024,128]{1,0:T(8,128)S(1)}, u32[]{:S(2)}, u32[]{:S(2)}) collective-permute-start(f32[1024,128]{1,0:T(8,128)S(1)} %get-tuple-element.23.refs_8_), channel_id=1, source_target_pairs={{0,1},{1,0},{2,3},{3,2},{4,5},{5,4},{6,7},{7,6},{8,9},{9,8},{10,11... | collective-permute-start | bytes 1572872 | tf_op jit(solution)/shard_map/ppermute | solution.py:23
  13.5 14.1 %collective-permute-start.3 = (f32[3,2,64,128]{3,2,1,0:T(8,128)S(1)}, f32[3,2,64,128]{3,2,1,0:T(8,128)S(1)}, u32[]{:S(2)}, u32[]{:S(2)}) collective-permute-start(f32[3,2,64,128]{3,2,1,0:T(8,128)S(1)} %get-tuple-element.28), channel_id=1, source_target_pairs={{0,248},{2,250},{4,252},{6,254},{8,16},{10,18},{12,20},{14,22},{16... | collective-permute-start | bytes 589832 | tf_op jit(solution)/shard_map/ppermute | solution.py:395
  16.2 8.3 %copy-start = (f32[64,1,16,128]{3,2,1,0:T(8,128)S(1)}, f32[64,1,16,128]{3,2,1,0:T(8,128)}, u32[]{:S(2)}) copy-start(f32[64,1,16,128]{3,2,1,0:T(8,128)} %param.15) | copy-start | bytes 1572868
  16.4 11.3 %collective-permute-start.2 = (f32[3,2,64,128]{3,2,1,0:T(8,128)S(1)}, f32[3,2,64,128]{3,2,1,0:T(8,128)S(1)}, u32[]{:S(2)}, u32[]{:S(2)}) collective-permute-start(f32[3,2,64,128]{3,2,1,0:T(8,128)S(1)} %pack_even.1.refs_5_), channel_id=1, source_target_pairs={{0,8},{2,10},{4,12},{6,14},{8,0},{10,2},{12,4},{14,6},{16,24},{18,... | collective-permute-start | bytes 589832 | tf_op jit(solution)/shard_map/ppermute | solution.py:395
  23.6 3.4 %collective-permute-start.4 = (f32[2,3072]{1,0:T(2,128)S(1)}, f32[2,3072]{1,0:T(2,128)S(1)}, u32[]{:S(2)}, u32[]{:S(2)}) collective-permute-start(f32[2,3072]{1,0:T(2,128)S(1)} %get-tuple-element.29), channel_id=1, source_target_pairs={{0,2},{2,0},{4,6},{6,4},{8,10},{10,8},{12,14},{14,12},{16,18},{18,... | collective-permute-start | bytes 73736 | tf_op jit(solution)/shard_map/ppermute | solution.py:395
  23.6 4.0 %collective-permute-start.5 = (f32[2,3072]{1,0:T(2,128)S(1)}, f32[2,3072]{1,0:T(2,128)S(1)}, u32[]{:S(2)}, u32[]{:S(2)}) collective-permute-start(f32[2,3072]{1,0:T(2,128)S(1)} %get-tuple-element.24.refs_6_), channel_id=1, source_target_pairs={{0,254},{2,4},{4,2},{6,8},{8,6},{10,12},{12,10},{14,16},{16,14},{1... | collective-permute-start | bytes 73736 | tf_op jit(solution)/shard_map/ppermute | solution.py:395
